TPU v7x, 32 devices: a whole 2x2x4 slice. The times are simulated.
32 devices in a mesh: grp: 2 (over x), row: 8 (over z, y), col: 2 (over core).
Axes of the slice: x: 2, y: 2, z: 4, core: 2. Of those that a mesh axis runs over, the one named last changes fastest.
Arguments:
- pair: bfloat16 [352, 176, 128], P(('grp', 'row'), 'col'), parts along dimension 0, may hold values from -6 to 6
- cotangent: bfloat16 [352, 176, 128], P(('grp', 'row'), 'col'), parts along dimension 0, may hold values from -6 to 6
- chain_lengths: int32 [16], P('grp'), parts along dimension 0, may hold values from 1 to 22, 132 in all
- input_norm_gain: float32 [128], replicated, may hold values from 0.1 to 1.9
- input_norm_bias: float32 [128], replicated, may hold values from -3 to 3
- w_in: bfloat16 [128, 640], replicated, may hold values from -0.5 to 0.5
- output_norm_gain: float32 [128], replicated, may hold values from 0.1 to 1.9
- output_norm_bias: float32 [128], replicated, may hold values from -3 to 3
- w_out: bfloat16 [128, 128], replicated, may hold values from -0.5 to 0.5
Outputs:
- update: bfloat16 [352, 176, 128], P(('grp', 'row'), 'col'), parts along dimension 0
- pair_gradient: bfloat16 [352, 176, 128], P(('grp', 'row'), 'col'), parts along dimension 0
- grad_w_in: float32 [256, 640], P('grp'), parts along dimension 0
- grad_w_out: float32 [256, 128], P('grp'), parts along dimension 0
There are 2 independent parts, one for each index of `grp`. A program takes and returns all parts, laid end to end along the dimension named above; an argument that names none is the same for every part. Nothing has to cross between parts.
Inputs may be any that keep to these rules, and one draw needn't show every extreme that they name: Chain slot c holds positions c * 22 to c * 22 + chain_lengths[c] - 1; the entries sum to 132 and one of them equals 22.
All inputs are finite; a program needn't handle non-finite values.
Results may differ from a plain program's by a relative error of at most 0.017.
Values may be sent and summed in bfloat16 or wider, within the bound.
No kernel may reach another device: no remote copies, remote signals or barrier semaphores. Data moves between devices by JAX's collectives and lax.ppermute only.
A program may use at most 192 MiB of HBM per device.

v0:
```python
import functools
import math

import jax
import jax.numpy as jnp
from jax import lax
from jax.experimental import pallas as pl
from jax.experimental.pallas import tpu as pltpu
from jax.sharding import PartitionSpec as P

eps = 1e-05
f32 = jnp.float32
bf16 = jnp.bfloat16
VMEM = pl.BlockSpec(memory_space=pltpu.VMEM)
SMEM = pl.BlockSpec(memory_space=pltpu.SMEM)
ANY = pl.BlockSpec(memory_space=pl.ANY)
MIB = 1 << 20


def layer_norm_backward(output_gradient, standardized_input, inverse_deviation, norm_gain):
    scaled_output = output_gradient * norm_gain
    first_operand = jnp.mean(scaled_output, axis=-1, keepdims=True)
    second_operand = jnp.mean(scaled_output * standardized_input, axis=-1, keepdims=True)
    return inverse_deviation * (scaled_output - first_operand - standardized_input * second_operand)


def standardize(values):
    centered = values - jnp.mean(values, axis=-1, keepdims=True)
    inverse = lax.rsqrt(jnp.mean(centered * centered, axis=-1, keepdims=True) + eps)
    return centered * inverse, inverse


def dot(a, b, ca, cb):
    return lax.dot_general(a, b, (((ca,), (cb,)), ((), ())), preferred_element_type=f32)


def ring_order(row_count):
    if row_count == 8:
        return [0, 2, 4, 6, 7, 5, 3, 1]
    return list(range(row_count))


def ring_place(row_count, row):
    if row_count == 8:
        return jnp.where(row % 2 == 0, row // 2, row_count - 1 - row // 2)
    return row


def ring_row(row_count, place):
    if row_count == 8:
        return jnp.where(place < row_count // 2, 2 * place, 2 * (row_count - 1 - place) + 1)
    return place


def half_index(row_count, offset, letter):
    place = ring_place(row_count, lax.axis_index("row"))
    return ring_row(row_count, (place + offset + row_count) % row_count) * 2 + letter


def arrival_slot(row_count, index):
    hops = row_count // 2
    letter = index % 2
    apart = ring_place(row_count, index // 2) - ring_place(row_count, lax.axis_index("row"))
    apart = (apart + row_count) % row_count
    near = jnp.where(letter == 0, row_count - apart, apart)
    first = 4 * near - 2 + letter
    second = 4 * (row_count - near) - 2 + 3 - letter
    return jnp.where(apart == 0, letter, jnp.where(near <= hops, first, second))


def present_count(row_count, lengths, slot, short, where):
    start = half_index(row_count, *where) * short
    return jnp.clip(lengths[start // slot] - start % slot, 0, short)


def swap_col(x):
    return lax.ppermute(x, "col", [(0, 1), (1, 0)])


def add(a, b):
    return (a.astype(f32) + b.astype(f32)).astype(bf16)


def call(kernel, name, args, specs, outs, scratch=(), after=(), microseconds=0, limit=0):
    held = sum(a.size * a.dtype.itemsize for a, s in zip(args, specs) if s is VMEM)
    after = [x for x in after if x is not None]
    held += sum(int(o.size) * o.dtype.itemsize for o in outs)
    held += sum(math.prod(s.inner_aval.shape) * 4 for s in scratch)

    def body(*refs):
        kernel(*refs[: len(args)], *refs[len(args) + len(after) :])

    return pl.pallas_call(
        body,
        out_shape=list(outs),
        in_specs=list(specs) + [ANY] * len(after),
        out_specs=[VMEM] * len(outs),
        scratch_shapes=list(scratch),
        compiler_params=pltpu.CompilerParams(vmem_limit_bytes=limit or min(56 * MIB, held * 5 // 4 + 6 * MIB)),
        cost_estimate=pl.CostEstimate(
            flops=int(microseconds * 1.1e9) + 1024, bytes_accessed=1024, transcendentals=0
        ),
        name=name,
    )(*args, *after)


def tiles(half):
    return [(k, min(16, half - k)) for k in range(0, half, 16)]


def parts(short):
    return [(0, (short + 1) // 2), ((short + 1) // 2, short)]


def joined(terms):
    chains = [terms[0::2], terms[1::2]]
    sums = []
    for chain in chains:
        total = chain[0]
        for term in chain[1:]:
            total = total + term
        sums.append(total.astype(f32))
    return sums[0] + sums[1]


def wide_row(ref, *at):
    return jnp.broadcast_to(ref[at], (16, ref.shape[-1])).astype(bf16)


def shape_of(dims, dtype):
    return jax.ShapeDtypeStruct(dims, dtype)


def present_row(lengths, slot, position):
    return (position % slot < lengths[position // slot]).astype(f32)


def present_columns(lengths, slot, half):
    at = lax.axis_index("col") * half + lax.broadcasted_iota(jnp.int32, (half, 128), 0)
    chain = at // slot
    held = jnp.zeros((half, 128), jnp.int32)
    for c in range(lengths.shape[0]):
        held = jnp.where(chain == c, lengths[c], held)
    return (at - chain * slot < held).astype(f32)


def first_row(here):
    return lax.axis_index("row") * here


def input_kernel(slot, lengths, pair, gain, bias, w, right, normed, mask):
    here, half, hidden = pair.shape
    mask[...] = present_columns(lengths, slot, half)

    for i in range(here):
        standard, _ = standardize(pair[i].astype(f32))
        values = (standard * gain[...] + bias[...]).astype(bf16)
        normed[i] = values
        proj = dot(values, w[:, 2 * hidden : 4 * hidden], 1, 0)
        shown = mask[...] * present_row(lengths, slot, first_row(here) + i)
        gated = jax.nn.sigmoid(proj[:, :hidden]) * proj[:, hidden:]
        right[i] = (shown * gated).astype(bf16)


def by_rows(here, body):
    def step(t, carry):
        for x in range(here // 2):
            body(t * (here // 2) + x)
        return carry

    lax.fori_loop(0, 2, step, 0)


def left_kernel(slot, lengths, normed, cotangent, w, left, outs, mask):
    here, half, hidden = normed.shape
    halves, _, padded, _ = outs.shape
    short = half // halves
    mask[...] = present_columns(lengths, slot, half)

    def body(i):
        proj = dot(normed[i], w[:, : 2 * hidden], 1, 0)
        shown = mask[...] * present_row(lengths, slot, first_row(here) + i)
        gated = shown * jax.nn.sigmoid(proj[:, :hidden]) * proj[:, hidden:]
        left[i, pl.ds(0, half), :] = gated.astype(bf16)
        if left.shape[1] > half:
            left[i, pl.ds(half, left.shape[1] - half), :] = jnp.zeros(
                (left.shape[1] - half, hidden), bf16
            )
        gate = jax.nn.sigmoid(dot(normed[i], w[:, 4 * hidden :], 1, 0))
        grads = cotangent[i].astype(f32) * gate
        empty = jnp.zeros((padded - short, hidden), f32)
        for m in range(halves):
            part = grads[m * short : (m + 1) * short]
            outs[m, i] = jnp.concatenate([part, empty], axis=0).astype(bf16)

    by_rows(here, body)


def triangle_kernel(row_count, slot, halves, arrays, lengths, left, *refs):
    rights, (out, rows, which) = refs[:arrays], refs[arrays:]
    here, deep, hidden = left.shape
    half = rights[0].shape[1]
    padded = out.shape[2]
    short = here // 2
    row = lax.broadcasted_iota(jnp.int32, which.shape, 0)
    lane = lax.broadcasted_iota(jnp.int32, which.shape, 1)
    which[...] = ((lane >= row * deep) & (lane < (row + 1) * deep)).astype(f32).astype(bf16)
    for s, (array, first, place) in enumerate(halves):
        rows[...] = jnp.zeros_like(rows)

        def column(j, carry, right=rights[array], first=first):
            held = right[first + j]
            if deep > half:
                held = jnp.concatenate([held, jnp.zeros((deep - half, hidden), bf16)], axis=0)
            products = jnp.concatenate([left[i] * held for i in range(here)], axis=0)
            total = dot(which[...], products, 1, 0)
            rows[pl.ds(j, here, stride=padded), :] = total[:here]
            return carry

        present = present_count(row_count, lengths, slot, short, place)
        lax.fori_loop(0, present, column, 0)
        out[s] = rows[...].astype(bf16).reshape(here, padded, hidden)


def triangle(row_count, slot, halves, lengths, left, rights, padded, after):
    count, (here, deep, hidden) = len(halves), left.shape
    return call(
        functools.partial(triangle_kernel, row_count, slot, halves, len(rights)),
        "triangle",
        [lengths, left, *rights],
        [SMEM] + [VMEM] * (len(rights) + 1),
        [shape_of((count, here, padded, hidden), bf16)],
        [
            pltpu.VMEM((here * padded, hidden), f32),
            pltpu.VMEM(((here + 15) // 16 * 16, here * deep), bf16),
        ],
        after,
    )[0]


def triangle_norm_kernel(
    row_count, places, mine, other, mine_out, other_out, w_out, gain, bias, grad, normed
):
    count, here, padded, hidden = mine.shape
    flat = (here * padded, hidden)

    for s in range(count):
        index = half_index(row_count, *places[s])
        outs = jnp.where(
            index // row_count == lax.axis_index("col"),
            mine_out[index % row_count],
            other_out[index % row_count],
        )
        total = (mine[s].astype(f32) + other[s].astype(f32)).reshape(flat)
        standard, inverse = standardize(total)
        normed[s] = (standard * gain[...] + bias[...]).astype(bf16).reshape(here, padded, hidden)
        grad_norm = dot(outs.reshape(flat), w_out[...], 1, 1)
        result = layer_norm_backward(grad_norm, standard, inverse, gain[...])
        grad[s] = result.astype(bf16).reshape(here, padded, hidden)


def triangle_norm(row_count, places, mine, other, outs, w_out, gain, bias, after):
    return call(
        functools.partial(triangle_norm_kernel, row_count, places),
        "triangle_norm",
        [mine, other, *outs, w_out, gain, bias],
        [VMEM] * 7,
        [shape_of(mine.shape, bf16)] * 2,
        (),
        after,
    )


def hop_kernel(row_count, slot, places, picks, carried, lengths, left, *refs):
    count = len(picks)
    grads, refs = refs[:count], refs[count:]
    arrived, refs = refs[: count * carried], refs[count * carried :]
    outs, wide = refs[:count], refs[count]
    here = left.shape[0]
    short, half, hidden = outs[0].shape
    for s in range(count):
        wide[...] = grads[s][picks[s]].astype(f32)
        out = outs[s]

        def columns(at, s=s, out=out):
            totals = []
            for j in at:
                total = []
                for k, size in tiles(half):
                    start = jnp.zeros((size, hidden), f32)
                    for more in range(carried):
                        start += arrived[s + more * count][j, pl.ds(k, size), :].astype(f32)
                    total.append(start)
                totals.append(total)
            for low in range(0, here, short):
                chosen = range(low, min(low + short, here))
                weights = [[wide_row(wide, i, pl.ds(j, 1)) for i in chosen] for j in at]
                for t, (k, size) in enumerate(tiles(half)):
                    held = [left[i, pl.ds(k, size), :] for i in chosen]
                    for total, weight in zip(totals, weights):
                        total[t] += joined([w[:size] * h for w, h in zip(weight, held)])
            for j, total in zip(at, totals):
                for t, (k, size) in enumerate(tiles(half)):
                    out[j, pl.ds(k, size), :] = total[t].astype(out.dtype)

        present = present_count(row_count, lengths, slot, short, places[s])
        for low, high in parts(short):

            @pl.when(present > low)
            def _(low=low, high=high, columns=columns):
                for j in range(low, high, 2):
                    columns(range(j, min(j + 2, high)))

            @pl.when(present <= low)
            def _(low=low, high=high, out=out):
                out[pl.ds(low, high - low)] = jnp.zeros((high - low, half, hidden), out.dtype)


def hop(row_count, slot, places, lengths, left, grads, picks, arrived, out, dtype, after):
    count = len(grads)
    carried = len(arrived) // count
    return call(
        functools.partial(hop_kernel, row_count, slot, places, picks, carried),
        "scatter_hop",
        [lengths, left, *grads, *arrived],
        [SMEM] + [VMEM] * (1 + count + len(arrived)),
        [shape_of(out, dtype)] * count,
        [pltpu.VMEM(grads[0].shape[1:], f32)],
        after,
    )


def left_gradient_kernel(halves, picks, arrays, carried, grads, *refs):
    count = len(picks)
    rights, refs = refs[:arrays], refs[arrays:]
    before, (out, wide) = refs[:carried], refs[carried:]
    here, half, hidden = out.shape
    short = here // 2
    for s, pick in enumerate(picks):
        wide[s] = grads[pick].astype(f32)

    def row(pair, carry):
        rows = (2 * pair, 2 * pair + 1)
        for s, pick in enumerate(picks):
            array, first, _ = halves[pick]
            weights = [[wide_row(wide, s, i, pl.ds(j, 1)) for j in range(short)] for i in rows]
            for k, size in tiles(half):
                held = [rights[array][first + j, pl.ds(k, size), :] for j in range(short)]
                for i, weight in zip(rows, weights):
                    total = joined([w[:size] * h for w, h in zip(weight, held)])
                    if s:
                        total += out[i, pl.ds(k, size), :]
                    elif carried:
                        total += before[0][i, pl.ds(k, size), :]
                    out[i, pl.ds(k, size), :] = total
        return carry

    lax.fori_loop(0, here // 2, row, 0)


def left_gradient(halves, picks, grads, rights, before, after):
    count, here = len(picks), grads.shape[1]
    half, hidden = rights[0].shape[1:]
    return call(
        functools.partial(left_gradient_kernel, halves, picks, len(rights), len(before)),
        "left_gradient",
        [grads, *rights, *before],
        [VMEM] * (1 + len(rights) + len(before)),
        [shape_of((here, half, hidden), f32)],
        [pltpu.VMEM((count,) + grads.shape[1:], f32)],
        after,
    )[0]


def output_kernel(
    row_count, slot, counts, lengths, normed, cotangent, grad_left, w, w_out, outs, *refs
):
    norms, (update, gradient, total, mask, picked) = refs[: len(counts)], refs[len(counts) :]
    here, half, hidden = normed.shape
    halves, _, padded, _ = picked.shape
    short = half // halves
    mask[...] = present_columns(lengths, slot, half)
    total[...] = jnp.zeros_like(total)
    for m in range(halves):
        low = 0
        stands = arrival_slot(row_count, lax.axis_index("col") * row_count + m)
        for norm, count in zip(norms, counts):

            @pl.when((stands >= low) & (stands < low + count))
            def _(m=m, norm=norm, low=low, stands=stands):
                picked[m] = norm[stands - low]

            low += count

    def body(i):
        values = normed[i]
        proj = dot(values, w[:, : 2 * hidden], 1, 0)
        sig_left = jax.nn.sigmoid(proj[:, :hidden])
        val_left = proj[:, hidden:]
        gate = jax.nn.sigmoid(dot(values, w[:, 4 * hidden :], 1, 0))
        tri = picked[:, i].reshape(halves * padded, hidden)
        product = dot(tri, w_out[...], 1, 0)
        projected = jnp.concatenate(
            [product[m * padded : m * padded + short] for m in range(halves)], axis=0
        )
        update[i] = (gate * projected).astype(bf16)
        grad_gate = (cotangent[i].astype(f32) * projected * gate * (1.0 - gate)).astype(bf16)
        shown = mask[...] * present_row(lengths, slot, first_row(here) + i)
        masked = grad_left[i] * shown
        grads = jnp.concatenate(
            [masked * val_left * sig_left * (1.0 - sig_left), masked * sig_left], axis=1
        ).astype(bf16)
        gradient[i] = dot(grads, w[:, : 2 * hidden], 1, 1) + dot(
            grad_gate, w[:, 4 * hidden :], 1, 1
        )
        total[:, : 2 * hidden] += dot(values, grads, 0, 0)
        total[:, 2 * hidden : 3 * hidden] += dot(values, grad_gate, 0, 0)
        total[:, 3 * hidden :] += dot(tri, outs[:, i].reshape(halves * padded, hidden), 0, 0)

    by_rows(here, body)


def right_gradient_kernel(slot, lengths, normed, w, early, own_a, own_b, *refs):
    arrived, (grads, keep, give, mask, total) = refs[:4], refs[4:]
    here, half, hidden = normed.shape
    short = here // 2
    mask[...] = present_columns(lengths, slot, half)
    total[...] = jnp.zeros_like(total)

    for own, others, first in ((own_a, arrived[:2], 0), (own_b, arrived[2:], short)):
        for t in range(short):
            j = first + t
            values = normed[j]
            proj = dot(values, w[:, 2 * hidden : 4 * hidden], 1, 0)
            sig_right = jax.nn.sigmoid(proj[:, :hidden])
            val_right = proj[:, hidden:]
            shown = mask[...] * present_row(lengths, slot, first_row(here) + j)
            masked = shown * (own[t] + others[0][t].astype(f32) + others[1][t].astype(f32))
            result = jnp.concatenate(
                [masked * val_right * sig_right * (1.0 - sig_right), masked * sig_right], axis=1
            ).astype(bf16)
            grads[j] = result
            total[...] += dot(values, result, 0, 0)
    rows, wide = keep.shape[0], early.shape[1]
    col = lax.axis_index("col")
    for out, start in ((keep, col * rows), (give, (1 - col) * rows)):
        chosen = pl.ds(pl.multiple_of(start, rows), rows)
        out[:, :wide] = early[chosen, :].astype(bf16)
        out[:, wide:] = total[chosen, :].astype(bf16)


def pair_gradient_kernel(pair, grads, gain, w, *refs):
    gradients, out = refs[:-1], refs[-1]
    hidden = pair.shape[2]

    i = 0
    for gradient in gradients:
        for at in range(gradient.shape[0]):
            standard, inverse = standardize(pair[i].astype(f32))
            total = gradient[at] + dot(grads[i], w[:, 2 * hidden : 4 * hidden], 1, 1)
            out[i] = layer_norm_backward(total, standard, inverse, gain[...]).astype(bf16)
            i += 1


def weights_kernel(mine, other, w_in, w_out):
    rows, hidden = mine.shape[0], w_out.shape[0]
    col = lax.axis_index("col")
    for part, start in ((mine, col * rows), (other, (1 - col) * rows)):
        chosen = pl.ds(pl.multiple_of(start, rows), rows)
        w_in[chosen, : 2 * hidden] = part[:, : 2 * hidden].astype(f32)
        w_in[chosen, 2 * hidden : 4 * hidden] = part[:, 4 * hidden :].astype(f32)
        w_in[chosen, 4 * hidden :] = part[:, 2 * hidden : 3 * hidden].astype(f32)
        w_out[chosen, :] = part[:, 3 * hidden : 4 * hidden].astype(f32)


def shards(
    pair,
    cotangent,
    chain_lengths,
    input_norm_gain,
    input_norm_bias,
    w_in,
    output_norm_gain,
    output_norm_bias,
    w_out,
):
    here, half, channels = pair.shape
    hidden = w_out.shape[0]
    row_count = lax.axis_size("row")
    slot = here * row_count // chain_lengths.shape[0]
    order = ring_order(row_count)
    short = here // 2
    padded = (short + 15) // 16 * 16
    forward = [(order[p], order[(p + 1) % row_count]) for p in range(row_count)]
    backward = [(order[p], order[(p - 1) % row_count]) for p in range(row_count)]
    in_gain, in_bias = input_norm_gain.reshape(1, -1), input_norm_bias.reshape(1, -1)
    out_gain, out_bias = output_norm_gain.reshape(1, -1), output_norm_bias.reshape(1, -1)
    block = (here, half, hidden)
    mask = pltpu.VMEM((half, 128), f32)

    def ahead(x):
        return lax.ppermute(x, "row", forward)

    def behind(x):
        return lax.ppermute(x, "row", backward)

    right, normed = call(
        functools.partial(input_kernel, slot),
        "input_side",
        [chain_lengths, pair, in_gain, in_bias, w_in],
        [SMEM] + [VMEM] * 4,
        [shape_of(block, bf16)] * 2,
        [mask],
    )

    hops = row_count // 2
    groups = [[right]]
    halves = [[(0, 0, (0, 0)), (0, short, (0, 1))]]
    for s in range(1, hops):
        halves.append(
            [(0, 0, (-s, 0)), (1, short, (s, 1)), (0, short, (-s, 1)), (1, 0, (s, 0))]
        )
    halves.append([(0, 0, (-hops, 0)), (1, 0, (hops, 1))])

    def gather(s, x, y):
        if s == hops:
            x, y = x[:short], y[short:]
        groups.append([ahead(x), behind(y)])

    gather(1, right, right)
    left, mine_out = call(
        functools.partial(left_kernel, slot),
        "left_side",
        [chain_lengths, normed, cotangent, w_in],
        [SMEM] + [VMEM] * 3,
        [
            shape_of((here, (half + 15) // 16 * 16, hidden), bf16),
            shape_of((row_count, here, padded, hidden), bf16),
        ],
        [mask],
        microseconds=4,
    )
    other_out = swap_col(mine_out)

    norms, grads, partials, others = [], [], [], []
    last = [left]
    pieces = []

    def triangles(s):
        partials.append(
            triangle(row_count, slot, halves[s], chain_lengths, left, groups[s], padded, last)
        )
        others.append(swap_col(partials[s]))
        last[:] = [partials[s]]

    def normal(s):
        places = [place for _, _, place in halves[s]]
        grad, norm = triangle_norm(
            row_count, places, partials[s], others[s], [mine_out, other_out], w_out, out_gain, out_bias, last
        )
        grads.append(grad)
        norms.append(norm)
        last[:] = [grad]

    def add_left(s):
        picks = range(len(halves[s]))
        pieces[:] = [
            left_gradient(halves[s], picks, grads[s], groups[s], pieces[:], last)
        ]
        last[:] = pieces

    def scatter(s, picks, arrived, dtype=bf16):
        x, y = hop(
            row_count,
            slot,
            [halves[s][pick][2] for pick in picks],
            chain_lengths,
            left,
            [grads[s]] * 2,
            picks,
            arrived,
            (short, half, hidden),
            dtype,
            last,
        )
        last[:] = [x]
        return x, y

    arrived = {0: [], 1: []}

    def send(s, chain):
        x, y = scatter(s, [2 * chain, 2 * chain + 1], arrived[chain])
        arrived[chain] = [behind(x), ahead(y)]

    def output_side():
        return call(
            functools.partial(output_kernel, row_count, slot, [len(h) for h in halves]),
            "output_side",
            [chain_lengths, normed, cotangent, pieces[0], w_in, w_out, mine_out, *norms],
            [SMEM] + [VMEM] * (6 + len(norms)),
            [
                shape_of(block, bf16),
                shape_of(block, f32),
                shape_of((channels, 4 * hidden), f32),
            ],
            [
                mask,
                pltpu.VMEM((row_count, here, padded, hidden), bf16),
            ],
            last,
            microseconds=6,
        )

    for s in range(hops + 1):
        triangles(s)
        if s:
            add_left(s - 1)
        normal(s)
        if s == hops - 1:
            send(s, 1)
        elif s < hops:
            x, y, _ = lax.optimization_barrier((*groups[s + 1], last[0]))
            gather(s + 2, x, y)
    send(hops, 0)
    add_left(hops)
    send(hops - 2, 1)
    for s in range(hops - 1, 0, -1):
        if s == 1:
            own_a, own_b = scatter(0, [0, 1], [], f32)
        send(s, 0)
        if s > 2:
            send(s - 2, 1)
    update, gradient, early = output_side()
    arrived1, arrived2 = arrived[0], [arrived[1][1], arrived[1][0]]

    late, keep, give = call(
        functools.partial(right_gradient_kernel, slot),
        "right_gradient",
        [chain_lengths, normed, w_in, early, own_a, own_b]
        + [arrived1[0], arrived2[0], arrived1[1], arrived2[1]],
        [SMEM] + [VMEM] * 9,
        [shape_of((here, half, 2 * hidden), bf16)]
        + [shape_of((channels // 2, 6 * hidden), bf16)] * 2,
        [mask, pltpu.VMEM((channels, 2 * hidden), f32)],
    )
    mine = add(keep, swap_col(give))
    step = 1
    while step < row_count:
        mine = add(
            mine, lax.ppermute(mine, "row", [(r, r ^ step) for r in range(row_count)])
        )
        step *= 2
    (pair_gradient,) = call(
        pair_gradient_kernel,
        "pair_gradient",
        [pair, late, in_gain, w_in, gradient],
        [VMEM] * 5,
        [shape_of(block, bf16)],
        microseconds=3,
    )
    mine, pair_gradient = lax.optimization_barrier((mine, pair_gradient))
    grad_w_in, grad_w_out = call(
        weights_kernel,
        "weight_gradients",
        [mine, swap_col(mine)],
        [VMEM] * 2,
        [shape_of(w_in.shape, f32), shape_of(w_out.shape, f32)],
    )
    return (update, pair_gradient, grad_w_in, grad_w_out)


def solution(mesh):
    placed = (
        P(("grp", "row"), "col", None),
        P(("grp", "row"), "col", None),
        P("grp"),
        P(),
        P(),
        P(),
        P(),
        P(),
        P(),
    )
    return jax.shard_map(
        shards,
        mesh=mesh,
        in_specs=placed,
        out_specs=(
            P(("grp", "row"), "col", None),
            P(("grp", "row"), "col", None),
            P("grp", None),
            P("grp", None),
        ),
        check_vma=False,
    )
```

profile of v0, /device:TPU:0, one launch (start us, length us, event | category | flops | bytes accessed | tf_op | source)
XLA Modules:
  0.0 144.4 jit_solution(4322500016743683395)
XLA Ops:
  0.7 0.6 copy-done.5
  1.3 0.9 copy-done.1
  2.2 1.0 copy-done.3
  3.3 1.5 %input_side.1 = (bf16[22,88,128]{2,1,0:T(8,128)(2,1)S(1)}, bf16[22,88,128]{2,1,0:T(8,128)(2,1)S(1)}) custom-call(s32[8]{0:T(128)S(1)} %copy-done.5, bf16[22,88,128]{2,1,0:T(8,128)(2,1)S(1)} %copy-done.3, f32[1,128]{1,0:T(1,128)S(1)} %bitcast.15, f32[1,128]{1,0:T(1,128)S(1)} %bitcast.14, bf16[128,640]{1,0:T(8,128)(2,1)S(1)} %copy-done.1), custom_call_target="tpu_custom_call" | custom-call | flops 1024 | bytes 1024 | tf_op jit(solution)/shard_map/input_side/pallas_call | solution.py:93
  4.8 1.4 left_side.1
  6.7 2.6 %collective-permute-start.1 = (bf16[22,88,128]{2,1,0:T(8,128)(2,1)S(1)}, bf16[22,88,128]{2,1,0:T(8,128)(2,1)S(1)}, u32[]{:S(2)}, u32[]{:S(2)}) collective-permute-start(bf16[22,88,128]{2,1,0:T(8,128)(2,1)S(1)} %get-tuple-element.52.refs_2_.refs_1_), channel_id=1, source_target_pairs={{0,2},{4,0},{8,4},{12,8},{14,12},{10,14},{6,10},{2,6},{1,3},{5,1},... | collective-permute-start | bytes 1486856 | tf_op jit(solution)/shard_map/ppermute | solution.py:505
  9.4 5.4 %triangle.5.refs_0_.refs_7_ = bf16[2,22,16,128]{3,2,1,0:T(8,128)(2,1)S(1)} custom-call(s32[8]{0:T(128)S(1)} %copy-done.5, bf16[22,96,128]{2,1,0:T(8,128)(2,1)S(1)} %get-tuple-element.51.refs_1_.refs_3_, bf16[22,88,128]{2,1,0:T(8,128)(2,1)S(1)} %get-tuple-element.52.refs_2_.refs_1_, bf16[22,96,128]{2,1,0:T(8,128)(2,1)S(1)} %get-tuple-element.51.refs_1_.refs_3_), custom_call_target="tpu_custom_call" | custom-call | flops 1024 | bytes 1024 | tf_op jit(solution)/shard_map/triangle/pallas_call | solution.py:93
  14.9 1.3 collective-permute-done.2.refs_1_
  16.3 0.6 copy-done.6
  17.5 3.7 %collective-permute-done.1.refs_3_.refs_2_ = bf16[22,88,128]{2,1,0:T(8,128)(2,1)S(1)} collective-permute-done((bf16[22,88,128]{2,1,0:T(8,128)(2,1)S(1)}, bf16[22,88,128]{2,1,0:T(8,128)(2,1)S(1)}, u32[]{:S(2)}, u32[]{:S(2)}) %collective-permute-start.1) | collective-permute-done | bytes 495648 | tf_op jit(solution)/shard_map/ppermute | solution.py:505
  21.2 1.4 collective-permute-done.refs_2_.refs_1_
  23.0 1.7 %collective-permute-start.5 = (bf16[22,88,128]{2,1,0:T(8,128)(2,1)S(1)}, bf16[22,88,128]{2,1,0:T(8,128)(2,1)S(1)}, u32[]{:S(2)}, u32[]{:S(2)}) collective-permute-start(bf16[22,88,128]{2,1,0:T(8,128)(2,1)S(1)} %collective-permute-done.1.refs_3_.refs_2_), channel_id=1, source_target_pairs={{0,2},{4,0},{8,4},{12,8},{14,12},{10,14},{6,10},{2,6},{1,3},{5,1},... | collective-permute-start | bytes 1486856 | tf_op jit(solution)/shard_map/ppermute | solution.py:505
  24.7 7.6 %triangle.6.refs_2_.refs_0_ = bf16[4,22,16,128]{3,2,1,0:T(8,128)(2,1)S(1)} custom-call(s32[8]{0:T(128)S(1)} %copy-done.5, bf16[22,96,128]{2,1,0:T(8,128)(2,1)S(1)} %get-tuple-element.51.refs_1_.refs_3_, bf16[22,88,128]{2,1,0:T(8,128)(2,1)S(1)} %collective-permute-done.refs_2_.refs_1_, bf16[22,88,128]{2,1,0:T(8,128)(2,1)S(1)} %collective-permute-done.1.refs_3_.refs_2_, ...), custom_call_target="tpu_custom_call" | custom-call | flops 1024 | bytes 1024 | tf_op jit(solution)/shard_map/triangle/pallas_call | solution.py:93
  32.4 1.1 left_gradient.5.refs_7_.refs_3_
  34.1 1.0 triangle_norm.6
  35.6 1.6 %collective-permute-start.7 = (bf16[22,88,128]{2,1,0:T(8,128)(2,1)S(1)}, bf16[22,88,128]{2,1,0:T(8,128)(2,1)S(1)}, u32[]{:S(2)}, u32[]{:S(2)}) collective-permute-start(bf16[22,88,128]{2,1,0:T(8,128)(2,1)S(1)} %collective-permute-done.4.refs_2_.refs_1_), channel_id=1, source_target_pairs={{0,4},{4,8},{8,12},{12,14},{14,10},{10,6},{6,2},{2,0},{1,5},{5,9},... | collective-permute-start | bytes 1486856 | tf_op jit(solution)/shard_map/ppermute | solution.py:502
  37.2 2.0 %collective-permute-start.8 = (bf16[22,88,128]{2,1,0:T(8,128)(2,1)S(1)}, bf16[22,88,128]{2,1,0:T(8,128)(2,1)S(1)}, u32[]{:S(2)}, u32[]{:S(2)}) collective-permute-start(bf16[22,88,128]{2,1,0:T(8,128)(2,1)S(1)} %collective-permute-done.5.refs_3_.refs_2_), channel_id=1, source_target_pairs={{0,2},{4,0},{8,4},{12,8},{14,12},{10,14},{6,10},{2,6},{1,3},{5,1},... | collective-permute-start | bytes 1486856 | tf_op jit(solution)/shard_map/ppermute | solution.py:505
  39.1 9.1 %triangle.7.refs_4_.refs_0_ = bf16[4,22,16,128]{3,2,1,0:T(8,128)(2,1)S(1)} custom-call(s32[8]{0:T(128)S(1)} %copy-done.5, bf16[22,96,128]{2,1,0:T(8,128)(2,1)S(1)} %get-tuple-element.51.refs_1_.refs_3_, bf16[22,88,128]{2,1,0:T(8,128)(2,1)S(1)} %collective-permute-done.4.refs_2_.refs_1_, bf16[22,88,128]{2,1,0:T(8,128)(2,1)S(1)} %collective-permute-done.5.refs_3_.refs_2_, ...), custom_call_target="tpu_custom_call" | custom-call | flops 1024 | bytes 1024 | tf_op jit(solution)/shard_map/triangle/pallas_call | solution.py:93
  48.4 2.3 %left_gradient.6.refs_7_.refs_3_ = f32[22,88,128]{2,1,0:T(8,128)S(1)} custom-call(bf16[4,22,16,128]{3,2,1,0:T(8,128)(2,1)S(1)} %get-tuple-element.57.refs_4_.refs_0_.refs_2_.refs_3_, bf16[22,88,128]{2,1,0:T(8,128)(2,1)S(1)} %collective-permute-done.refs_2_.refs_1_, bf16[22,88,128]{2,1,0:T(8,128)(2,1)S(1)} %collective-permute-done.1.refs_3_.refs_2_, ...), custom_call_target="tpu_custom_call" | custom-call | flops 1024 | bytes 1024 | tf_op jit(solution)/shard_map/left_gradient/pallas_call | solution.py:93
  50.7 1.0 triangle_norm.7
  51.7 5.9 %triangle.8.refs_4_.refs_0_ = bf16[4,22,16,128]{3,2,1,0:T(8,128)(2,1)S(1)} custom-call(s32[8]{0:T(128)S(1)} %copy-done.5, bf16[22,96,128]{2,1,0:T(8,128)(2,1)S(1)} %get-tuple-element.51.refs_1_.refs_3_, bf16[22,88,128]{2,1,0:T(8,128)(2,1)S(1)} %collective-permute-done.7.refs_2_.refs_1_, bf16[22,88,128]{2,1,0:T(8,128)(2,1)S(1)} %collective-permute-done.8.refs_3_.refs_2_, ...), custom_call_target="tpu_custom_call" | custom-call | flops 1024 | bytes 1024 | tf_op jit(solution)/shard_map/triangle/pallas_call | solution.py:93
  58.2 2.3 %collective-permute-start.11 = (bf16[11,88,128]{2,1,0:T(8,128)(2,1)S(1)}, bf16[11,88,128]{2,1,0:T(8,128)(2,1)S(1)}, u32[]{:S(2)}, u32[]{:S(2)}) collective-permute-start(bf16[11,88,128]{2,1,0:T(8,128)(2,1)S(1)} %slice.7), channel_id=1, source_target_pairs={{0,2},{4,0},{8,4},{12,8},{14,12},{10,14},{6,10},{2,6},{1,3},{5,1},... | collective-permute-start | bytes 743432 | tf_op jit(solution)/shard_map/ppermute | solution.py:505
  60.5 2.3 %left_gradient.7.refs_7_.refs_3_ = f32[22,88,128]{2,1,0:T(8,128)S(1)} custom-call(bf16[4,22,16,128]{3,2,1,0:T(8,128)(2,1)S(1)} %get-tuple-element.60.refs_4_.refs_0_.refs_2_.refs_3_, bf16[22,88,128]{2,1,0:T(8,128)(2,1)S(1)} %collective-permute-done.4.refs_2_.refs_1_, bf16[22,88,128]{2,1,0:T(8,128)(2,1)S(1)} %collective-permute-done.5.refs_3_.refs_2_, ...), custom_call_target="tpu_custom_call" | custom-call | flops 1024 | bytes 1024 | tf_op jit(solution)/shard_map/left_gradient/pallas_call | solution.py:93
  62.8 1.0 triangle_norm.8
  63.8 1.2 scatter_hop.8
  65.0 1.4 collective-permute-done.11.refs_3_.refs_2_
  66.4 2.2 %collective-permute-done.10.refs_2_.refs_1_ = bf16[11,88,128]{2,1,0:T(8,128)(2,1)S(1)} collective-permute-done((bf16[11,88,128]{2,1,0:T(8,128)(2,1)S(1)}, bf16[11,88,128]{2,1,0:T(8,128)(2,1)S(1)}, u32[]{:S(2)}, u32[]{:S(2)}) %collective-permute-start.10) | collective-permute-done | bytes 247840 | tf_op jit(solution)/shard_map/ppermute | solution.py:502
  68.6 3.9 %triangle.9.refs_4_.refs_0_ = bf16[2,22,16,128]{3,2,1,0:T(8,128)(2,1)S(1)} custom-call(s32[8]{0:T(128)S(1)} %copy-done.5, bf16[22,96,128]{2,1,0:T(8,128)(2,1)S(1)} %get-tuple-element.51.refs_1_.refs_3_, bf16[11,88,128]{2,1,0:T(8,128)(2,1)S(1)} %collective-permute-done.10.refs_2_.refs_1_, bf16[11,88,128]{2,1,0:T(8,128)(2,1)S(1)} %collective-permute-done.11.refs_3_.refs_2_, ...), custom_call_target="tpu_custom_call" | custom-call | flops 1024 | bytes 1024 | tf_op jit(solution)/shard_map/triangle/pallas_call | solution.py:93
  72.6 1.3 collective-permute-start.16
  74.0 0.7 collective-permute-start.17
  74.7 2.3 %left_gradient.8.refs_7_.refs_3_ = f32[22,88,128]{2,1,0:T(8,128)S(1)} custom-call(bf16[4,22,16,128]{3,2,1,0:T(8,128)(2,1)S(1)} %get-tuple-element.63.refs_2_.refs_3_.refs_4_.refs_0_, bf16[22,88,128]{2,1,0:T(8,128)(2,1)S(1)} %collective-permute-done.7.refs_2_.refs_1_, bf16[22,88,128]{2,1,0:T(8,128)(2,1)S(1)} %collective-permute-done.8.refs_3_.refs_2_, ...), custom_call_target="tpu_custom_call" | custom-call | flops 1024 | bytes 1024 | tf_op jit(solution)/shard_map/left_gradient/pallas_call | solution.py:93
  77.5 1.6 %scatter_hop.9 = (bf16[11,88,128]{2,1,0:T(8,128)(2,1)S(1)}, bf16[11,88,128]{2,1,0:T(8,128)(2,1)S(1)}) custom-call(s32[8]{0:T(128)S(1)} %copy-done.5, bf16[22,96,128]{2,1,0:T(8,128)(2,1)S(1)} %get-tuple-element.51.refs_1_.refs_3_, bf16[2,22,16,128]{3,2,1,0:T(8,128)(2,1)S(1)} %get-tuple-element.65.refs_2_.refs_3_.refs_4_.refs_0_, ...), custom_call_target="tpu_custom_call" | custom-call | flops 1024 | bytes 1024 | tf_op jit(solution)/shard_map/scatter_hop/pallas_call | solution.py:93
  79.2 1.4 collective-permute-start.15
  80.6 0.8 collective-permute-start.14
  81.4 1.2 left_gradient.9.refs_6_.refs_3_
  82.6 1.0 collective-permute-done.17.refs_5_
  83.6 1.7 %scatter_hop.10 = (bf16[11,88,128]{2,1,0:T(8,128)(2,1)S(1)}, bf16[11,88,128]{2,1,0:T(8,128)(2,1)S(1)}) custom-call(s32[8]{0:T(128)S(1)} %copy-done.5, bf16[22,96,128]{2,1,0:T(8,128)(2,1)S(1)} %get-tuple-element.51.refs_1_.refs_3_, bf16[4,22,16,128]{3,2,1,0:T(8,128)(2,1)S(1)} %get-tuple-element.60.refs_4_.refs_0_.refs_2_.refs_3_, ...), custom_call_target="tpu_custom_call" | custom-call | flops 1024 | bytes 1024 | tf_op jit(solution)/shard_map/scatter_hop/pallas_call | solution.py:93
  85.8 1.6 %collective-permute-start.20 = (bf16[11,88,128]{2,1,0:T(8,128)(2,1)S(1)}, bf16[11,88,128]{2,1,0:T(8,128)(2,1)S(1)}, u32[]{:S(2)}, u32[]{:S(2)}) collective-permute-start(bf16[11,88,128]{2,1,0:T(8,128)(2,1)S(1)} %get-tuple-element.74.refs_6_), channel_id=1, source_target_pairs={{0,2},{4,0},{8,4},{12,8},{14,12},{10,14},{6,10},{2,6},{1,3},{5,1},... | collective-permute-start | bytes 743432 | tf_op jit(solution)/shard_map/ppermute | solution.py:505
  87.4 1.5 %collective-permute-done.15.refs_5_ = bf16[11,88,128]{2,1,0:T(8,128)(2,1)S(1)} collective-permute-done((bf16[11,88,128]{2,1,0:T(8,128)(2,1)S(1)}, bf16[11,88,128]{2,1,0:T(8,128)(2,1)S(1)}, u32[]{:S(2)}, u32[]{:S(2)}) %collective-permute-start.15) | collective-permute-done | bytes 247840 | tf_op jit(solution)/shard_map/ppermute | solution.py:502
  88.9 0.7 collective-permute-done.14.refs_4_
  89.6 1.5 %scatter_hop.11 = (bf16[11,88,128]{2,1,0:T(8,128)(2,1)S(1)}, bf16[11,88,128]{2,1,0:T(8,128)(2,1)S(1)}) custom-call(s32[8]{0:T(128)S(1)} %copy-done.5, bf16[22,96,128]{2,1,0:T(8,128)(2,1)S(1)} %get-tuple-element.51.refs_1_.refs_3_, bf16[4,22,16,128]{3,2,1,0:T(8,128)(2,1)S(1)} %get-tuple-element.63.refs_2_.refs_3_.refs_4_.refs_0_, ...), custom_call_target="tpu_custom_call" | custom-call | flops 1024 | bytes 1024 | tf_op jit(solution)/shard_map/scatter_hop/pallas_call | solution.py:93
  91.1 1.8 %collective-permute-start.19 = (bf16[11,88,128]{2,1,0:T(8,128)(2,1)S(1)}, bf16[11,88,128]{2,1,0:T(8,128)(2,1)S(1)}, u32[]{:S(2)}, u32[]{:S(2)}) collective-permute-start(bf16[11,88,128]{2,1,0:T(8,128)(2,1)S(1)} %get-tuple-element.76), channel_id=1, source_target_pairs={{0,4},{4,8},{8,12},{12,14},{14,10},{10,6},{6,2},{2,0},{1,5},{5,9},... | collective-permute-start | bytes 743432 | tf_op jit(solution)/shard_map/ppermute | solution.py:502
  93.2 1.2 collective-permute-done.21.refs_5_
  94.8 1.5 %scatter_hop.12 = (bf16[11,88,128]{2,1,0:T(8,128)(2,1)S(1)}, bf16[11,88,128]{2,1,0:T(8,128)(2,1)S(1)}) custom-call(s32[8]{0:T(128)S(1)} %copy-done.5, bf16[22,96,128]{2,1,0:T(8,128)(2,1)S(1)} %get-tuple-element.51.refs_1_.refs_3_, bf16[4,22,16,128]{3,2,1,0:T(8,128)(2,1)S(1)} %get-tuple-element.57.refs_4_.refs_0_.refs_2_.refs_3_, ...), custom_call_target="tpu_custom_call" | custom-call | flops 1024 | bytes 1024 | tf_op jit(solution)/shard_map/scatter_hop/pallas_call | solution.py:93
  96.3 2.7 %collective-permute-done.19.refs_5_ = bf16[11,88,128]{2,1,0:T(8,128)(2,1)S(1)} collective-permute-done((bf16[11,88,128]{2,1,0:T(8,128)(2,1)S(1)}, bf16[11,88,128]{2,1,0:T(8,128)(2,1)S(1)}, u32[]{:S(2)}, u32[]{:S(2)}) %collective-permute-start.19) | collective-permute-done | bytes 247840 | tf_op jit(solution)/shard_map/ppermute | solution.py:502
  99.4 1.7 %scatter_hop.13 = (bf16[11,88,128]{2,1,0:T(8,128)(2,1)S(1)}, bf16[11,88,128]{2,1,0:T(8,128)(2,1)S(1)}) custom-call(s32[8]{0:T(128)S(1)} %copy-done.5, bf16[22,96,128]{2,1,0:T(8,128)(2,1)S(1)} %get-tuple-element.51.refs_1_.refs_3_, bf16[4,22,16,128]{3,2,1,0:T(8,128)(2,1)S(1)} %get-tuple-element.60.refs_4_.refs_0_.refs_2_.refs_3_, ...), custom_call_target="tpu_custom_call" | custom-call | flops 1024 | bytes 1024 | tf_op jit(solution)/shard_map/scatter_hop/pallas_call | solution.py:93
  101.2 1.6 %collective-permute-start.23 = (bf16[11,88,128]{2,1,0:T(8,128)(2,1)S(1)}, bf16[11,88,128]{2,1,0:T(8,128)(2,1)S(1)}, u32[]{:S(2)}, u32[]{:S(2)}) collective-permute-start(bf16[11,88,128]{2,1,0:T(8,128)(2,1)S(1)} %get-tuple-element.80), channel_id=1, source_target_pairs={{0,4},{4,8},{8,12},{12,14},{14,10},{10,6},{6,2},{2,0},{1,5},{5,9},... | collective-permute-start | bytes 743432 | tf_op jit(solution)/shard_map/ppermute | solution.py:502
  103.3 1.1 collective-permute-start.27
  104.4 0.9 collective-permute-start.25
  105.3 1.7 %scatter_hop.14 = (f32[11,88,128]{2,1,0:T(8,128)S(1)}, f32[11,88,128]{2,1,0:T(8,128)S(1)}) custom-call(s32[8]{0:T(128)S(1)} %copy-done.5, bf16[22,96,128]{2,1,0:T(8,128)(2,1)S(1)} %get-tuple-element.51.refs_1_.refs_3_, bf16[2,22,16,128]{3,2,1,0:T(8,128)(2,1)S(1)} %get-tuple-element.54.refs_4_.refs_0_.refs_2_.refs_3_, ...), custom_call_target="tpu_custom_call" | custom-call | flops 1024 | bytes 1024 | tf_op jit(solution)/shard_map/scatter_hop/pallas_call | solution.py:93
  106.9 3.2 %collective-permute-done.23.refs_5_ = bf16[11,88,128]{2,1,0:T(8,128)(2,1)S(1)} collective-permute-done((bf16[11,88,128]{2,1,0:T(8,128)(2,1)S(1)}, bf16[11,88,128]{2,1,0:T(8,128)(2,1)S(1)}, u32[]{:S(2)}, u32[]{:S(2)}) %collective-permute-start.23) | collective-permute-done | bytes 247840 | tf_op jit(solution)/shard_map/ppermute | solution.py:502
  110.7 1.5 %scatter_hop.15 = (bf16[11,88,128]{2,1,0:T(8,128)(2,1)S(1)}, bf16[11,88,128]{2,1,0:T(8,128)(2,1)S(1)}) custom-call(s32[8]{0:T(128)S(1)} %copy-done.5, bf16[22,96,128]{2,1,0:T(8,128)(2,1)S(1)} %get-tuple-element.51.refs_1_.refs_3_, bf16[4,22,16,128]{3,2,1,0:T(8,128)(2,1)S(1)} %get-tuple-element.57.refs_4_.refs_0_.refs_2_.refs_3_, ...), custom_call_target="tpu_custom_call" | custom-call | flops 1024 | bytes 1024 | tf_op jit(solution)/shard_map/scatter_hop/pallas_call | solution.py:93
  112.2 3.2 %collective-permute-start.26 = (bf16[11,88,128]{2,1,0:T(8,128)(2,1)S(1)}, bf16[11,88,128]{2,1,0:T(8,128)(2,1)S(1)}, u32[]{:S(2)}, u32[]{:S(2)}) collective-permute-start(bf16[11,88,128]{2,1,0:T(8,128)(2,1)S(1)} %get-tuple-element.87), channel_id=1, source_target_pairs={{0,4},{4,8},{8,12},{12,14},{14,10},{10,6},{6,2},{2,0},{1,5},{5,9},... | collective-permute-start | bytes 743432 | tf_op jit(solution)/shard_map/ppermute | solution.py:502
  115.4 6.8 %output_side.1 = (bf16[22,88,128]{2,1,0:T(8,128)(2,1)}, f32[22,88,128]{2,1,0:T(8,128)S(1)}, f32[128,512]{1,0:T(8,128)S(1)}) custom-call(s32[8]{0:T(128)S(1)} %copy-done.5, bf16[22,88,128]{2,1,0:T(8,128)(2,1)S(1)} %get-tuple-element.50.refs_1_, bf16[22,88,128]{2,1,0:T(8,128)(2,1)S(1)} %copy-done.10, f32[22,88,128]{2,1,0:T(8,128)S(1)} %left_gradient.9.refs_6_.refs_3_, ...), custom_call_target="tpu_custom_call" | custom-call | flops 6600001024 | bytes 1024 | tf_op jit(solution)/shard_map/output_side/pallas_call | solution.py:93
  122.3 2.0 %right_gradient.1 = (bf16[22,88,256]{2,1,0:T(8,128)(2,1)S(1)}, bf16[64,768]{1,0:T(8,128)(2,1)S(1)}, bf16[64,768]{1,0:T(8,128)(2,1)S(1)}) custom-call(s32[8]{0:T(128)S(1)} %copy-done.5, bf16[22,88,128]{2,1,0:T(8,128)(2,1)S(1)} %get-tuple-element.50.refs_1_, bf16[128,640]{1,0:T(8,128)(2,1)S(1)} %copy-done.2, f32[128,512]{1,0:T(8,128)S(1)} %get-tuple-element.84.refs_3_, ...), custom_call_target="tpu_custom_call" | custom-call | flops 1024 | bytes 1024 | tf_op jit(solution)/shard_map/right_gradient/pallas_call | solution.py:93
  124.4 1.3 collective-permute-done.28
  125.7 0.6 collective-permute-start.29
  126.4 4.3 %collective-permute-done.29 = bf16[64,768]{1,0:T(8,128)(2,1)S(1)} collective-permute-done((bf16[64,768]{1,0:T(8,128)(2,1)S(1)}, bf16[64,768]{1,0:T(8,128)(2,1)S(1)}, u32[]{:S(2)}, u32[]{:S(2)}) %collective-permute-start.29) | collective-permute-done | bytes 98336 | tf_op jit(solution)/shard_map/ppermute | solution.py:650
  130.7 2.1 %collective-permute-start.30 = (bf16[64,768]{1,0:T(8,128)(2,1)S(1)}, bf16[64,768]{1,0:T(8,128)(2,1)S(1)}, u32[]{:S(2)}, u32[]{:S(2)}) collective-permute-start(bf16[64,768]{1,0:T(8,128)(2,1)S(1)} %add_convert_fusion.2), channel_id=1, source_target_pairs={{0,4},{2,6},{4,0},{6,2},{8,12},{10,14},{12,8},{14,10},{1,5},{3,7},... | collective-permute-start | bytes 294920 | tf_op jit(solution)/shard_map/ppermute | solution.py:650
  132.8 2.6 %collective-permute-done.30 = bf16[64,768]{1,0:T(8,128)(2,1)S(1)} collective-permute-done((bf16[64,768]{1,0:T(8,128)(2,1)S(1)}, bf16[64,768]{1,0:T(8,128)(2,1)S(1)}, u32[]{:S(2)}, u32[]{:S(2)}) %collective-permute-start.30) | collective-permute-done | bytes 98336 | tf_op jit(solution)/shard_map/ppermute | solution.py:650
  135.4 2.7 %collective-permute-start.31 = (bf16[64,768]{1,0:T(8,128)(2,1)S(1)}, bf16[64,768]{1,0:T(8,128)(2,1)S(1)}, u32[]{:S(2)}, u32[]{:S(2)}) collective-permute-start(bf16[64,768]{1,0:T(8,128)(2,1)S(1)} %add_convert_fusion.1), channel_id=1, source_target_pairs={{0,8},{2,10},{4,12},{6,14},{8,0},{10,2},{12,4},{14,6},{1,9},{3,11}... | collective-permute-start | bytes 294920 | tf_op jit(solution)/shard_map/ppermute | solution.py:650
  138.2 4.1 %pair_gradient.1 = bf16[22,88,128]{2,1,0:T(8,128)(2,1)} custom-call(bf16[22,88,128]{2,1,0:T(8,128)(2,1)S(1)} %copy-done.4, bf16[22,88,256]{2,1,0:T(8,128)(2,1)S(1)} %get-tuple-element.90.refs_1_, f32[1,128]{1,0:T(1,128)S(1)} %bitcast.16, bf16[128,640]{1,0:T(8,128)(2,1)S(1)} %copy-done.2, f32[22,88,128]{2,1,0:T(8,128)S(1)} %get-tuple-element.91.refs_4_), custom_call_target="tpu_custom_call" | custom-call | flops 3300001024 | bytes 1024 | tf_op jit(solution)/shard_map/pair_gradient/pallas_call | solution.py:93
  142.3 1.3 collective-permute-done.32.refs_1_
  143.6 0.8 weight_gradients.1
  (59 shorter events, 7.2 us)
Async XLA Ops:
  0.6 0.7 copy-start.5
  0.6 0.7 copy-start.8
  0.7 0.7 copy-start.9
  1.3 0.9 copy-start.1
  2.2 1.0 copy-start.3
  3.3 1.5 %copy-start.2 = (bf16[128,640]{1,0:T(8,128)(2,1)S(1)}, bf16[128,640]{1,0:T(8,128)(2,1)}, u32[]{:S(2)}) copy-start(bf16[128,640]{1,0:T(8,128)(2,1)} %refs_3_.3) | copy-start | bytes 491524
  3.3 1.5 %copy-start.10 = (bf16[22,88,128]{2,1,0:T(8,128)(2,1)S(1)}, bf16[22,88,128]{2,1,0:T(8,128)(2,1)}, u32[]{:S(2)}) copy-start(bf16[22,88,128]{2,1,0:T(8,128)(2,1)} %refs_2_.4) | copy-start | bytes 1486852
  6.2 10.1 %collective-permute-start.3 = (bf16[8,22,16,128]{3,2,1,0:T(8,128)(2,1)S(1)}, bf16[8,22,16,128]{3,2,1,0:T(8,128)(2,1)S(1)}, u32[]{:S(2)}, u32[]{:S(2)}) collective-permute-start(bf16[8,22,16,128]{3,2,1,0:T(8,128)(2,1)S(1)} %get-tuple-element.53.refs_2_.refs_6_), channel_id=1, source_target_pairs={{0,1},{1,0},{2,3},{3,2},{4,5},{5,4},{6,7},{7,6},{8,9},{9,8},{10,11... | collective-permute-start | bytes 2162696 | tf_op jit(solution)/shard_map/ppermute | solution.py:77
  6.7 14.6 %collective-permute-start.1 = (bf16[22,88,128]{2,1,0:T(8,128)(2,1)S(1)}, bf16[22,88,128]{2,1,0:T(8,128)(2,1)S(1)}, u32[]{:S(2)}, u32[]{:S(2)}) collective-permute-start(bf16[22,88,128]{2,1,0:T(8,128)(2,1)S(1)} %get-tuple-element.52.refs_2_.refs_1_), channel_id=1, source_target_pairs={{0,2},{4,0},{8,4},{12,8},{14,12},{10,14},{6,10},{2,6},{1,3},{5,1},... | collective-permute-start | bytes 1486856 | tf_op jit(solution)/shard_map/ppermute | solution.py:505
  9.3 13.4 %collective-permute-start = (bf16[22,88,128]{2,1,0:T(8,128)(2,1)S(1)}, bf16[22,88,128]{2,1,0:T(8,128)(2,1)S(1)}, u32[]{:S(2)}, u32[]{:S(2)}) collective-permute-start(bf16[22,88,128]{2,1,0:T(8,128)(2,1)S(1)} %get-tuple-element.52.refs_2_.refs_1_), channel_id=1, source_target_pairs={{0,4},{4,8},{8,12},{12,14},{14,10},{10,6},{6,2},{2,0},{1,5},{5,9},... | collective-permute-start | bytes 1486856 | tf_op jit(solution)/shard_map/ppermute | solution.py:502
  9.4 6.9 %copy-start = (bf16[128,128]{1,0:T(8,128)(2,1)S(1)}, bf16[128,128]{1,0:T(8,128)(2,1)}, u32[]{:S(2)}) copy-start(bf16[128,128]{1,0:T(8,128)(2,1)} %refs_5_.1) | copy-start | bytes 98308
  14.8 1.5 %collective-permute-start.2 = (bf16[2,22,16,128]{3,2,1,0:T(8,128)(2,1)S(1)}, bf16[2,22,16,128]{3,2,1,0:T(8,128)(2,1)S(1)}, u32[]{:S(2)}, u32[]{:S(2)}) collective-permute-start(bf16[2,22,16,128]{3,2,1,0:T(8,128)(2,1)S(1)} %triangle.5.refs_0_.refs_7_), channel_id=1, source_target_pairs={{0,1},{1,0},{2,3},{3,2},{4,5},{5,4},{6,7},{7,6},{8,9},{9,8},{10,11... | collective-permute-start | bytes 540680 | tf_op jit(solution)/shard_map/ppermute | solution.py:77
  16.3 0.7 copy-start.6
  16.3 0.7 copy-start.7
  22.6 12.6 %collective-permute-start.4 = (bf16[22,88,128]{2,1,0:T(8,128)(2,1)S(1)}, bf16[22,88,128]{2,1,0:T(8,128)(2,1)S(1)}, u32[]{:S(2)}, u32[]{:S(2)}) collective-permute-start(bf16[22,88,128]{2,1,0:T(8,128)(2,1)S(1)} %collective-permute-done.refs_2_.refs_1_), channel_id=1, source_target_pairs={{0,4},{4,8},{8,12},{12,14},{14,10},{10,6},{6,2},{2,0},{1,5},{5,9},... | collective-permute-start | bytes 1486856 | tf_op jit(solution)/shard_map/ppermute | solution.py:502
  23.0 12.6 %collective-permute-start.5 = (bf16[22,88,128]{2,1,0:T(8,128)(2,1)S(1)}, bf16[22,88,128]{2,1,0:T(8,128)(2,1)S(1)}, u32[]{:S(2)}, u32[]{:S(2)}) collective-permute-start(bf16[22,88,128]{2,1,0:T(8,128)(2,1)S(1)} %collective-permute-done.1.refs_3_.refs_2_), channel_id=1, source_target_pairs={{0,2},{4,0},{8,4},{12,8},{14,12},{10,14},{6,10},{2,6},{1,3},{5,1},... | collective-permute-start | bytes 1486856 | tf_op jit(solution)/shard_map/ppermute | solution.py:505
  32.3 1.7 %collective-permute-start.6 = (bf16[4,22,16,128]{3,2,1,0:T(8,128)(2,1)S(1)}, bf16[4,22,16,128]{3,2,1,0:T(8,128)(2,1)S(1)}, u32[]{:S(2)}, u32[]{:S(2)}) collective-permute-start(bf16[4,22,16,128]{3,2,1,0:T(8,128)(2,1)S(1)} %triangle.6.refs_2_.refs_0_), channel_id=1, source_target_pairs={{0,1},{1,0},{2,3},{3,2},{4,5},{5,4},{6,7},{7,6},{8,9},{9,8},{10,11... | collective-permute-start | bytes 1081352 | tf_op jit(solution)/shard_map/ppermute | solution.py:77
  35.6 16.1 %collective-permute-start.7 = (bf16[22,88,128]{2,1,0:T(8,128)(2,1)S(1)}, bf16[22,88,128]{2,1,0:T(8,128)(2,1)S(1)}, u32[]{:S(2)}, u32[]{:S(2)}) collective-permute-start(bf16[22,88,128]{2,1,0:T(8,128)(2,1)S(1)} %collective-permute-done.4.refs_2_.refs_1_), channel_id=1, source_target_pairs={{0,4},{4,8},{8,12},{12,14},{14,10},{10,6},{6,2},{2,0},{1,5},{5,9},... | collective-permute-start | bytes 1486856 | tf_op jit(solution)/shard_map/ppermute | solution.py:502
  37.2 14.5 %collective-permute-start.8 = (bf16[22,88,128]{2,1,0:T(8,128)(2,1)S(1)}, bf16[22,88,128]{2,1,0:T(8,128)(2,1)S(1)}, u32[]{:S(2)}, u32[]{:S(2)}) collective-permute-start(bf16[22,88,128]{2,1,0:T(8,128)(2,1)S(1)} %collective-permute-done.5.refs_3_.refs_2_), channel_id=1, source_target_pairs={{0,2},{4,0},{8,4},{12,8},{14,12},{10,14},{6,10},{2,6},{1,3},{5,1},... | collective-permute-start | bytes 1486856 | tf_op jit(solution)/shard_map/ppermute | solution.py:505
  48.3 2.4 %collective-permute-start.9 = (bf16[4,22,16,128]{3,2,1,0:T(8,128)(2,1)S(1)}, bf16[4,22,16,128]{3,2,1,0:T(8,128)(2,1)S(1)}, u32[]{:S(2)}, u32[]{:S(2)}) collective-permute-start(bf16[4,22,16,128]{3,2,1,0:T(8,128)(2,1)S(1)} %triangle.7.refs_4_.refs_0_), channel_id=1, source_target_pairs={{0,1},{1,0},{2,3},{3,2},{4,5},{5,4},{6,7},{7,6},{8,9},{9,8},{10,11... | collective-permute-start | bytes 1081352 | tf_op jit(solution)/shard_map/ppermute | solution.py:77
  57.6 5.2 %collective-permute-start.12 = (bf16[4,22,16,128]{3,2,1,0:T(8,128)(2,1)S(1)}, bf16[4,22,16,128]{3,2,1,0:T(8,128)(2,1)S(1)}, u32[]{:S(2)}, u32[]{:S(2)}) collective-permute-start(bf16[4,22,16,128]{3,2,1,0:T(8,128)(2,1)S(1)} %triangle.8.refs_4_.refs_0_), channel_id=1, source_target_pairs={{0,1},{1,0},{2,3},{3,2},{4,5},{5,4},{6,7},{7,6},{8,9},{9,8},{10,11... | collective-permute-start | bytes 1081352 | tf_op jit(solution)/shard_map/ppermute | solution.py:77
  58.2 8.2 %collective-permute-start.11 = (bf16[11,88,128]{2,1,0:T(8,128)(2,1)S(1)}, bf16[11,88,128]{2,1,0:T(8,128)(2,1)S(1)}, u32[]{:S(2)}, u32[]{:S(2)}) collective-permute-start(bf16[11,88,128]{2,1,0:T(8,128)(2,1)S(1)} %slice.7), channel_id=1, source_target_pairs={{0,2},{4,0},{8,4},{12,8},{14,12},{10,14},{6,10},{2,6},{1,3},{5,1},... | collective-permute-start | bytes 743432 | tf_op jit(solution)/shard_map/ppermute | solution.py:505
  60.5 8.1 %collective-permute-start.10 = (bf16[11,88,128]{2,1,0:T(8,128)(2,1)S(1)}, bf16[11,88,128]{2,1,0:T(8,128)(2,1)S(1)}, u32[]{:S(2)}, u32[]{:S(2)}) collective-permute-start(bf16[11,88,128]{2,1,0:T(8,128)(2,1)S(1)} %slice.6), channel_id=1, source_target_pairs={{0,4},{4,8},{8,12},{12,14},{14,10},{10,6},{6,2},{2,0},{1,5},{5,9},... | collective-permute-start | bytes 743432 | tf_op jit(solution)/shard_map/ppermute | solution.py:502
  72.5 4.4 %collective-permute-start.13 = (bf16[2,22,16,128]{3,2,1,0:T(8,128)(2,1)S(1)}, bf16[2,22,16,128]{3,2,1,0:T(8,128)(2,1)S(1)}, u32[]{:S(2)}, u32[]{:S(2)}) collective-permute-start(bf16[2,22,16,128]{3,2,1,0:T(8,128)(2,1)S(1)} %triangle.9.refs_4_.refs_0_), channel_id=1, source_target_pairs={{0,1},{1,0},{2,3},{3,2},{4,5},{5,4},{6,7},{7,6},{8,9},{9,8},{10,11... | collective-permute-start | bytes 540680 | tf_op jit(solution)/shard_map/ppermute | solution.py:77
  72.6 11.0 %collective-permute-start.16 = (bf16[11,88,128]{2,1,0:T(8,128)(2,1)S(1)}, bf16[11,88,128]{2,1,0:T(8,128)(2,1)S(1)}, u32[]{:S(2)}, u32[]{:S(2)}) collective-permute-start(bf16[11,88,128]{2,1,0:T(8,128)(2,1)S(1)} %get-tuple-element.64.refs_4_), channel_id=1, source_target_pairs={{0,2},{4,0},{8,4},{12,8},{14,12},{10,14},{6,10},{2,6},{1,3},{5,1},... | collective-permute-start | bytes 743432 | tf_op jit(solution)/shard_map/ppermute | solution.py:505
  74.0 9.6 %collective-permute-start.17 = (bf16[11,88,128]{2,1,0:T(8,128)(2,1)S(1)}, bf16[11,88,128]{2,1,0:T(8,128)(2,1)S(1)}, u32[]{:S(2)}, u32[]{:S(2)}) collective-permute-start(bf16[11,88,128]{2,1,0:T(8,128)(2,1)S(1)} %get-tuple-element.73), channel_id=1, source_target_pairs={{0,4},{4,8},{8,12},{12,14},{14,10},{10,6},{6,2},{2,0},{1,5},{5,9},... | collective-permute-start | bytes 743432 | tf_op jit(solution)/shard_map/ppermute | solution.py:502
  79.2 9.7 %collective-permute-start.15 = (bf16[11,88,128]{2,1,0:T(8,128)(2,1)S(1)}, bf16[11,88,128]{2,1,0:T(8,128)(2,1)S(1)}, u32[]{:S(2)}, u32[]{:S(2)}) collective-permute-start(bf16[11,88,128]{2,1,0:T(8,128)(2,1)S(1)} %get-tuple-element.72), channel_id=1, source_target_pairs={{0,4},{4,8},{8,12},{12,14},{14,10},{10,6},{6,2},{2,0},{1,5},{5,9},... | collective-permute-start | bytes 743432 | tf_op jit(solution)/shard_map/ppermute | solution.py:502
  80.6 9.0 %collective-permute-start.14 = (bf16[11,88,128]{2,1,0:T(8,128)(2,1)S(1)}, bf16[11,88,128]{2,1,0:T(8,128)(2,1)S(1)}, u32[]{:S(2)}, u32[]{:S(2)}) collective-permute-start(bf16[11,88,128]{2,1,0:T(8,128)(2,1)S(1)} %get-tuple-element.66.refs_4_), channel_id=1, source_target_pairs={{0,2},{4,0},{8,4},{12,8},{14,12},{10,14},{6,10},{2,6},{1,3},{5,1},... | collective-permute-start | bytes 743432 | tf_op jit(solution)/shard_map/ppermute | solution.py:505
  85.3 9.0 %collective-permute-start.21 = (bf16[11,88,128]{2,1,0:T(8,128)(2,1)S(1)}, bf16[11,88,128]{2,1,0:T(8,128)(2,1)S(1)}, u32[]{:S(2)}, u32[]{:S(2)}) collective-permute-start(bf16[11,88,128]{2,1,0:T(8,128)(2,1)S(1)} %get-tuple-element.77), channel_id=1, source_target_pairs={{0,4},{4,8},{8,12},{12,14},{14,10},{10,6},{6,2},{2,0},{1,5},{5,9},... | collective-permute-start | bytes 743432 | tf_op jit(solution)/shard_map/ppermute | solution.py:502
  85.8 9.0 %collective-permute-start.20 = (bf16[11,88,128]{2,1,0:T(8,128)(2,1)S(1)}, bf16[11,88,128]{2,1,0:T(8,128)(2,1)S(1)}, u32[]{:S(2)}, u32[]{:S(2)}) collective-permute-start(bf16[11,88,128]{2,1,0:T(8,128)(2,1)S(1)} %get-tuple-element.74.refs_6_), channel_id=1, source_target_pairs={{0,2},{4,0},{8,4},{12,8},{14,12},{10,14},{6,10},{2,6},{1,3},{5,1},... | collective-permute-start | bytes 743432 | tf_op jit(solution)/shard_map/ppermute | solution.py:505
  91.1 8.0 %collective-permute-start.19 = (bf16[11,88,128]{2,1,0:T(8,128)(2,1)S(1)}, bf16[11,88,128]{2,1,0:T(8,128)(2,1)S(1)}, u32[]{:S(2)}, u32[]{:S(2)}) collective-permute-start(bf16[11,88,128]{2,1,0:T(8,128)(2,1)S(1)} %get-tuple-element.76), channel_id=1, source_target_pairs={{0,4},{4,8},{8,12},{12,14},{14,10},{10,6},{6,2},{2,0},{1,5},{5,9},... | collective-permute-start | bytes 743432 | tf_op jit(solution)/shard_map/ppermute | solution.py:502
  92.9 6.6 %collective-permute-start.18 = (bf16[11,88,128]{2,1,0:T(8,128)(2,1)S(1)}, bf16[11,88,128]{2,1,0:T(8,128)(2,1)S(1)}, u32[]{:S(2)}, u32[]{:S(2)}) collective-permute-start(bf16[11,88,128]{2,1,0:T(8,128)(2,1)S(1)} %get-tuple-element.75.refs_6_), channel_id=1, source_target_pairs={{0,2},{4,0},{8,4},{12,8},{14,12},{10,14},{6,10},{2,6},{1,3},{5,1},... | collective-permute-start | bytes 743432 | tf_op jit(solution)/shard_map/ppermute | solution.py:505
  101.2 9.0 %collective-permute-start.23 = (bf16[11,88,128]{2,1,0:T(8,128)(2,1)S(1)}, bf16[11,88,128]{2,1,0:T(8,128)(2,1)S(1)}, u32[]{:S(2)}, u32[]{:S(2)}) collective-permute-start(bf16[11,88,128]{2,1,0:T(8,128)(2,1)S(1)} %get-tuple-element.80), channel_id=1, source_target_pairs={{0,4},{4,8},{8,12},{12,14},{14,10},{10,6},{6,2},{2,0},{1,5},{5,9},... | collective-permute-start | bytes 743432 | tf_op jit(solution)/shard_map/ppermute | solution.py:502
  102.7 8.0 %collective-permute-start.22 = (bf16[11,88,128]{2,1,0:T(8,128)(2,1)S(1)}, bf16[11,88,128]{2,1,0:T(8,128)(2,1)S(1)}, u32[]{:S(2)}, u32[]{:S(2)}) collective-permute-start(bf16[11,88,128]{2,1,0:T(8,128)(2,1)S(1)} %get-tuple-element.79.refs_4_), channel_id=1, source_target_pairs={{0,2},{4,0},{8,4},{12,8},{14,12},{10,14},{6,10},{2,6},{1,3},{5,1},... | collective-permute-start | bytes 743432 | tf_op jit(solution)/shard_map/ppermute | solution.py:505
  103.3 19.0 %collective-permute-start.27 = (bf16[11,88,128]{2,1,0:T(8,128)(2,1)S(1)}, bf16[11,88,128]{2,1,0:T(8,128)(2,1)S(1)}, u32[]{:S(2)}, u32[]{:S(2)}) collective-permute-start(bf16[11,88,128]{2,1,0:T(8,128)(2,1)S(1)} %get-tuple-element.78.refs_6_), channel_id=1, source_target_pairs={{0,2},{4,0},{8,4},{12,8},{14,12},{10,14},{6,10},{2,6},{1,3},{5,1},... | collective-permute-start | bytes 743432 | tf_op jit(solution)/shard_map/ppermute | solution.py:505
  104.4 17.9 %collective-permute-start.25 = (bf16[11,88,128]{2,1,0:T(8,128)(2,1)S(1)}, bf16[11,88,128]{2,1,0:T(8,128)(2,1)S(1)}, u32[]{:S(2)}, u32[]{:S(2)}) collective-permute-start(bf16[11,88,128]{2,1,0:T(8,128)(2,1)S(1)} %get-tuple-element.86), channel_id=1, source_target_pairs={{0,4},{4,8},{8,12},{12,14},{14,10},{10,6},{6,2},{2,0},{1,5},{5,9},... | collective-permute-start | bytes 743432 | tf_op jit(solution)/shard_map/ppermute | solution.py:502
  112.2 10.0 %collective-permute-start.26 = (bf16[11,88,128]{2,1,0:T(8,128)(2,1)S(1)}, bf16[11,88,128]{2,1,0:T(8,128)(2,1)S(1)}, u32[]{:S(2)}, u32[]{:S(2)}) collective-permute-start(bf16[11,88,128]{2,1,0:T(8,128)(2,1)S(1)} %get-tuple-element.87), channel_id=1, source_target_pairs={{0,4},{4,8},{8,12},{12,14},{14,10},{10,6},{6,2},{2,0},{1,5},{5,9},... | collective-permute-start | bytes 743432 | tf_op jit(solution)/shard_map/ppermute | solution.py:502
  115.4 6.8 %collective-permute-start.24 = (bf16[11,88,128]{2,1,0:T(8,128)(2,1)S(1)}, bf16[11,88,128]{2,1,0:T(8,128)(2,1)S(1)}, u32[]{:S(2)}, u32[]{:S(2)}) collective-permute-start(bf16[11,88,128]{2,1,0:T(8,128)(2,1)S(1)} %get-tuple-element.82.refs_12_), channel_id=1, source_target_pairs={{0,2},{4,0},{8,4},{12,8},{14,12},{10,14},{6,10},{2,6},{1,3},{5,1},... | collective-permute-start | bytes 743432 | tf_op jit(solution)/shard_map/ppermute | solution.py:505
  124.3 13.8 %copy-start.4 = (bf16[22,88,128]{2,1,0:T(8,128)(2,1)S(1)}, bf16[22,88,128]{2,1,0:T(8,128)(2,1)}, u32[]{:S(2)}) copy-start(bf16[22,88,128]{2,1,0:T(8,128)(2,1)} %refs_0_.35) | copy-start | bytes 1486852
  124.3 1.4 collective-permute-start.28
  125.7 4.9 %collective-permute-start.29 = (bf16[64,768]{1,0:T(8,128)(2,1)S(1)}, bf16[64,768]{1,0:T(8,128)(2,1)S(1)}, u32[]{:S(2)}, u32[]{:S(2)}) collective-permute-start(bf16[64,768]{1,0:T(8,128)(2,1)S(1)} %add_convert_fusion.3), channel_id=1, source_target_pairs={{0,2},{2,0},{4,6},{6,4},{8,10},{10,8},{12,14},{14,12},{1,3},{3,1},... | collective-permute-start | bytes 294920 | tf_op jit(solution)/shard_map/ppermute | solution.py:650
  130.7 4.7 %collective-permute-start.30 = (bf16[64,768]{1,0:T(8,128)(2,1)S(1)}, bf16[64,768]{1,0:T(8,128)(2,1)S(1)}, u32[]{:S(2)}, u32[]{:S(2)}) collective-permute-start(bf16[64,768]{1,0:T(8,128)(2,1)S(1)} %add_convert_fusion.2), channel_id=1, source_target_pairs={{0,4},{2,6},{4,0},{6,2},{8,12},{10,14},{12,8},{14,10},{1,5},{3,7},... | collective-permute-start | bytes 294920 | tf_op jit(solution)/shard_map/ppermute | solution.py:650
  135.4 6.8 %collective-permute-start.31 = (bf16[64,768]{1,0:T(8,128)(2,1)S(1)}, bf16[64,768]{1,0:T(8,128)(2,1)S(1)}, u32[]{:S(2)}, u32[]{:S(2)}) collective-permute-start(bf16[64,768]{1,0:T(8,128)(2,1)S(1)} %add_convert_fusion.1), channel_id=1, source_target_pairs={{0,8},{2,10},{4,12},{6,14},{8,0},{10,2},{12,4},{14,6},{1,9},{3,11}... | collective-permute-start | bytes 294920 | tf_op jit(solution)/shard_map/ppermute | solution.py:650
  142.2 1.4 collective-permute-start.32
where the time goes:
time: 144 us
  Pallas kernels  74.2 us (52%)
  starting transfers between devices  33.5 us (23%)
  waiting for transfers between devices  32.3 us (22%)
  local copies, waits for them, and re-layouts  3.33 us (2%)
    pallas_call x29, Pallas kernels, call(): pl.pallas_call(body, out_shape=list(outs), in_specs=list(specs) + [ANY] *...  74.2 us
    ppermute x11, starting transfers between devices, behind(): return lax.ppermute(x, 'row', backward)  14.2 us
    ppermute x11, waiting for transfers between devices, ahead(): return lax.ppermute(x, 'row', forward)  13.3 us
    ppermute x11, starting transfers between devices, ahead(): return lax.ppermute(x, 'row', forward)  12.2 us
    ppermute x11, waiting for transfers between devices, behind(): return lax.ppermute(x, 'row', backward)  7.62 us
    ppermute x3, waiting for transfers between devices, shards(): lax.ppermute(mine, 'row', [(r, r ^ step) for r in range(row_count)])  6.87 us
    ppermute x3, starting transfers between devices, shards(): lax.ppermute(mine, 'row', [(r, r ^ step) for r in range(row_count)])  5.48 us
    ppermute x8, waiting for transfers between devices, swap_col(): return lax.ppermute(x, 'col', [(0, 1), (1, 0)])  4.45 us
  transfers between devices with their start and end apart: 33, of which 21 were waited for; matrix products, arithmetic and copies ran while one was open for 0% of the time, Pallas kernels for 39%

commit v1 on v0

--- a/solution.py
+++ b/solution.py
@@ -181,11 +181,7 @@
         proj = dot(normed[i], w[:, : 2 * hidden], 1, 0)
         shown = mask[...] * present_row(lengths, slot, first_row(here) + i)
         gated = shown * jax.nn.sigmoid(proj[:, :hidden]) * proj[:, hidden:]
-        left[i, pl.ds(0, half), :] = gated.astype(bf16)
-        if left.shape[1] > half:
-            left[i, pl.ds(half, left.shape[1] - half), :] = jnp.zeros(
-                (left.shape[1] - half, hidden), bf16
-            )
+        left[i] = gated.astype(bf16)
         gate = jax.nn.sigmoid(dot(normed[i], w[:, 4 * hidden :], 1, 0))
         grads = cotangent[i].astype(f32) * gate
         empty = jnp.zeros((padded - short, hidden), f32)
@@ -197,33 +193,44 @@
 
 
 def triangle_kernel(row_count, slot, halves, arrays, lengths, left, *refs):
-    rights, (out, rows, which) = refs[:arrays], refs[arrays:]
-    here, deep, hidden = left.shape
-    half = rights[0].shape[1]
+    rights, (out, partial, rows) = refs[:arrays], refs[arrays:]
+    here, half, hidden = left.shape
     padded = out.shape[2]
     short = here // 2
-    row = lax.broadcasted_iota(jnp.int32, which.shape, 0)
-    lane = lax.broadcasted_iota(jnp.int32, which.shape, 1)
-    which[...] = ((lane >= row * deep) & (lane < (row + 1) * deep)).astype(f32).astype(bf16)
+    cuts = tiles(half)
     for s, (array, first, place) in enumerate(halves):
         rows[...] = jnp.zeros_like(rows)
 
-        def column(j, carry, right=rights[array], first=first):
-            held = right[first + j]
-            if deep > half:
-                held = jnp.concatenate([held, jnp.zeros((deep - half, hidden), bf16)], axis=0)
-            products = jnp.concatenate([left[i] * held for i in range(here)], axis=0)
-            total = dot(which[...], products, 1, 0)
-            rows[pl.ds(j, here, stride=padded), :] = total[:here]
+        def columns(pair, carry, right=rights[array], first=first):
+            at = [jnp.minimum(2 * pair + x, short - 1) for x in range(2)]
+            held = [[right[first + j, pl.ds(k, size), :] for k, size in cuts] for j in at]
+            for i in range(here):
+                given = [left[i, pl.ds(k, size), :] for k, size in cuts]
+                for x in range(2):
+                    products = [a * b for a, b in zip(given, held[x])]
+                    rest = products.pop() if half % 16 else None
+                    total = products[0]
+                    for product in products[1:]:
+                        total = total + product
+                    total = total.astype(f32)
+                    total = total[:8] + total[8:]
+                    if rest is not None:
+                        total += rest.astype(f32)
+                    partial[x, pl.ds(8 * i, 8), :] = total
+            for x in range(2):
+                total = partial[x, pl.ds(0, here, stride=8), :]
+                for sub in range(1, 8):
+                    total += partial[x, pl.ds(sub, here, stride=8), :]
+                rows[pl.ds(at[x], here, stride=padded), :] = total
             return carry
 
         present = present_count(row_count, lengths, slot, short, place)
-        lax.fori_loop(0, present, column, 0)
+        lax.fori_loop(0, (present + 1) // 2, columns, 0)
         out[s] = rows[...].astype(bf16).reshape(here, padded, hidden)
 
 
 def triangle(row_count, slot, halves, lengths, left, rights, padded, after):
-    count, (here, deep, hidden) = len(halves), left.shape
+    count, (here, half, hidden) = len(halves), left.shape
     return call(
         functools.partial(triangle_kernel, row_count, slot, halves, len(rights)),
         "triangle",
@@ -231,8 +238,8 @@
         [SMEM] + [VMEM] * (len(rights) + 1),
         [shape_of((count, here, padded, hidden), bf16)],
         [
+            pltpu.VMEM((2, here * 8, hidden), f32),
             pltpu.VMEM((here * padded, hidden), f32),
-            pltpu.VMEM(((here + 15) // 16 * 16, here * deep), bf16),
         ],
         after,
     )[0]
@@ -328,6 +335,11 @@
         [pltpu.VMEM(grads[0].shape[1:], f32)],
         after,
     )
+
+
+def add_kernel(one, two, first, second, out_one, out_two):
+    out_one[...] = (one[...] + first[...].astype(f32)).astype(bf16)
+    out_two[...] = (two[...] + second[...].astype(f32)).astype(bf16)
 
 
 def left_gradient_kernel(halves, picks, arrays, carried, grads, *refs):
@@ -533,10 +545,7 @@
         "left_side",
         [chain_lengths, normed, cotangent, w_in],
         [SMEM] + [VMEM] * 3,
-        [
-            shape_of((here, (half + 15) // 16 * 16, hidden), bf16),
-            shape_of((row_count, here, padded, hidden), bf16),
-        ],
+        [shape_of(block, bf16), shape_of((row_count, here, padded, hidden), bf16)],
         [mask],
         microseconds=4,
     )
@@ -588,8 +597,22 @@
 
     arrived = {0: [], 1: []}
 
-    def send(s, chain):
-        x, y = scatter(s, [2 * chain, 2 * chain + 1], arrived[chain])
+    def send(s, chain, after=()):
+        picks = [2 * chain, 2 * chain + 1]
+        if arrived[chain]:
+            terms = scatter(s, picks, [], f32)
+            x, y = call(
+                add_kernel,
+                "scatter_add",
+                [*terms, *arrived[chain]],
+                [VMEM] * 4,
+                [shape_of((short, half, hidden), bf16)] * 2,
+                (),
+                [*last, *after],
+            )
+            last[:] = [x]
+        else:
+            x, y = scatter(s, picks, [])
         arrived[chain] = [behind(x), ahead(y)]
 
     def output_side():
@@ -627,7 +650,7 @@
     for s in range(hops - 1, 0, -1):
         if s == 1:
             own_a, own_b = scatter(0, [0, 1], [], f32)
-        send(s, 0)
+        send(s, 0, arrived[1] if s == 1 else ())
         if s > 2:
             send(s - 2, 1)
     update, gradient, early = output_side()

time: 144 us -> 132 us (0.917)
  Pallas kernels: 74.2 us -> 58 us
  waiting for transfers between devices: 32.3 us -> 38.8 us
  starting transfers between devices: 33.5 us -> 30.3 us
    pallas_call x29 -> x34, Pallas kernels: 74.2 us -> 58 us  [call(): pl.pallas_call(body, out_shape=list(outs), in_specs=list(specs) + [ANY] *...]
    ppermute x11, waiting for transfers between devices: 7.62 us -> 16.7 us  [behind(): return lax.ppermute(x, 'row', backward)]
    ppermute x11, waiting for transfers between devices: 13.3 us -> 10.6 us  [ahead(): return lax.ppermute(x, 'row', forward)]
  transfers between devices with their start and end apart: 33 -> 33, of which waited for: 21 -> 21; matrix products, arithmetic and copies ran while one was open for 0% -> 0% of each run, Pallas kernels for 39% -> 36%
where the time goes in v1:
time: 132 us
  Pallas kernels  58 us (44%)
  waiting for transfers between devices  38.8 us (29%)
  starting transfers between devices  30.3 us (23%)
  local copies, waits for them, and re-layouts  3.33 us (3%)
    pallas_call x34, Pallas kernels, call(): pl.pallas_call(body, out_shape=list(outs), in_specs=list(specs) + [ANY] *...  58 us
    ppermute x11, waiting for transfers between devices, behind(): return lax.ppermute(x, 'row', backward)  16.7 us
    ppermute x11, starting transfers between devices, behind(): return lax.ppermute(x, 'row', backward)  13 us
    ppermute x11, starting transfers between devices, ahead(): return lax.ppermute(x, 'row', forward)  12.1 us
    ppermute x11, waiting for transfers between devices, ahead(): return lax.ppermute(x, 'row', forward)  10.6 us
    ppermute x3, waiting for transfers between devices, shards(): lax.ppermute(mine, 'row', [(r, r ^ step) for r in range(row_count)])  7.11 us
    ppermute x8, waiting for transfers between devices, swap_col(): return lax.ppermute(x, 'col', [(0, 1), (1, 0)])  4.44 us
    ppermute x3, starting transfers between devices, shards(): lax.ppermute(mine, 'row', [(r, r ^ step) for r in range(row_count)])  4.09 us
  transfers between devices with their start and end apart: 33, of which 21 were waited for; matrix products, arithmetic and copies ran while one was open for 0% of the time, Pallas kernels for 36%

profile of v1, /device:TPU:0, one launch (start us, length us, event | category | flops | bytes accessed | tf_op | source)
XLA Modules:
  0.0 131.5 jit_solution(1154531867978881230)
XLA Ops:
  1.3 0.9 copy-done.1
  2.2 1.0 copy-done.3
  3.3 1.5 %input_side.1 = (bf16[22,88,128]{2,1,0:T(8,128)(2,1)S(1)}, bf16[22,88,128]{2,1,0:T(8,128)(2,1)S(1)}) custom-call(s32[8]{0:T(128)S(1)} %copy-done.5, bf16[22,88,128]{2,1,0:T(8,128)(2,1)S(1)} %copy-done.3, f32[1,128]{1,0:T(1,128)S(1)} %bitcast.15, f32[1,128]{1,0:T(1,128)S(1)} %bitcast.14, bf16[128,640]{1,0:T(8,128)(2,1)S(1)} %copy-done.1), custom_call_target="tpu_custom_call" | custom-call | flops 1024 | bytes 1024 | tf_op jit(solution)/shard_map/input_side/pallas_call | solution.py:93
  4.8 1.4 %left_side.1 = (bf16[22,88,128]{2,1,0:T(8,128)(2,1)S(1)}, bf16[8,22,16,128]{3,2,1,0:T(8,128)(2,1)S(1)}) custom-call(s32[8]{0:T(128)S(1)} %copy-done.5, bf16[22,88,128]{2,1,0:T(8,128)(2,1)S(1)} %get-tuple-element.60.refs_1_, bf16[22,88,128]{2,1,0:T(8,128)(2,1)S(1)} %copy-done.10, bf16[128,640]{1,0:T(8,128)(2,1)S(1)} %copy-done.2), custom_call_target="tpu_custom_call" | custom-call | flops 4400001024 | bytes 1024 | tf_op jit(solution)/shard_map/left_side/pallas_call | solution.py:93
  6.7 2.6 %collective-permute-start.1 = (bf16[22,88,128]{2,1,0:T(8,128)(2,1)S(1)}, bf16[22,88,128]{2,1,0:T(8,128)(2,1)S(1)}, u32[]{:S(2)}, u32[]{:S(2)}) collective-permute-start(bf16[22,88,128]{2,1,0:T(8,128)(2,1)S(1)} %get-tuple-element.62.refs_2_.refs_1_), channel_id=1, source_target_pairs={{0,2},{4,0},{8,4},{12,8},{14,12},{10,14},{6,10},{2,6},{1,3},{5,1},... | collective-permute-start | bytes 1486856 | tf_op jit(solution)/shard_map/ppermute | solution.py:517
  9.4 1.5 %triangle.5.refs_0_.refs_7_ = bf16[2,22,16,128]{3,2,1,0:T(8,128)(2,1)S(1)} custom-call(s32[8]{0:T(128)S(1)} %copy-done.5, bf16[22,88,128]{2,1,0:T(8,128)(2,1)S(1)} %get-tuple-element.61.refs_1_.refs_3_, bf16[22,88,128]{2,1,0:T(8,128)(2,1)S(1)} %get-tuple-element.62.refs_2_.refs_1_, bf16[22,88,128]{2,1,0:T(8,128)(2,1)S(1)} %get-tuple-element.61.refs_1_.refs_3_), custom_call_target="tpu_custom_call" | custom-call | flops 1024 | bytes 1024 | tf_op jit(solution)/shard_map/triangle/pallas_call | solution.py:93
  11.1 1.3 %collective-permute-done.2.refs_1_ = bf16[2,22,16,128]{3,2,1,0:T(8,128)(2,1)S(1)} collective-permute-done((bf16[2,22,16,128]{3,2,1,0:T(8,128)(2,1)S(1)}, bf16[2,22,16,128]{3,2,1,0:T(8,128)(2,1)S(1)}, u32[]{:S(2)}, u32[]{:S(2)}) %collective-permute-start.2) | collective-permute-done | bytes 180256 | tf_op jit(solution)/shard_map/ppermute | solution.py:77
  12.4 0.6 copy-done.6
  13.6 7.6 %collective-permute-done.1.refs_3_.refs_2_ = bf16[22,88,128]{2,1,0:T(8,128)(2,1)S(1)} collective-permute-done((bf16[22,88,128]{2,1,0:T(8,128)(2,1)S(1)}, bf16[22,88,128]{2,1,0:T(8,128)(2,1)S(1)}, u32[]{:S(2)}, u32[]{:S(2)}) %collective-permute-start.1) | collective-permute-done | bytes 495648 | tf_op jit(solution)/shard_map/ppermute | solution.py:517
  21.2 1.4 %collective-permute-done.refs_2_.refs_1_ = bf16[22,88,128]{2,1,0:T(8,128)(2,1)S(1)} collective-permute-done((bf16[22,88,128]{2,1,0:T(8,128)(2,1)S(1)}, bf16[22,88,128]{2,1,0:T(8,128)(2,1)S(1)}, u32[]{:S(2)}, u32[]{:S(2)}) %collective-permute-start) | collective-permute-done | bytes 495648 | tf_op jit(solution)/shard_map/ppermute | solution.py:514
  23.0 1.7 %collective-permute-start.5 = (bf16[22,88,128]{2,1,0:T(8,128)(2,1)S(1)}, bf16[22,88,128]{2,1,0:T(8,128)(2,1)S(1)}, u32[]{:S(2)}, u32[]{:S(2)}) collective-permute-start(bf16[22,88,128]{2,1,0:T(8,128)(2,1)S(1)} %collective-permute-done.1.refs_3_.refs_2_), channel_id=1, source_target_pairs={{0,2},{4,0},{8,4},{12,8},{14,12},{10,14},{6,10},{2,6},{1,3},{5,1},... | collective-permute-start | bytes 1486856 | tf_op jit(solution)/shard_map/ppermute | solution.py:517
  24.7 4.1 %triangle.6.refs_2_.refs_0_ = bf16[4,22,16,128]{3,2,1,0:T(8,128)(2,1)S(1)} custom-call(s32[8]{0:T(128)S(1)} %copy-done.5, bf16[22,88,128]{2,1,0:T(8,128)(2,1)S(1)} %get-tuple-element.61.refs_1_.refs_3_, bf16[22,88,128]{2,1,0:T(8,128)(2,1)S(1)} %collective-permute-done.refs_2_.refs_1_, bf16[22,88,128]{2,1,0:T(8,128)(2,1)S(1)} %collective-permute-done.1.refs_3_.refs_2_, ...), custom_call_target="tpu_custom_call" | custom-call | flops 1024 | bytes 1024 | tf_op jit(solution)/shard_map/triangle/pallas_call | solution.py:93
  28.9 1.1 left_gradient.5.refs_7_.refs_3_
  30.6 1.0 triangle_norm.6
  31.6 3.6 %collective-permute-done.4.refs_2_.refs_1_ = bf16[22,88,128]{2,1,0:T(8,128)(2,1)S(1)} collective-permute-done((bf16[22,88,128]{2,1,0:T(8,128)(2,1)S(1)}, bf16[22,88,128]{2,1,0:T(8,128)(2,1)S(1)}, u32[]{:S(2)}, u32[]{:S(2)}) %collective-permute-start.4) | collective-permute-done | bytes 495648 | tf_op jit(solution)/shard_map/ppermute | solution.py:514
  35.6 1.6 %collective-permute-start.7 = (bf16[22,88,128]{2,1,0:T(8,128)(2,1)S(1)}, bf16[22,88,128]{2,1,0:T(8,128)(2,1)S(1)}, u32[]{:S(2)}, u32[]{:S(2)}) collective-permute-start(bf16[22,88,128]{2,1,0:T(8,128)(2,1)S(1)} %collective-permute-done.4.refs_2_.refs_1_), channel_id=1, source_target_pairs={{0,4},{4,8},{8,12},{12,14},{14,10},{10,6},{6,2},{2,0},{1,5},{5,9},... | collective-permute-start | bytes 1486856 | tf_op jit(solution)/shard_map/ppermute | solution.py:514
  37.6 4.6 %triangle.7.refs_4_.refs_0_ = bf16[4,22,16,128]{3,2,1,0:T(8,128)(2,1)S(1)} custom-call(s32[8]{0:T(128)S(1)} %copy-done.5, bf16[22,88,128]{2,1,0:T(8,128)(2,1)S(1)} %get-tuple-element.61.refs_1_.refs_3_, bf16[22,88,128]{2,1,0:T(8,128)(2,1)S(1)} %collective-permute-done.4.refs_2_.refs_1_, bf16[22,88,128]{2,1,0:T(8,128)(2,1)S(1)} %collective-permute-done.5.refs_3_.refs_2_, ...), custom_call_target="tpu_custom_call" | custom-call | flops 1024 | bytes 1024 | tf_op jit(solution)/shard_map/triangle/pallas_call | solution.py:93
  42.3 2.3 %left_gradient.6.refs_7_.refs_3_ = f32[22,88,128]{2,1,0:T(8,128)S(1)} custom-call(bf16[4,22,16,128]{3,2,1,0:T(8,128)(2,1)S(1)} %get-tuple-element.67.refs_4_.refs_0_.refs_2_.refs_3_, bf16[22,88,128]{2,1,0:T(8,128)(2,1)S(1)} %collective-permute-done.refs_2_.refs_1_, bf16[22,88,128]{2,1,0:T(8,128)(2,1)S(1)} %collective-permute-done.1.refs_3_.refs_2_, ...), custom_call_target="tpu_custom_call" | custom-call | flops 1024 | bytes 1024 | tf_op jit(solution)/shard_map/left_gradient/pallas_call | solution.py:93
  44.6 1.0 triangle_norm.7
  45.6 1.6 %collective-permute-done.7.refs_2_.refs_1_ = bf16[22,88,128]{2,1,0:T(8,128)(2,1)S(1)} collective-permute-done((bf16[22,88,128]{2,1,0:T(8,128)(2,1)S(1)}, bf16[22,88,128]{2,1,0:T(8,128)(2,1)S(1)}, u32[]{:S(2)}, u32[]{:S(2)}) %collective-permute-start.7) | collective-permute-done | bytes 495648 | tf_op jit(solution)/shard_map/ppermute | solution.py:514
  47.3 1.1 collective-permute-done.8.refs_3_.refs_2_
  48.4 2.8 %triangle.8.refs_4_.refs_0_ = bf16[4,22,16,128]{3,2,1,0:T(8,128)(2,1)S(1)} custom-call(s32[8]{0:T(128)S(1)} %copy-done.5, bf16[22,88,128]{2,1,0:T(8,128)(2,1)S(1)} %get-tuple-element.61.refs_1_.refs_3_, bf16[22,88,128]{2,1,0:T(8,128)(2,1)S(1)} %collective-permute-done.7.refs_2_.refs_1_, bf16[22,88,128]{2,1,0:T(8,128)(2,1)S(1)} %collective-permute-done.8.refs_3_.refs_2_, ...), custom_call_target="tpu_custom_call" | custom-call | flops 1024 | bytes 1024 | tf_op jit(solution)/shard_map/triangle/pallas_call | solution.py:93
  51.3 2.6 %collective-permute-start.11 = (bf16[11,88,128]{2,1,0:T(8,128)(2,1)S(1)}, bf16[11,88,128]{2,1,0:T(8,128)(2,1)S(1)}, u32[]{:S(2)}, u32[]{:S(2)}) collective-permute-start(bf16[11,88,128]{2,1,0:T(8,128)(2,1)S(1)} %slice.7), channel_id=1, source_target_pairs={{0,2},{4,0},{8,4},{12,8},{14,12},{10,14},{6,10},{2,6},{1,3},{5,1},... | collective-permute-start | bytes 743432 | tf_op jit(solution)/shard_map/ppermute | solution.py:517
  53.8 1.2 collective-permute-start.10
  55.0 2.3 %left_gradient.7.refs_7_.refs_3_ = f32[22,88,128]{2,1,0:T(8,128)S(1)} custom-call(bf16[4,22,16,128]{3,2,1,0:T(8,128)(2,1)S(1)} %get-tuple-element.70.refs_4_.refs_0_.refs_2_.refs_3_, bf16[22,88,128]{2,1,0:T(8,128)(2,1)S(1)} %collective-permute-done.4.refs_2_.refs_1_, bf16[22,88,128]{2,1,0:T(8,128)(2,1)S(1)} %collective-permute-done.5.refs_3_.refs_2_, ...), custom_call_target="tpu_custom_call" | custom-call | flops 1024 | bytes 1024 | tf_op jit(solution)/shard_map/left_gradient/pallas_call | solution.py:93
  57.3 1.0 triangle_norm.8
  58.3 1.2 scatter_hop.8
  59.5 2.1 %collective-permute-done.11.refs_3_.refs_2_ = bf16[11,88,128]{2,1,0:T(8,128)(2,1)S(1)} collective-permute-done((bf16[11,88,128]{2,1,0:T(8,128)(2,1)S(1)}, bf16[11,88,128]{2,1,0:T(8,128)(2,1)S(1)}, u32[]{:S(2)}, u32[]{:S(2)}) %collective-permute-start.11) | collective-permute-done | bytes 247840 | tf_op jit(solution)/shard_map/ppermute | solution.py:517
  62.0 2.7 %triangle.9.refs_4_.refs_0_ = bf16[2,22,16,128]{3,2,1,0:T(8,128)(2,1)S(1)} custom-call(s32[8]{0:T(128)S(1)} %copy-done.5, bf16[22,88,128]{2,1,0:T(8,128)(2,1)S(1)} %get-tuple-element.61.refs_1_.refs_3_, bf16[11,88,128]{2,1,0:T(8,128)(2,1)S(1)} %collective-permute-done.10.refs_2_.refs_1_, bf16[11,88,128]{2,1,0:T(8,128)(2,1)S(1)} %collective-permute-done.11.refs_3_.refs_2_, ...), custom_call_target="tpu_custom_call" | custom-call | flops 1024 | bytes 1024 | tf_op jit(solution)/shard_map/triangle/pallas_call | solution.py:93
  65.1 1.8 %collective-permute-start.14 = (bf16[11,88,128]{2,1,0:T(8,128)(2,1)S(1)}, bf16[11,88,128]{2,1,0:T(8,128)(2,1)S(1)}, u32[]{:S(2)}, u32[]{:S(2)}) collective-permute-start(bf16[11,88,128]{2,1,0:T(8,128)(2,1)S(1)} %get-tuple-element.74.refs_4_), channel_id=1, source_target_pairs={{0,2},{4,0},{8,4},{12,8},{14,12},{10,14},{6,10},{2,6},{1,3},{5,1},... | collective-permute-start | bytes 743432 | tf_op jit(solution)/shard_map/ppermute | solution.py:517
  66.8 2.3 %left_gradient.8.refs_7_.refs_3_ = f32[22,88,128]{2,1,0:T(8,128)S(1)} custom-call(bf16[4,22,16,128]{3,2,1,0:T(8,128)(2,1)S(1)} %get-tuple-element.73.refs_2_.refs_3_.refs_4_.refs_0_, bf16[22,88,128]{2,1,0:T(8,128)(2,1)S(1)} %collective-permute-done.7.refs_2_.refs_1_, bf16[22,88,128]{2,1,0:T(8,128)(2,1)S(1)} %collective-permute-done.8.refs_3_.refs_2_, ...), custom_call_target="tpu_custom_call" | custom-call | flops 1024 | bytes 1024 | tf_op jit(solution)/shard_map/left_gradient/pallas_call | solution.py:93
  69.7 1.7 %scatter_hop.9 = (bf16[11,88,128]{2,1,0:T(8,128)(2,1)S(1)}, bf16[11,88,128]{2,1,0:T(8,128)(2,1)S(1)}) custom-call(s32[8]{0:T(128)S(1)} %copy-done.5, bf16[22,88,128]{2,1,0:T(8,128)(2,1)S(1)} %get-tuple-element.61.refs_1_.refs_3_, bf16[2,22,16,128]{3,2,1,0:T(8,128)(2,1)S(1)} %get-tuple-element.75.refs_2_.refs_3_.refs_4_.refs_0_, ...), custom_call_target="tpu_custom_call" | custom-call | flops 1024 | bytes 1024 | tf_op jit(solution)/shard_map/scatter_hop/pallas_call | solution.py:93
  71.4 0.7 collective-permute-start.17
  72.1 1.4 %collective-permute-start.16 = (bf16[11,88,128]{2,1,0:T(8,128)(2,1)S(1)}, bf16[11,88,128]{2,1,0:T(8,128)(2,1)S(1)}, u32[]{:S(2)}, u32[]{:S(2)}) collective-permute-start(bf16[11,88,128]{2,1,0:T(8,128)(2,1)S(1)} %get-tuple-element.76.refs_4_), channel_id=1, source_target_pairs={{0,2},{4,0},{8,4},{12,8},{14,12},{10,14},{6,10},{2,6},{1,3},{5,1},... | collective-permute-start | bytes 743432 | tf_op jit(solution)/shard_map/ppermute | solution.py:517
  73.5 1.2 left_gradient.9.refs_4_.refs_3_
  74.6 1.7 %scatter_hop.10 = (f32[11,88,128]{2,1,0:T(8,128)S(1)}, f32[11,88,128]{2,1,0:T(8,128)S(1)}) custom-call(s32[8]{0:T(128)S(1)} %copy-done.5, bf16[22,88,128]{2,1,0:T(8,128)(2,1)S(1)} %get-tuple-element.61.refs_1_.refs_3_, bf16[4,22,16,128]{3,2,1,0:T(8,128)(2,1)S(1)} %get-tuple-element.70.refs_4_.refs_0_.refs_2_.refs_3_, ...), custom_call_target="tpu_custom_call" | custom-call | flops 1024 | bytes 1024 | tf_op jit(solution)/shard_map/scatter_hop/pallas_call | solution.py:93
  76.5 1.2 collective-permute-start.19
  77.6 0.9 collective-permute-start.18
  78.5 1.4 %scatter_hop.11 = (f32[11,88,128]{2,1,0:T(8,128)S(1)}, f32[11,88,128]{2,1,0:T(8,128)S(1)}) custom-call(s32[8]{0:T(128)S(1)} %copy-done.5, bf16[22,88,128]{2,1,0:T(8,128)(2,1)S(1)} %get-tuple-element.61.refs_1_.refs_3_, bf16[4,22,16,128]{3,2,1,0:T(8,128)(2,1)S(1)} %get-tuple-element.73.refs_2_.refs_3_.refs_4_.refs_0_, ...), custom_call_target="tpu_custom_call" | custom-call | flops 1024 | bytes 1024 | tf_op jit(solution)/shard_map/scatter_hop/pallas_call | solution.py:93
  80.0 1.1 collective-permute-done.16.refs_2_
  81.2 2.3 %collective-permute-start.21 = (bf16[11,88,128]{2,1,0:T(8,128)(2,1)S(1)}, bf16[11,88,128]{2,1,0:T(8,128)(2,1)S(1)}, u32[]{:S(2)}, u32[]{:S(2)}) collective-permute-start(bf16[11,88,128]{2,1,0:T(8,128)(2,1)S(1)} %get-tuple-element.96), channel_id=1, source_target_pairs={{0,4},{4,8},{8,12},{12,14},{14,10},{10,6},{6,2},{2,0},{1,5},{5,9},... | collective-permute-start | bytes 743432 | tf_op jit(solution)/shard_map/ppermute | solution.py:514
  83.4 1.7 %scatter_hop.12 = (f32[11,88,128]{2,1,0:T(8,128)S(1)}, f32[11,88,128]{2,1,0:T(8,128)S(1)}) custom-call(s32[8]{0:T(128)S(1)} %copy-done.5, bf16[22,88,128]{2,1,0:T(8,128)(2,1)S(1)} %get-tuple-element.61.refs_1_.refs_3_, bf16[4,22,16,128]{3,2,1,0:T(8,128)(2,1)S(1)} %get-tuple-element.67.refs_4_.refs_0_.refs_2_.refs_3_, ...), custom_call_target="tpu_custom_call" | custom-call | flops 1024 | bytes 1024 | tf_op jit(solution)/shard_map/scatter_hop/pallas_call | solution.py:93
  85.5 1.1 collective-permute-done.18.refs_2_
  86.7 0.9 collective-permute-start.24
  87.6 1.7 %scatter_hop.13 = (f32[11,88,128]{2,1,0:T(8,128)S(1)}, f32[11,88,128]{2,1,0:T(8,128)S(1)}) custom-call(s32[8]{0:T(128)S(1)} %copy-done.5, bf16[22,88,128]{2,1,0:T(8,128)(2,1)S(1)} %get-tuple-element.61.refs_1_.refs_3_, bf16[4,22,16,128]{3,2,1,0:T(8,128)(2,1)S(1)} %get-tuple-element.70.refs_4_.refs_0_.refs_2_.refs_3_, ...), custom_call_target="tpu_custom_call" | custom-call | flops 1024 | bytes 1024 | tf_op jit(solution)/shard_map/scatter_hop/pallas_call | solution.py:93
  89.3 1.0 collective-permute-start.25
  90.3 2.1 %collective-permute-done.20.refs_2_ = bf16[11,88,128]{2,1,0:T(8,128)(2,1)S(1)} collective-permute-done((bf16[11,88,128]{2,1,0:T(8,128)(2,1)S(1)}, bf16[11,88,128]{2,1,0:T(8,128)(2,1)S(1)}, u32[]{:S(2)}, u32[]{:S(2)}) %collective-permute-start.20) | collective-permute-done | bytes 247840 | tf_op jit(solution)/shard_map/ppermute | solution.py:517
  92.5 1.6 %collective-permute-start.23 = (bf16[11,88,128]{2,1,0:T(8,128)(2,1)S(1)}, bf16[11,88,128]{2,1,0:T(8,128)(2,1)S(1)}, u32[]{:S(2)}, u32[]{:S(2)}) collective-permute-start(bf16[11,88,128]{2,1,0:T(8,128)(2,1)S(1)} %get-tuple-element.101), channel_id=1, source_target_pairs={{0,4},{4,8},{8,12},{12,14},{14,10},{10,6},{6,2},{2,0},{1,5},{5,9},... | collective-permute-start | bytes 743432 | tf_op jit(solution)/shard_map/ppermute | solution.py:514
  94.6 1.2 scatter_hop.14
  95.8 1.4 %scatter_hop.15 = (f32[11,88,128]{2,1,0:T(8,128)S(1)}, f32[11,88,128]{2,1,0:T(8,128)S(1)}) custom-call(s32[8]{0:T(128)S(1)} %copy-done.5, bf16[22,88,128]{2,1,0:T(8,128)(2,1)S(1)} %get-tuple-element.61.refs_1_.refs_3_, bf16[4,22,16,128]{3,2,1,0:T(8,128)(2,1)S(1)} %get-tuple-element.67.refs_4_.refs_0_.refs_2_.refs_3_, ...), custom_call_target="tpu_custom_call" | custom-call | flops 1024 | bytes 1024 | tf_op jit(solution)/shard_map/scatter_hop/pallas_call | solution.py:93
  97.8 2.7 %collective-permute-done.23.refs_3_ = bf16[11,88,128]{2,1,0:T(8,128)(2,1)S(1)} collective-permute-done((bf16[11,88,128]{2,1,0:T(8,128)(2,1)S(1)}, bf16[11,88,128]{2,1,0:T(8,128)(2,1)S(1)}, u32[]{:S(2)}, u32[]{:S(2)}) %collective-permute-start.23) | collective-permute-done | bytes 247840 | tf_op jit(solution)/shard_map/ppermute | solution.py:514
  100.5 1.1 collective-permute-done.22.refs_2_
  101.7 1.8 %collective-permute-start.27 = (bf16[11,88,128]{2,1,0:T(8,128)(2,1)S(1)}, bf16[11,88,128]{2,1,0:T(8,128)(2,1)S(1)}, u32[]{:S(2)}, u32[]{:S(2)}) collective-permute-start(bf16[11,88,128]{2,1,0:T(8,128)(2,1)S(1)} %get-tuple-element.107), channel_id=1, source_target_pairs={{0,4},{4,8},{8,12},{12,14},{14,10},{10,6},{6,2},{2,0},{1,5},{5,9},... | collective-permute-start | bytes 743432 | tf_op jit(solution)/shard_map/ppermute | solution.py:514
  103.8 6.8 %output_side.1 = (bf16[22,88,128]{2,1,0:T(8,128)(2,1)}, f32[22,88,128]{2,1,0:T(8,128)S(1)}, f32[128,512]{1,0:T(8,128)S(1)}) custom-call(s32[8]{0:T(128)S(1)} %copy-done.5, bf16[22,88,128]{2,1,0:T(8,128)(2,1)S(1)} %get-tuple-element.60.refs_1_, bf16[22,88,128]{2,1,0:T(8,128)(2,1)S(1)} %copy-done.10, f32[22,88,128]{2,1,0:T(8,128)S(1)} %left_gradient.9.refs_4_.refs_3_, ...), custom_call_target="tpu_custom_call" | custom-call | flops 6600001024 | bytes 1024 | tf_op jit(solution)/shard_map/output_side/pallas_call | solution.py:93
  110.6 2.0 %right_gradient.1 = (bf16[22,88,256]{2,1,0:T(8,128)(2,1)S(1)}, bf16[64,768]{1,0:T(8,128)(2,1)S(1)}, bf16[64,768]{1,0:T(8,128)(2,1)S(1)}) custom-call(s32[8]{0:T(128)S(1)} %copy-done.5, bf16[22,88,128]{2,1,0:T(8,128)(2,1)S(1)} %get-tuple-element.60.refs_1_, bf16[128,640]{1,0:T(8,128)(2,1)S(1)} %copy-done.2, f32[128,512]{1,0:T(8,128)S(1)} %get-tuple-element.105.refs_3_, ...), custom_call_target="tpu_custom_call" | custom-call | flops 1024 | bytes 1024 | tf_op jit(solution)/shard_map/right_gradient/pallas_call | solution.py:93
  112.7 1.3 collective-permute-done.28
  114.1 0.7 collective-permute-start.29
  114.7 4.2 %collective-permute-done.29 = bf16[64,768]{1,0:T(8,128)(2,1)S(1)} collective-permute-done((bf16[64,768]{1,0:T(8,128)(2,1)S(1)}, bf16[64,768]{1,0:T(8,128)(2,1)S(1)}, u32[]{:S(2)}, u32[]{:S(2)}) %collective-permute-start.29) | collective-permute-done | bytes 98336 | tf_op jit(solution)/shard_map/ppermute | solution.py:673
  119.0 1.8 %collective-permute-start.30 = (bf16[64,768]{1,0:T(8,128)(2,1)S(1)}, bf16[64,768]{1,0:T(8,128)(2,1)S(1)}, u32[]{:S(2)}, u32[]{:S(2)}) collective-permute-start(bf16[64,768]{1,0:T(8,128)(2,1)S(1)} %add_convert_fusion.2), channel_id=1, source_target_pairs={{0,4},{2,6},{4,0},{6,2},{8,12},{10,14},{12,8},{14,10},{1,5},{3,7},... | collective-permute-start | bytes 294920 | tf_op jit(solution)/shard_map/ppermute | solution.py:673
  120.8 2.9 %collective-permute-done.30 = bf16[64,768]{1,0:T(8,128)(2,1)S(1)} collective-permute-done((bf16[64,768]{1,0:T(8,128)(2,1)S(1)}, bf16[64,768]{1,0:T(8,128)(2,1)S(1)}, u32[]{:S(2)}, u32[]{:S(2)}) %collective-permute-start.30) | collective-permute-done | bytes 98336 | tf_op jit(solution)/shard_map/ppermute | solution.py:673
  123.7 1.6 %collective-permute-start.31 = (bf16[64,768]{1,0:T(8,128)(2,1)S(1)}, bf16[64,768]{1,0:T(8,128)(2,1)S(1)}, u32[]{:S(2)}, u32[]{:S(2)}) collective-permute-start(bf16[64,768]{1,0:T(8,128)(2,1)S(1)} %add_convert_fusion.1), channel_id=1, source_target_pairs={{0,8},{2,10},{4,12},{6,14},{8,0},{10,2},{12,4},{14,6},{1,9},{3,11}... | collective-permute-start | bytes 294920 | tf_op jit(solution)/shard_map/ppermute | solution.py:673
  125.3 4.1 %pair_gradient.1 = bf16[22,88,128]{2,1,0:T(8,128)(2,1)} custom-call(bf16[22,88,128]{2,1,0:T(8,128)(2,1)S(1)} %copy-done.4, bf16[22,88,256]{2,1,0:T(8,128)(2,1)S(1)} %get-tuple-element.110.refs_1_, f32[1,128]{1,0:T(1,128)S(1)} %bitcast.16, bf16[128,640]{1,0:T(8,128)(2,1)S(1)} %copy-done.2, f32[22,88,128]{2,1,0:T(8,128)S(1)} %get-tuple-element.111.refs_4_), custom_call_target="tpu_custom_call" | custom-call | flops 3300001024 | bytes 1024 | tf_op jit(solution)/shard_map/pair_gradient/pallas_call | solution.py:93
  129.5 1.3 collective-permute-done.32.refs_1_
  130.8 0.8 weight_gradients.1
  (64 shorter events, 7.9 us)
Async XLA Ops:
  0.6 0.7 copy-start.5
  0.6 0.7 copy-start.8
  0.7 0.7 copy-start.9
  1.3 0.9 copy-start.1
  2.2 1.0 copy-start.3
  3.3 1.5 %copy-start.2 = (bf16[128,640]{1,0:T(8,128)(2,1)S(1)}, bf16[128,640]{1,0:T(8,128)(2,1)}, u32[]{:S(2)}) copy-start(bf16[128,640]{1,0:T(8,128)(2,1)} %refs_3_.3) | copy-start | bytes 491524
  3.3 1.5 %copy-start.10 = (bf16[22,88,128]{2,1,0:T(8,128)(2,1)S(1)}, bf16[22,88,128]{2,1,0:T(8,128)(2,1)}, u32[]{:S(2)}) copy-start(bf16[22,88,128]{2,1,0:T(8,128)(2,1)} %refs_2_.4) | copy-start | bytes 1486852
  6.2 6.2 %collective-permute-start.3 = (bf16[8,22,16,128]{3,2,1,0:T(8,128)(2,1)S(1)}, bf16[8,22,16,128]{3,2,1,0:T(8,128)(2,1)S(1)}, u32[]{:S(2)}, u32[]{:S(2)}) collective-permute-start(bf16[8,22,16,128]{3,2,1,0:T(8,128)(2,1)S(1)} %get-tuple-element.63.refs_2_.refs_6_), channel_id=1, source_target_pairs={{0,1},{1,0},{2,3},{3,2},{4,5},{5,4},{6,7},{7,6},{8,9},{9,8},{10,11... | collective-permute-start | bytes 2162696 | tf_op jit(solution)/shard_map/ppermute | solution.py:77
  6.7 14.6 %collective-permute-start.1 = (bf16[22,88,128]{2,1,0:T(8,128)(2,1)S(1)}, bf16[22,88,128]{2,1,0:T(8,128)(2,1)S(1)}, u32[]{:S(2)}, u32[]{:S(2)}) collective-permute-start(bf16[22,88,128]{2,1,0:T(8,128)(2,1)S(1)} %get-tuple-element.62.refs_2_.refs_1_), channel_id=1, source_target_pairs={{0,2},{4,0},{8,4},{12,8},{14,12},{10,14},{6,10},{2,6},{1,3},{5,1},... | collective-permute-start | bytes 1486856 | tf_op jit(solution)/shard_map/ppermute | solution.py:517
  9.3 13.4 %collective-permute-start = (bf16[22,88,128]{2,1,0:T(8,128)(2,1)S(1)}, bf16[22,88,128]{2,1,0:T(8,128)(2,1)S(1)}, u32[]{:S(2)}, u32[]{:S(2)}) collective-permute-start(bf16[22,88,128]{2,1,0:T(8,128)(2,1)S(1)} %get-tuple-element.62.refs_2_.refs_1_), channel_id=1, source_target_pairs={{0,4},{4,8},{8,12},{12,14},{14,10},{10,6},{6,2},{2,0},{1,5},{5,9},... | collective-permute-start | bytes 1486856 | tf_op jit(solution)/shard_map/ppermute | solution.py:514
  9.4 3.0 %copy-start = (bf16[128,128]{1,0:T(8,128)(2,1)S(1)}, bf16[128,128]{1,0:T(8,128)(2,1)}, u32[]{:S(2)}) copy-start(bf16[128,128]{1,0:T(8,128)(2,1)} %refs_5_.1) | copy-start | bytes 98308
  10.9 1.5 %collective-permute-start.2 = (bf16[2,22,16,128]{3,2,1,0:T(8,128)(2,1)S(1)}, bf16[2,22,16,128]{3,2,1,0:T(8,128)(2,1)S(1)}, u32[]{:S(2)}, u32[]{:S(2)}) collective-permute-start(bf16[2,22,16,128]{3,2,1,0:T(8,128)(2,1)S(1)} %triangle.5.refs_0_.refs_7_), channel_id=1, source_target_pairs={{0,1},{1,0},{2,3},{3,2},{4,5},{5,4},{6,7},{7,6},{8,9},{9,8},{10,11... | collective-permute-start | bytes 540680 | tf_op jit(solution)/shard_map/ppermute | solution.py:77
  12.4 0.7 copy-start.6
  12.4 0.7 copy-start.7
  22.6 12.6 %collective-permute-start.4 = (bf16[22,88,128]{2,1,0:T(8,128)(2,1)S(1)}, bf16[22,88,128]{2,1,0:T(8,128)(2,1)S(1)}, u32[]{:S(2)}, u32[]{:S(2)}) collective-permute-start(bf16[22,88,128]{2,1,0:T(8,128)(2,1)S(1)} %collective-permute-done.refs_2_.refs_1_), channel_id=1, source_target_pairs={{0,4},{4,8},{8,12},{12,14},{14,10},{10,6},{6,2},{2,0},{1,5},{5,9},... | collective-permute-start | bytes 1486856 | tf_op jit(solution)/shard_map/ppermute | solution.py:514
  23.0 12.6 %collective-permute-start.5 = (bf16[22,88,128]{2,1,0:T(8,128)(2,1)S(1)}, bf16[22,88,128]{2,1,0:T(8,128)(2,1)S(1)}, u32[]{:S(2)}, u32[]{:S(2)}) collective-permute-start(bf16[22,88,128]{2,1,0:T(8,128)(2,1)S(1)} %collective-permute-done.1.refs_3_.refs_2_), channel_id=1, source_target_pairs={{0,2},{4,0},{8,4},{12,8},{14,12},{10,14},{6,10},{2,6},{1,3},{5,1},... | collective-permute-start | bytes 1486856 | tf_op jit(solution)/shard_map/ppermute | solution.py:517
  28.8 1.7 %collective-permute-start.6 = (bf16[4,22,16,128]{3,2,1,0:T(8,128)(2,1)S(1)}, bf16[4,22,16,128]{3,2,1,0:T(8,128)(2,1)S(1)}, u32[]{:S(2)}, u32[]{:S(2)}) collective-permute-start(bf16[4,22,16,128]{3,2,1,0:T(8,128)(2,1)S(1)} %triangle.6.refs_2_.refs_0_), channel_id=1, source_target_pairs={{0,1},{1,0},{2,3},{3,2},{4,5},{5,4},{6,7},{7,6},{8,9},{9,8},{10,11... | collective-permute-start | bytes 1081352 | tf_op jit(solution)/shard_map/ppermute | solution.py:77
  35.6 11.7 %collective-permute-start.7 = (bf16[22,88,128]{2,1,0:T(8,128)(2,1)S(1)}, bf16[22,88,128]{2,1,0:T(8,128)(2,1)S(1)}, u32[]{:S(2)}, u32[]{:S(2)}) collective-permute-start(bf16[22,88,128]{2,1,0:T(8,128)(2,1)S(1)} %collective-permute-done.4.refs_2_.refs_1_), channel_id=1, source_target_pairs={{0,4},{4,8},{8,12},{12,14},{14,10},{10,6},{6,2},{2,0},{1,5},{5,9},... | collective-permute-start | bytes 1486856 | tf_op jit(solution)/shard_map/ppermute | solution.py:514
  37.2 11.2 %collective-permute-start.8 = (bf16[22,88,128]{2,1,0:T(8,128)(2,1)S(1)}, bf16[22,88,128]{2,1,0:T(8,128)(2,1)S(1)}, u32[]{:S(2)}, u32[]{:S(2)}) collective-permute-start(bf16[22,88,128]{2,1,0:T(8,128)(2,1)S(1)} %collective-permute-done.5.refs_3_.refs_2_), channel_id=1, source_target_pairs={{0,2},{4,0},{8,4},{12,8},{14,12},{10,14},{6,10},{2,6},{1,3},{5,1},... | collective-permute-start | bytes 1486856 | tf_op jit(solution)/shard_map/ppermute | solution.py:517
  42.3 2.4 %collective-permute-start.9 = (bf16[4,22,16,128]{3,2,1,0:T(8,128)(2,1)S(1)}, bf16[4,22,16,128]{3,2,1,0:T(8,128)(2,1)S(1)}, u32[]{:S(2)}, u32[]{:S(2)}) collective-permute-start(bf16[4,22,16,128]{3,2,1,0:T(8,128)(2,1)S(1)} %triangle.7.refs_4_.refs_0_), channel_id=1, source_target_pairs={{0,1},{1,0},{2,3},{3,2},{4,5},{5,4},{6,7},{7,6},{8,9},{9,8},{10,11... | collective-permute-start | bytes 1081352 | tf_op jit(solution)/shard_map/ppermute | solution.py:77
  51.1 6.2 %collective-permute-start.12 = (bf16[4,22,16,128]{3,2,1,0:T(8,128)(2,1)S(1)}, bf16[4,22,16,128]{3,2,1,0:T(8,128)(2,1)S(1)}, u32[]{:S(2)}, u32[]{:S(2)}) collective-permute-start(bf16[4,22,16,128]{3,2,1,0:T(8,128)(2,1)S(1)} %triangle.8.refs_4_.refs_0_), channel_id=1, source_target_pairs={{0,1},{1,0},{2,3},{3,2},{4,5},{5,4},{6,7},{7,6},{8,9},{9,8},{10,11... | collective-permute-start | bytes 1081352 | tf_op jit(solution)/shard_map/ppermute | solution.py:77
  51.3 10.3 %collective-permute-start.11 = (bf16[11,88,128]{2,1,0:T(8,128)(2,1)S(1)}, bf16[11,88,128]{2,1,0:T(8,128)(2,1)S(1)}, u32[]{:S(2)}, u32[]{:S(2)}) collective-permute-start(bf16[11,88,128]{2,1,0:T(8,128)(2,1)S(1)} %slice.7), channel_id=1, source_target_pairs={{0,2},{4,0},{8,4},{12,8},{14,12},{10,14},{6,10},{2,6},{1,3},{5,1},... | collective-permute-start | bytes 743432 | tf_op jit(solution)/shard_map/ppermute | solution.py:517
  53.8 8.1 %collective-permute-start.10 = (bf16[11,88,128]{2,1,0:T(8,128)(2,1)S(1)}, bf16[11,88,128]{2,1,0:T(8,128)(2,1)S(1)}, u32[]{:S(2)}, u32[]{:S(2)}) collective-permute-start(bf16[11,88,128]{2,1,0:T(8,128)(2,1)S(1)} %slice.6), channel_id=1, source_target_pairs={{0,4},{4,8},{8,12},{12,14},{14,10},{10,6},{6,2},{2,0},{1,5},{5,9},... | collective-permute-start | bytes 743432 | tf_op jit(solution)/shard_map/ppermute | solution.py:514
  64.7 4.5 %collective-permute-start.13 = (bf16[2,22,16,128]{3,2,1,0:T(8,128)(2,1)S(1)}, bf16[2,22,16,128]{3,2,1,0:T(8,128)(2,1)S(1)}, u32[]{:S(2)}, u32[]{:S(2)}) collective-permute-start(bf16[2,22,16,128]{3,2,1,0:T(8,128)(2,1)S(1)} %triangle.9.refs_4_.refs_0_), channel_id=1, source_target_pairs={{0,1},{1,0},{2,3},{3,2},{4,5},{5,4},{6,7},{7,6},{8,9},{9,8},{10,11... | collective-permute-start | bytes 540680 | tf_op jit(solution)/shard_map/ppermute | solution.py:77
  64.7 11.6 %collective-permute-start.15 = (bf16[11,88,128]{2,1,0:T(8,128)(2,1)S(1)}, bf16[11,88,128]{2,1,0:T(8,128)(2,1)S(1)}, u32[]{:S(2)}, u32[]{:S(2)}) collective-permute-start(bf16[11,88,128]{2,1,0:T(8,128)(2,1)S(1)} %get-tuple-element.84), channel_id=1, source_target_pairs={{0,4},{4,8},{8,12},{12,14},{14,10},{10,6},{6,2},{2,0},{1,5},{5,9},... | collective-permute-start | bytes 743432 | tf_op jit(solution)/shard_map/ppermute | solution.py:514
  65.1 11.2 %collective-permute-start.14 = (bf16[11,88,128]{2,1,0:T(8,128)(2,1)S(1)}, bf16[11,88,128]{2,1,0:T(8,128)(2,1)S(1)}, u32[]{:S(2)}, u32[]{:S(2)}) collective-permute-start(bf16[11,88,128]{2,1,0:T(8,128)(2,1)S(1)} %get-tuple-element.74.refs_4_), channel_id=1, source_target_pairs={{0,2},{4,0},{8,4},{12,8},{14,12},{10,14},{6,10},{2,6},{1,3},{5,1},... | collective-permute-start | bytes 743432 | tf_op jit(solution)/shard_map/ppermute | solution.py:517
  71.4 8.6 %collective-permute-start.17 = (bf16[11,88,128]{2,1,0:T(8,128)(2,1)S(1)}, bf16[11,88,128]{2,1,0:T(8,128)(2,1)S(1)}, u32[]{:S(2)}, u32[]{:S(2)}) collective-permute-start(bf16[11,88,128]{2,1,0:T(8,128)(2,1)S(1)} %get-tuple-element.88), channel_id=1, source_target_pairs={{0,4},{4,8},{8,12},{12,14},{14,10},{10,6},{6,2},{2,0},{1,5},{5,9},... | collective-permute-start | bytes 743432 | tf_op jit(solution)/shard_map/ppermute | solution.py:514
  72.1 9.0 %collective-permute-start.16 = (bf16[11,88,128]{2,1,0:T(8,128)(2,1)S(1)}, bf16[11,88,128]{2,1,0:T(8,128)(2,1)S(1)}, u32[]{:S(2)}, u32[]{:S(2)}) collective-permute-start(bf16[11,88,128]{2,1,0:T(8,128)(2,1)S(1)} %get-tuple-element.76.refs_4_), channel_id=1, source_target_pairs={{0,2},{4,0},{8,4},{12,8},{14,12},{10,14},{6,10},{2,6},{1,3},{5,1},... | collective-permute-start | bytes 743432 | tf_op jit(solution)/shard_map/ppermute | solution.py:517
  76.5 9.0 %collective-permute-start.19 = (bf16[11,88,128]{2,1,0:T(8,128)(2,1)S(1)}, bf16[11,88,128]{2,1,0:T(8,128)(2,1)S(1)}, u32[]{:S(2)}, u32[]{:S(2)}) collective-permute-start(bf16[11,88,128]{2,1,0:T(8,128)(2,1)S(1)} %get-tuple-element.92), channel_id=1, source_target_pairs={{0,4},{4,8},{8,12},{12,14},{14,10},{10,6},{6,2},{2,0},{1,5},{5,9},... | collective-permute-start | bytes 743432 | tf_op jit(solution)/shard_map/ppermute | solution.py:514
  77.6 8.9 %collective-permute-start.18 = (bf16[11,88,128]{2,1,0:T(8,128)(2,1)S(1)}, bf16[11,88,128]{2,1,0:T(8,128)(2,1)S(1)}, u32[]{:S(2)}, u32[]{:S(2)}) collective-permute-start(bf16[11,88,128]{2,1,0:T(8,128)(2,1)S(1)} %get-tuple-element.85.refs_4_), channel_id=1, source_target_pairs={{0,2},{4,0},{8,4},{12,8},{14,12},{10,14},{6,10},{2,6},{1,3},{5,1},... | collective-permute-start | bytes 743432 | tf_op jit(solution)/shard_map/ppermute | solution.py:517
  81.2 9.1 %collective-permute-start.21 = (bf16[11,88,128]{2,1,0:T(8,128)(2,1)S(1)}, bf16[11,88,128]{2,1,0:T(8,128)(2,1)S(1)}, u32[]{:S(2)}, u32[]{:S(2)}) collective-permute-start(bf16[11,88,128]{2,1,0:T(8,128)(2,1)S(1)} %get-tuple-element.96), channel_id=1, source_target_pairs={{0,4},{4,8},{8,12},{12,14},{14,10},{10,6},{6,2},{2,0},{1,5},{5,9},... | collective-permute-start | bytes 743432 | tf_op jit(solution)/shard_map/ppermute | solution.py:514
  83.4 8.9 %collective-permute-start.20 = (bf16[11,88,128]{2,1,0:T(8,128)(2,1)S(1)}, bf16[11,88,128]{2,1,0:T(8,128)(2,1)S(1)}, u32[]{:S(2)}, u32[]{:S(2)}) collective-permute-start(bf16[11,88,128]{2,1,0:T(8,128)(2,1)S(1)} %get-tuple-element.89.refs_4_), channel_id=1, source_target_pairs={{0,2},{4,0},{8,4},{12,8},{14,12},{10,14},{6,10},{2,6},{1,3},{5,1},... | collective-permute-start | bytes 743432 | tf_op jit(solution)/shard_map/ppermute | solution.py:517
  86.7 11.1 %collective-permute-start.24 = (bf16[11,88,128]{2,1,0:T(8,128)(2,1)S(1)}, bf16[11,88,128]{2,1,0:T(8,128)(2,1)S(1)}, u32[]{:S(2)}, u32[]{:S(2)}) collective-permute-start(bf16[11,88,128]{2,1,0:T(8,128)(2,1)S(1)} %get-tuple-element.93.refs_4_), channel_id=1, source_target_pairs={{0,2},{4,0},{8,4},{12,8},{14,12},{10,14},{6,10},{2,6},{1,3},{5,1},... | collective-permute-start | bytes 743432 | tf_op jit(solution)/shard_map/ppermute | solution.py:517
  89.3 8.5 %collective-permute-start.25 = (bf16[11,88,128]{2,1,0:T(8,128)(2,1)S(1)}, bf16[11,88,128]{2,1,0:T(8,128)(2,1)S(1)}, u32[]{:S(2)}, u32[]{:S(2)}) collective-permute-start(bf16[11,88,128]{2,1,0:T(8,128)(2,1)S(1)} %get-tuple-element.102), channel_id=1, source_target_pairs={{0,4},{4,8},{8,12},{12,14},{14,10},{10,6},{6,2},{2,0},{1,5},{5,9},... | collective-permute-start | bytes 743432 | tf_op jit(solution)/shard_map/ppermute | solution.py:514
  92.5 7.9 %collective-permute-start.23 = (bf16[11,88,128]{2,1,0:T(8,128)(2,1)S(1)}, bf16[11,88,128]{2,1,0:T(8,128)(2,1)S(1)}, u32[]{:S(2)}, u32[]{:S(2)}) collective-permute-start(bf16[11,88,128]{2,1,0:T(8,128)(2,1)S(1)} %get-tuple-element.101), channel_id=1, source_target_pairs={{0,4},{4,8},{8,12},{12,14},{14,10},{10,6},{6,2},{2,0},{1,5},{5,9},... | collective-permute-start | bytes 743432 | tf_op jit(solution)/shard_map/ppermute | solution.py:514
  94.1 7.5 %collective-permute-start.22 = (bf16[11,88,128]{2,1,0:T(8,128)(2,1)S(1)}, bf16[11,88,128]{2,1,0:T(8,128)(2,1)S(1)}, u32[]{:S(2)}, u32[]{:S(2)}) collective-permute-start(bf16[11,88,128]{2,1,0:T(8,128)(2,1)S(1)} %get-tuple-element.97.refs_4_), channel_id=1, source_target_pairs={{0,2},{4,0},{8,4},{12,8},{14,12},{10,14},{6,10},{2,6},{1,3},{5,1},... | collective-permute-start | bytes 743432 | tf_op jit(solution)/shard_map/ppermute | solution.py:517
  101.7 8.9 %collective-permute-start.27 = (bf16[11,88,128]{2,1,0:T(8,128)(2,1)S(1)}, bf16[11,88,128]{2,1,0:T(8,128)(2,1)S(1)}, u32[]{:S(2)}, u32[]{:S(2)}) collective-permute-start(bf16[11,88,128]{2,1,0:T(8,128)(2,1)S(1)} %get-tuple-element.107), channel_id=1, source_target_pairs={{0,4},{4,8},{8,12},{12,14},{14,10},{10,6},{6,2},{2,0},{1,5},{5,9},... | collective-permute-start | bytes 743432 | tf_op jit(solution)/shard_map/ppermute | solution.py:514
  103.5 7.1 %collective-permute-start.26 = (bf16[11,88,128]{2,1,0:T(8,128)(2,1)S(1)}, bf16[11,88,128]{2,1,0:T(8,128)(2,1)S(1)}, u32[]{:S(2)}, u32[]{:S(2)}) collective-permute-start(bf16[11,88,128]{2,1,0:T(8,128)(2,1)S(1)} %get-tuple-element.103.refs_12_), channel_id=1, source_target_pairs={{0,2},{4,0},{8,4},{12,8},{14,12},{10,14},{6,10},{2,6},{1,3},{5,1},... | collective-permute-start | bytes 743432 | tf_op jit(solution)/shard_map/ppermute | solution.py:517
  112.7 12.7 %copy-start.4 = (bf16[22,88,128]{2,1,0:T(8,128)(2,1)S(1)}, bf16[22,88,128]{2,1,0:T(8,128)(2,1)}, u32[]{:S(2)}) copy-start(bf16[22,88,128]{2,1,0:T(8,128)(2,1)} %refs_0_.35) | copy-start | bytes 1486852
  112.7 1.4 %collective-permute-start.28 = (bf16[64,768]{1,0:T(8,128)(2,1)S(1)}, bf16[64,768]{1,0:T(8,128)(2,1)S(1)}, u32[]{:S(2)}, u32[]{:S(2)}) collective-permute-start(bf16[64,768]{1,0:T(8,128)(2,1)S(1)} %get-tuple-element.109), channel_id=1, source_target_pairs={{0,1},{1,0},{2,3},{3,2},{4,5},{5,4},{6,7},{7,6},{8,9},{9,8},{10,11... | collective-permute-start | bytes 294920 | tf_op jit(solution)/shard_map/ppermute | solution.py:77
  114.1 4.9 %collective-permute-start.29 = (bf16[64,768]{1,0:T(8,128)(2,1)S(1)}, bf16[64,768]{1,0:T(8,128)(2,1)S(1)}, u32[]{:S(2)}, u32[]{:S(2)}) collective-permute-start(bf16[64,768]{1,0:T(8,128)(2,1)S(1)} %add_convert_fusion.3), channel_id=1, source_target_pairs={{0,2},{2,0},{4,6},{6,4},{8,10},{10,8},{12,14},{14,12},{1,3},{3,1},... | collective-permute-start | bytes 294920 | tf_op jit(solution)/shard_map/ppermute | solution.py:673
  119.0 4.7 %collective-permute-start.30 = (bf16[64,768]{1,0:T(8,128)(2,1)S(1)}, bf16[64,768]{1,0:T(8,128)(2,1)S(1)}, u32[]{:S(2)}, u32[]{:S(2)}) collective-permute-start(bf16[64,768]{1,0:T(8,128)(2,1)S(1)} %add_convert_fusion.2), channel_id=1, source_target_pairs={{0,4},{2,6},{4,0},{6,2},{8,12},{10,14},{12,8},{14,10},{1,5},{3,7},... | collective-permute-start | bytes 294920 | tf_op jit(solution)/shard_map/ppermute | solution.py:673
  123.7 5.7 %collective-permute-start.31 = (bf16[64,768]{1,0:T(8,128)(2,1)S(1)}, bf16[64,768]{1,0:T(8,128)(2,1)S(1)}, u32[]{:S(2)}, u32[]{:S(2)}) collective-permute-start(bf16[64,768]{1,0:T(8,128)(2,1)S(1)} %add_convert_fusion.1), channel_id=1, source_target_pairs={{0,8},{2,10},{4,12},{6,14},{8,0},{10,2},{12,4},{14,6},{1,9},{3,11}... | collective-permute-start | bytes 294920 | tf_op jit(solution)/shard_map/ppermute | solution.py:673
  129.4 1.4 %collective-permute-start.32 = (bf16[64,768]{1,0:T(8,128)(2,1)S(1)}, bf16[64,768]{1,0:T(8,128)(2,1)S(1)}, u32[]{:S(2)}, u32[]{:S(2)}) collective-permute-start(bf16[64,768]{1,0:T(8,128)(2,1)S(1)} %add_convert_fusion.refs_0_), channel_id=1, source_target_pairs={{0,1},{1,0},{2,3},{3,2},{4,5},{5,4},{6,7},{7,6},{8,9},{9,8},{10,11... | collective-permute-start | bytes 294920 | tf_op jit(solution)/shard_map/ppermute | solution.py:77

commit v2 on v1

--- a/solution.py
+++ b/solution.py
@@ -64,7 +64,7 @@
     apart = (apart + row_count) % row_count
     near = jnp.where(letter == 0, row_count - apart, apart)
     first = 4 * near - 2 + letter
-    second = 4 * (row_count - near) - 2 + 3 - letter
+    second = 4 * (row_count - near) + 1 - letter
     return jnp.where(apart == 0, letter, jnp.where(near <= hops, first, second))
 
 
@@ -148,7 +148,7 @@
     return lax.axis_index("row") * here
 
 
-def input_kernel(slot, lengths, pair, gain, bias, w, right, normed, mask):
+def input_kernel(slot, lengths, pair, gain, bias, w, right_a, right_b, normed, mask):
     here, half, hidden = pair.shape
     mask[...] = present_columns(lengths, slot, half)
 
@@ -159,7 +159,8 @@
         proj = dot(values, w[:, 2 * hidden : 4 * hidden], 1, 0)
         shown = mask[...] * present_row(lengths, slot, first_row(here) + i)
         gated = jax.nn.sigmoid(proj[:, :hidden]) * proj[:, hidden:]
-        right[i] = (shown * gated).astype(bf16)
+        out, at = (right_a, i) if i < here // 2 else (right_b, i - here // 2)
+        out[at] = (shown * gated).astype(bf16)
 
 
 def by_rows(here, body):
@@ -516,30 +517,29 @@
     def behind(x):
         return lax.ppermute(x, "row", backward)
 
-    right, normed = call(
+    right_a, right_b, normed = call(
         functools.partial(input_kernel, slot),
         "input_side",
         [chain_lengths, pair, in_gain, in_bias, w_in],
         [SMEM] + [VMEM] * 4,
-        [shape_of(block, bf16)] * 2,
+        [shape_of((short, half, hidden), bf16)] * 2 + [shape_of(block, bf16)],
         [mask],
     )
 
     hops = row_count // 2
-    groups = [[right]]
-    halves = [[(0, 0, (0, 0)), (0, short, (0, 1))]]
-    for s in range(1, hops):
-        halves.append(
-            [(0, 0, (-s, 0)), (1, short, (s, 1)), (0, short, (-s, 1)), (1, 0, (s, 0))]
-        )
-    halves.append([(0, 0, (-hops, 0)), (1, 0, (hops, 1))])
-
-    def gather(s, x, y):
-        if s == hops:
-            x, y = x[:short], y[short:]
+    steps = 2 * hops
+    groups = [[right_a, right_b]]
+    halves = [[(0, 0, (0, 0)), (1, 0, (0, 1))]]
+    for s in range(1, hops + 1):
+        halves.append([(0, 0, (-s, 0)), (1, 0, (s, 1))])
+        if s < hops:
+            halves.append([(0, 0, (-s, 1)), (1, 0, (s, 0))])
+
+    def gather(x, y):
         groups.append([ahead(x), behind(y)])
 
-    gather(1, right, right)
+    gather(right_a, right_b)
+    gather(right_b, right_a)
     left, mine_out = call(
         functools.partial(left_kernel, slot),
         "left_side",
@@ -598,9 +598,9 @@
     arrived = {0: [], 1: []}
 
     def send(s, chain, after=()):
-        picks = [2 * chain, 2 * chain + 1]
+        group, picks = 2 * s - 1 + chain, [0, 1]
         if arrived[chain]:
-            terms = scatter(s, picks, [], f32)
+            terms = scatter(group, picks, [], f32)
             x, y = call(
                 add_kernel,
                 "scatter_add",
@@ -612,7 +612,7 @@
             )
             last[:] = [x]
         else:
-            x, y = scatter(s, picks, [])
+            x, y = scatter(group, picks, [])
         arrived[chain] = [behind(x), ahead(y)]
 
     def output_side():
@@ -634,25 +634,37 @@
             microseconds=6,
         )
 
-    for s in range(hops + 1):
+    for s in range(steps):
+        if s and s + 2 < steps:
+            x, y, _ = lax.optimization_barrier((*groups[s], last[0]))
+            gather(x, y)
+        if s == steps - 1:
+            normal(s - 1)
+            send(hops - 1, 1)
         triangles(s)
-        if s:
-            add_left(s - 1)
-        normal(s)
-        if s == hops - 1:
-            send(s, 1)
-        elif s < hops:
-            x, y, _ = lax.optimization_barrier((*groups[s + 1], last[0]))
-            gather(s + 2, x, y)
+        if 0 < s < steps - 1:
+            normal(s - 1)
+    waiting = list(range(steps))
+
+    def add_lefts(count):
+        for _ in range(min(count, len(waiting))):
+            add_left(waiting.pop(0))
+
+    add_lefts(1)
+    normal(steps - 1)
     send(hops, 0)
-    add_left(hops)
+    add_lefts(1)
     send(hops - 2, 1)
     for s in range(hops - 1, 0, -1):
+        add_lefts(1)
         if s == 1:
             own_a, own_b = scatter(0, [0, 1], [], f32)
+            add_lefts(2)
         send(s, 0, arrived[1] if s == 1 else ())
         if s > 2:
+            add_lefts(1)
             send(s - 2, 1)
+    add_lefts(steps)
     update, gradient, early = output_side()
     arrived1, arrived2 = arrived[0], [arrived[1][1], arrived[1][0]]
 
@@ -667,11 +679,17 @@
         [mask, pltpu.VMEM((channels, 2 * hidden), f32)],
     )
     mine = add(keep, swap_col(give))
+
+    def from_row(apart):
+        return lax.ppermute(mine, "row", [(r, r ^ apart) for r in range(row_count)])
+
     step = 1
+    if row_count % 4 == 0:
+        one, two, three = [from_row(apart).astype(f32) for apart in (1, 2, 3)]
+        mine = ((mine.astype(f32) + one) + (two + three)).astype(bf16)
+        step = 4
     while step < row_count:
-        mine = add(
-            mine, lax.ppermute(mine, "row", [(r, r ^ step) for r in range(row_count)])
-        )
+        mine = add(mine, from_row(step))
         step *= 2
     (pair_gradient,) = call(
         pair_gradient_kernel,

time: 132 us -> 124 us (0.939)
  waiting for transfers between devices: 38.8 us -> 17.9 us
  starting transfers between devices: 30.3 us -> 40.6 us
  Pallas kernels: 58 us -> 60.9 us
    ppermute x11 -> x14, waiting for transfers between devices: 16.7 us -> 4.68 us  [behind(): return lax.ppermute(x, 'row', backward)]
    ppermute x11 -> x14, starting transfers between devices: 12.1 us -> 18.8 us  [ahead(): return lax.ppermute(x, 'row', forward)]
    ppermute x11 -> x14, waiting for transfers between devices: 10.6 us -> 4.39 us  [ahead(): return lax.ppermute(x, 'row', forward)]
    pallas_call x34 -> x43, Pallas kernels: 58 us -> 60.9 us  [call(): pl.pallas_call(body, out_shape=list(outs), in_specs=list(specs) + [ANY] *...]
    ppermute x3 -> x4, starting transfers between devices: 4.09 us -> 6.74 us  [from_row(): return lax.ppermute(mine, 'row', [(r, r ^ apart) for r in range(row_count)])]
    ppermute x3 -> x4, waiting for transfers between devices: 7.11 us -> 5.64 us  [from_row(): return lax.ppermute(mine, 'row', [(r, r ^ apart) for r in range(row_count)])]
    ppermute x8 -> x11, waiting for transfers between devices: 4.44 us -> 3.23 us  [swap_col(): return lax.ppermute(x, 'col', [(0, 1), (1, 0)])]
    ppermute x11 -> x14, starting transfers between devices: 13 us -> 13.2 us  [behind(): return lax.ppermute(x, 'row', backward)]
  transfers between devices with their start and end apart: 33 -> 43, of which waited for: 21 -> 14; matrix products, arithmetic and copies ran while one was open for 0% -> 0% of each run, Pallas kernels for 36% -> 42%
where the time goes in v2:
time: 124 us
  Pallas kernels  60.9 us (49%)
  starting transfers between devices  40.6 us (33%)
  waiting for transfers between devices  17.9 us (14%)
  local copies, waits for them, and re-layouts  3.28 us (3%)
    pallas_call x43, Pallas kernels, call(): pl.pallas_call(body, out_shape=list(outs), in_specs=list(specs) + [ANY] *...  60.9 us
    ppermute x14, starting transfers between devices, ahead(): return lax.ppermute(x, 'row', forward)  18.8 us
    ppermute x14, starting transfers between devices, behind(): return lax.ppermute(x, 'row', backward)  13.2 us
    ppermute x4, starting transfers between devices, from_row(): return lax.ppermute(mine, 'row', [(r, r ^ apart) for r in range(row_count)])  6.74 us
    ppermute x4, waiting for transfers between devices, from_row(): return lax.ppermute(mine, 'row', [(r, r ^ apart) for r in range(row_count)])  5.64 us
    ppermute x14, waiting for transfers between devices, behind(): return lax.ppermute(x, 'row', backward)  4.68 us
    ppermute x14, waiting for transfers between devices, ahead(): return lax.ppermute(x, 'row', forward)  4.39 us
    unnamed x22, local copies, waits for them, and re-layouts  3.28 us
  transfers between devices with their start and end apart: 43, of which 14 were waited for; matrix products, arithmetic and copies ran while one was open for 0% of the time, Pallas kernels for 42%

profile of v2, /device:TPU:0, one launch (start us, length us, event | category | flops | bytes accessed | tf_op | source)
XLA Modules:
  0.0 124.0 jit_solution(15982457679617400058)
XLA Ops:
  1.3 0.9 copy-done.1
  2.2 1.0 copy-done.3
  3.3 1.5 %input_side.1 = (bf16[11,88,128]{2,1,0:T(8,128)(2,1)S(1)}, bf16[11,88,128]{2,1,0:T(8,128)(2,1)S(1)}, bf16[22,88,128]{2,1,0:T(8,128)(2,1)S(1)}) custom-call(s32[8]{0:T(128)S(1)} %copy-done.5, bf16[22,88,128]{2,1,0:T(8,128)(2,1)S(1)} %copy-done.3, f32[1,128]{1,0:T(1,128)S(1)} %bitcast.21, f32[1,128]{1,0:T(1,128)S(1)} %bitcast.20, bf16[128,640]{1,0:T(8,128)(2,1)S(1)} %copy-done.1), custom_call_target="tpu_custom_call" | custom-call | flops 1024 | bytes 1024 | tf_op jit(solution)/shard_map/input_side/pallas_call | solution.py:93
  4.8 1.4 %left_side.1 = (bf16[22,88,128]{2,1,0:T(8,128)(2,1)S(1)}, bf16[8,22,16,128]{3,2,1,0:T(8,128)(2,1)S(1)}) custom-call(s32[8]{0:T(128)S(1)} %copy-done.5, bf16[22,88,128]{2,1,0:T(8,128)(2,1)S(1)} %get-tuple-element.71.refs_1_, bf16[22,88,128]{2,1,0:T(8,128)(2,1)S(1)} %copy-done.10, bf16[128,640]{1,0:T(8,128)(2,1)S(1)} %copy-done.2), custom_call_target="tpu_custom_call" | custom-call | flops 4400001024 | bytes 1024 | tf_op jit(solution)/shard_map/left_side/pallas_call | solution.py:93
  6.7 2.6 %collective-permute-start = (bf16[11,88,128]{2,1,0:T(8,128)(2,1)S(1)}, bf16[11,88,128]{2,1,0:T(8,128)(2,1)S(1)}, u32[]{:S(2)}, u32[]{:S(2)}) collective-permute-start(bf16[11,88,128]{2,1,0:T(8,128)(2,1)S(1)} %get-tuple-element.73.refs_2_.refs_1_), channel_id=1, source_target_pairs={{0,4},{4,8},{8,12},{12,14},{14,10},{10,6},{6,2},{2,0},{1,5},{5,9},... | collective-permute-start | bytes 743432 | tf_op jit(solution)/shard_map/ppermute | solution.py:515
  9.4 2.7 %triangle.8.refs_4_.refs_0_ = bf16[2,22,16,128]{3,2,1,0:T(8,128)(2,1)S(1)} custom-call(s32[8]{0:T(128)S(1)} %copy-done.5, bf16[22,88,128]{2,1,0:T(8,128)(2,1)S(1)} %get-tuple-element.72.refs_1_.refs_4_, bf16[11,88,128]{2,1,0:T(8,128)(2,1)S(1)} %get-tuple-element.73.refs_2_.refs_1_, bf16[11,88,128]{2,1,0:T(8,128)(2,1)S(1)} %get-tuple-element.74.refs_3_.refs_2_, ...), custom_call_target="tpu_custom_call" | custom-call | flops 1024 | bytes 1024 | tf_op jit(solution)/shard_map/triangle/pallas_call | solution.py:93
  12.3 1.2 collective-permute-start.7
  13.4 2.4 %collective-permute-done.refs_2_.refs_1_ = bf16[11,88,128]{2,1,0:T(8,128)(2,1)S(1)} collective-permute-done((bf16[11,88,128]{2,1,0:T(8,128)(2,1)S(1)}, bf16[11,88,128]{2,1,0:T(8,128)(2,1)S(1)}, u32[]{:S(2)}, u32[]{:S(2)}) %collective-permute-start) | collective-permute-done | bytes 247840 | tf_op jit(solution)/shard_map/ppermute | solution.py:515
  15.9 1.8 %collective-permute-start.6 = (bf16[11,88,128]{2,1,0:T(8,128)(2,1)S(1)}, bf16[11,88,128]{2,1,0:T(8,128)(2,1)S(1)}, u32[]{:S(2)}, u32[]{:S(2)}) collective-permute-start(bf16[11,88,128]{2,1,0:T(8,128)(2,1)S(1)} %get-tuple-element.74.refs_3_.refs_2_), channel_id=1, source_target_pairs={{0,4},{4,8},{8,12},{12,14},{14,10},{10,6},{6,2},{2,0},{1,5},{5,9},... | collective-permute-start | bytes 743432 | tf_op jit(solution)/shard_map/ppermute | solution.py:515
  18.2 2.0 %triangle.9.refs_7_.refs_0_ = bf16[2,22,16,128]{3,2,1,0:T(8,128)(2,1)S(1)} custom-call(s32[8]{0:T(128)S(1)} %copy-done.5, bf16[22,88,128]{2,1,0:T(8,128)(2,1)S(1)} %get-tuple-element.72.refs_1_.refs_4_, bf16[11,88,128]{2,1,0:T(8,128)(2,1)S(1)} %collective-permute-done.refs_2_.refs_1_, bf16[11,88,128]{2,1,0:T(8,128)(2,1)S(1)} %collective-permute-done.1.refs_3_.refs_2_, ...), custom_call_target="tpu_custom_call" | custom-call | flops 1024 | bytes 1024 | tf_op jit(solution)/shard_map/triangle/pallas_call | solution.py:93
  20.3 2.3 %collective-permute-start.2 = (bf16[11,88,128]{2,1,0:T(8,128)(2,1)S(1)}, bf16[11,88,128]{2,1,0:T(8,128)(2,1)S(1)}, u32[]{:S(2)}, u32[]{:S(2)}) collective-permute-start(bf16[11,88,128]{2,1,0:T(8,128)(2,1)S(1)} %collective-permute-done.refs_2_.refs_1_), channel_id=1, source_target_pairs={{0,4},{4,8},{8,12},{12,14},{14,10},{10,6},{6,2},{2,0},{1,5},{5,9},... | collective-permute-start | bytes 743432 | tf_op jit(solution)/shard_map/ppermute | solution.py:515
  22.6 0.6 copy-done.6
  23.9 2.1 %collective-permute-start.12 = (bf16[11,88,128]{2,1,0:T(8,128)(2,1)S(1)}, bf16[11,88,128]{2,1,0:T(8,128)(2,1)S(1)}, u32[]{:S(2)}, u32[]{:S(2)}) collective-permute-start(bf16[11,88,128]{2,1,0:T(8,128)(2,1)S(1)} %collective-permute-done.6.refs_2_.refs_1_), channel_id=1, source_target_pairs={{0,4},{4,8},{8,12},{12,14},{14,10},{10,6},{6,2},{2,0},{1,5},{5,9},... | collective-permute-start | bytes 743432 | tf_op jit(solution)/shard_map/ppermute | solution.py:515
  26.3 2.0 %triangle.10.refs_7_.refs_0_ = bf16[2,22,16,128]{3,2,1,0:T(8,128)(2,1)S(1)} custom-call(s32[8]{0:T(128)S(1)} %copy-done.5, bf16[22,88,128]{2,1,0:T(8,128)(2,1)S(1)} %get-tuple-element.72.refs_1_.refs_4_, bf16[11,88,128]{2,1,0:T(8,128)(2,1)S(1)} %collective-permute-done.6.refs_2_.refs_1_, bf16[11,88,128]{2,1,0:T(8,128)(2,1)S(1)} %collective-permute-done.7.refs_3_.refs_2_, ...), custom_call_target="tpu_custom_call" | custom-call | flops 1024 | bytes 1024 | tf_op jit(solution)/shard_map/triangle/pallas_call | solution.py:93
  29.2 2.2 %collective-permute-done.3.refs_3_.refs_2_ = bf16[11,88,128]{2,1,0:T(8,128)(2,1)S(1)} collective-permute-done((bf16[11,88,128]{2,1,0:T(8,128)(2,1)S(1)}, bf16[11,88,128]{2,1,0:T(8,128)(2,1)S(1)}, u32[]{:S(2)}, u32[]{:S(2)}) %collective-permute-start.3) | collective-permute-done | bytes 247840 | tf_op jit(solution)/shard_map/ppermute | solution.py:518
  31.4 2.7 %triangle.11.refs_7_.refs_0_ = bf16[2,22,16,128]{3,2,1,0:T(8,128)(2,1)S(1)} custom-call(s32[8]{0:T(128)S(1)} %copy-done.5, bf16[22,88,128]{2,1,0:T(8,128)(2,1)S(1)} %get-tuple-element.72.refs_1_.refs_4_, bf16[11,88,128]{2,1,0:T(8,128)(2,1)S(1)} %collective-permute-done.2.refs_2_.refs_1_, bf16[11,88,128]{2,1,0:T(8,128)(2,1)S(1)} %collective-permute-done.3.refs_3_.refs_2_, ...), custom_call_target="tpu_custom_call" | custom-call | flops 1024 | bytes 1024 | tf_op jit(solution)/shard_map/triangle/pallas_call | solution.py:93
  34.2 1.3 %collective-permute-start.9 = (bf16[11,88,128]{2,1,0:T(8,128)(2,1)S(1)}, bf16[11,88,128]{2,1,0:T(8,128)(2,1)S(1)}, u32[]{:S(2)}, u32[]{:S(2)}) collective-permute-start(bf16[11,88,128]{2,1,0:T(8,128)(2,1)S(1)} %collective-permute-done.2.refs_2_.refs_1_), channel_id=1, source_target_pairs={{0,4},{4,8},{8,12},{12,14},{14,10},{10,6},{6,2},{2,0},{1,5},{5,9},... | collective-permute-start | bytes 743432 | tf_op jit(solution)/shard_map/ppermute | solution.py:515
  35.5 0.8 collective-permute-start.10
  36.9 1.3 %collective-permute-start.17 = (bf16[11,88,128]{2,1,0:T(8,128)(2,1)S(1)}, bf16[11,88,128]{2,1,0:T(8,128)(2,1)S(1)}, u32[]{:S(2)}, u32[]{:S(2)}) collective-permute-start(bf16[11,88,128]{2,1,0:T(8,128)(2,1)S(1)} %collective-permute-done.12.refs_2_.refs_1_), channel_id=1, source_target_pairs={{0,4},{4,8},{8,12},{12,14},{14,10},{10,6},{6,2},{2,0},{1,5},{5,9},... | collective-permute-start | bytes 743432 | tf_op jit(solution)/shard_map/ppermute | solution.py:515
  38.2 0.8 collective-permute-start.18
  39.0 1.8 %triangle.12.refs_7_.refs_0_ = bf16[2,22,16,128]{3,2,1,0:T(8,128)(2,1)S(1)} custom-call(s32[8]{0:T(128)S(1)} %copy-done.5, bf16[22,88,128]{2,1,0:T(8,128)(2,1)S(1)} %get-tuple-element.72.refs_1_.refs_4_, bf16[11,88,128]{2,1,0:T(8,128)(2,1)S(1)} %collective-permute-done.12.refs_2_.refs_1_, bf16[11,88,128]{2,1,0:T(8,128)(2,1)S(1)} %collective-permute-done.13.refs_3_.refs_2_, ...), custom_call_target="tpu_custom_call" | custom-call | flops 1024 | bytes 1024 | tf_op jit(solution)/shard_map/triangle/pallas_call | solution.py:93
  41.5 1.6 %collective-permute-done.9.refs_2_.refs_1_ = bf16[11,88,128]{2,1,0:T(8,128)(2,1)S(1)} collective-permute-done((bf16[11,88,128]{2,1,0:T(8,128)(2,1)S(1)}, bf16[11,88,128]{2,1,0:T(8,128)(2,1)S(1)}, u32[]{:S(2)}, u32[]{:S(2)}) %collective-permute-start.9) | collective-permute-done | bytes 247840 | tf_op jit(solution)/shard_map/ppermute | solution.py:515
  43.1 1.3 %collective-permute-done.10.refs_3_.refs_2_ = bf16[11,88,128]{2,1,0:T(8,128)(2,1)S(1)} collective-permute-done((bf16[11,88,128]{2,1,0:T(8,128)(2,1)S(1)}, bf16[11,88,128]{2,1,0:T(8,128)(2,1)S(1)}, u32[]{:S(2)}, u32[]{:S(2)}) %collective-permute-start.10) | collective-permute-done | bytes 247840 | tf_op jit(solution)/shard_map/ppermute | solution.py:518
  44.4 0.8 collective-permute-start.15
  45.2 1.2 collective-permute-start.16
  46.4 2.4 %triangle.13.refs_7_.refs_0_ = bf16[2,22,16,128]{3,2,1,0:T(8,128)(2,1)S(1)} custom-call(s32[8]{0:T(128)S(1)} %copy-done.5, bf16[22,88,128]{2,1,0:T(8,128)(2,1)S(1)} %get-tuple-element.72.refs_1_.refs_4_, bf16[11,88,128]{2,1,0:T(8,128)(2,1)S(1)} %collective-permute-done.9.refs_2_.refs_1_, bf16[11,88,128]{2,1,0:T(8,128)(2,1)S(1)} %collective-permute-done.10.refs_3_.refs_2_, ...), custom_call_target="tpu_custom_call" | custom-call | flops 1024 | bytes 1024 | tf_op jit(solution)/shard_map/triangle/pallas_call | solution.py:93
  49.7 1.7 %triangle.14.refs_7_.refs_0_ = bf16[2,22,16,128]{3,2,1,0:T(8,128)(2,1)S(1)} custom-call(s32[8]{0:T(128)S(1)} %copy-done.5, bf16[22,88,128]{2,1,0:T(8,128)(2,1)S(1)} %get-tuple-element.72.refs_1_.refs_4_, bf16[11,88,128]{2,1,0:T(8,128)(2,1)S(1)} %collective-permute-done.17.refs_2_.refs_1_, bf16[11,88,128]{2,1,0:T(8,128)(2,1)S(1)} %collective-permute-done.18.refs_3_.refs_2_, ...), custom_call_target="tpu_custom_call" | custom-call | flops 1024 | bytes 1024 | tf_op jit(solution)/shard_map/triangle/pallas_call | solution.py:93
  52.2 0.6 collective-permute-done.20.refs_1_
  53.4 1.2 scatter_hop.8
  54.6 2.4 %triangle.15.refs_3_.refs_0_ = bf16[2,22,16,128]{3,2,1,0:T(8,128)(2,1)S(1)} custom-call(s32[8]{0:T(128)S(1)} %copy-done.5, bf16[22,88,128]{2,1,0:T(8,128)(2,1)S(1)} %get-tuple-element.72.refs_1_.refs_4_, bf16[11,88,128]{2,1,0:T(8,128)(2,1)S(1)} %collective-permute-done.15.refs_2_.refs_1_, bf16[11,88,128]{2,1,0:T(8,128)(2,1)S(1)} %collective-permute-done.16.refs_3_.refs_2_, ...), custom_call_target="tpu_custom_call" | custom-call | flops 1024 | bytes 1024 | tf_op jit(solution)/shard_map/triangle/pallas_call | solution.py:93
  57.8 1.8 %collective-permute-start.23 = (bf16[11,88,128]{2,1,0:T(8,128)(2,1)S(1)}, bf16[11,88,128]{2,1,0:T(8,128)(2,1)S(1)}, u32[]{:S(2)}, u32[]{:S(2)}) collective-permute-start(bf16[11,88,128]{2,1,0:T(8,128)(2,1)S(1)} %get-tuple-element.93.refs_4_), channel_id=1, source_target_pairs={{0,2},{4,0},{8,4},{12,8},{14,12},{10,14},{6,10},{2,6},{1,3},{5,1},... | collective-permute-start | bytes 743432 | tf_op jit(solution)/shard_map/ppermute | solution.py:518
  59.6 1.1 left_gradient.8.refs_7_.refs_3_
  61.3 1.5 %scatter_hop.9 = (bf16[11,88,128]{2,1,0:T(8,128)(2,1)S(1)}, bf16[11,88,128]{2,1,0:T(8,128)(2,1)S(1)}) custom-call(s32[8]{0:T(128)S(1)} %copy-done.5, bf16[22,88,128]{2,1,0:T(8,128)(2,1)S(1)} %get-tuple-element.72.refs_1_.refs_4_, bf16[2,22,16,128]{3,2,1,0:T(8,128)(2,1)S(1)} %get-tuple-element.94.refs_2_.refs_3_.refs_4_.refs_0_, ...), custom_call_target="tpu_custom_call" | custom-call | flops 1024 | bytes 1024 | tf_op jit(solution)/shard_map/scatter_hop/pallas_call | solution.py:93
  62.8 2.3 %collective-permute-start.25 = (bf16[11,88,128]{2,1,0:T(8,128)(2,1)S(1)}, bf16[11,88,128]{2,1,0:T(8,128)(2,1)S(1)}, u32[]{:S(2)}, u32[]{:S(2)}) collective-permute-start(bf16[11,88,128]{2,1,0:T(8,128)(2,1)S(1)} %get-tuple-element.95.refs_4_), channel_id=1, source_target_pairs={{0,2},{4,0},{8,4},{12,8},{14,12},{10,14},{6,10},{2,6},{1,3},{5,1},... | collective-permute-start | bytes 743432 | tf_op jit(solution)/shard_map/ppermute | solution.py:518
  65.1 1.2 left_gradient.9.refs_4_.refs_3_
  66.3 1.5 %scatter_hop.10 = (f32[11,88,128]{2,1,0:T(8,128)S(1)}, f32[11,88,128]{2,1,0:T(8,128)S(1)}) custom-call(s32[8]{0:T(128)S(1)} %copy-done.5, bf16[22,88,128]{2,1,0:T(8,128)(2,1)S(1)} %get-tuple-element.72.refs_1_.refs_4_, bf16[2,22,16,128]{3,2,1,0:T(8,128)(2,1)S(1)} %get-tuple-element.90.refs_4_.refs_2_.refs_3_.refs_0_, ...), custom_call_target="tpu_custom_call" | custom-call | flops 1024 | bytes 1024 | tf_op jit(solution)/shard_map/scatter_hop/pallas_call | solution.py:93
  68.0 0.8 collective-permute-start.28
  68.8 1.2 left_gradient.10.refs_4_.refs_3_
  70.0 1.3 %collective-permute-start.27 = (bf16[11,88,128]{2,1,0:T(8,128)(2,1)S(1)}, bf16[11,88,128]{2,1,0:T(8,128)(2,1)S(1)}, u32[]{:S(2)}, u32[]{:S(2)}) collective-permute-start(bf16[11,88,128]{2,1,0:T(8,128)(2,1)S(1)} %get-tuple-element.99.refs_4_), channel_id=1, source_target_pairs={{0,2},{4,0},{8,4},{12,8},{14,12},{10,14},{6,10},{2,6},{1,3},{5,1},... | collective-permute-start | bytes 743432 | tf_op jit(solution)/shard_map/ppermute | solution.py:518
  71.3 1.7 %scatter_hop.11 = (f32[11,88,128]{2,1,0:T(8,128)S(1)}, f32[11,88,128]{2,1,0:T(8,128)S(1)}) custom-call(s32[8]{0:T(128)S(1)} %copy-done.5, bf16[22,88,128]{2,1,0:T(8,128)(2,1)S(1)} %get-tuple-element.72.refs_1_.refs_4_, bf16[2,22,16,128]{3,2,1,0:T(8,128)(2,1)S(1)} %get-tuple-element.91.refs_7_.refs_2_.refs_3_.refs_0_, ...), custom_call_target="tpu_custom_call" | custom-call | flops 1024 | bytes 1024 | tf_op jit(solution)/shard_map/scatter_hop/pallas_call | solution.py:93
  73.7 1.5 %collective-permute-start.29 = (bf16[11,88,128]{2,1,0:T(8,128)(2,1)S(1)}, bf16[11,88,128]{2,1,0:T(8,128)(2,1)S(1)}, u32[]{:S(2)}, u32[]{:S(2)}) collective-permute-start(bf16[11,88,128]{2,1,0:T(8,128)(2,1)S(1)} %get-tuple-element.103.refs_4_), channel_id=1, source_target_pairs={{0,2},{4,0},{8,4},{12,8},{14,12},{10,14},{6,10},{2,6},{1,3},{5,1},... | collective-permute-start | bytes 743432 | tf_op jit(solution)/shard_map/ppermute | solution.py:518
  75.2 1.2 left_gradient.11.refs_4_.refs_3_
  76.4 1.5 %scatter_hop.12 = (f32[11,88,128]{2,1,0:T(8,128)S(1)}, f32[11,88,128]{2,1,0:T(8,128)S(1)}) custom-call(s32[8]{0:T(128)S(1)} %copy-done.5, bf16[22,88,128]{2,1,0:T(8,128)(2,1)S(1)} %get-tuple-element.72.refs_1_.refs_4_, bf16[2,22,16,128]{3,2,1,0:T(8,128)(2,1)S(1)} %get-tuple-element.84.refs_4_.refs_0_.refs_2_.refs_3_, ...), custom_call_target="tpu_custom_call" | custom-call | flops 1024 | bytes 1024 | tf_op jit(solution)/shard_map/scatter_hop/pallas_call | solution.py:93
  78.4 1.9 %collective-permute-start.33 = (bf16[11,88,128]{2,1,0:T(8,128)(2,1)S(1)}, bf16[11,88,128]{2,1,0:T(8,128)(2,1)S(1)}, u32[]{:S(2)}, u32[]{:S(2)}) collective-permute-start(bf16[11,88,128]{2,1,0:T(8,128)(2,1)S(1)} %get-tuple-element.107.refs_4_), channel_id=1, source_target_pairs={{0,2},{4,0},{8,4},{12,8},{14,12},{10,14},{6,10},{2,6},{1,3},{5,1},... | collective-permute-start | bytes 743432 | tf_op jit(solution)/shard_map/ppermute | solution.py:518
  80.3 1.2 left_gradient.12.refs_4_.refs_3_
  81.9 1.7 %scatter_hop.13 = (f32[11,88,128]{2,1,0:T(8,128)S(1)}, f32[11,88,128]{2,1,0:T(8,128)S(1)}) custom-call(s32[8]{0:T(128)S(1)} %copy-done.5, bf16[22,88,128]{2,1,0:T(8,128)(2,1)S(1)} %get-tuple-element.72.refs_1_.refs_4_, bf16[2,22,16,128]{3,2,1,0:T(8,128)(2,1)S(1)} %get-tuple-element.85.refs_4_.refs_0_.refs_2_.refs_3_, ...), custom_call_target="tpu_custom_call" | custom-call | flops 1024 | bytes 1024 | tf_op jit(solution)/shard_map/scatter_hop/pallas_call | solution.py:93
  83.7 2.2 %collective-permute-start.32 = (bf16[11,88,128]{2,1,0:T(8,128)(2,1)S(1)}, bf16[11,88,128]{2,1,0:T(8,128)(2,1)S(1)}, u32[]{:S(2)}, u32[]{:S(2)}) collective-permute-start(bf16[11,88,128]{2,1,0:T(8,128)(2,1)S(1)} %get-tuple-element.123), channel_id=1, source_target_pairs={{0,4},{4,8},{8,12},{12,14},{14,10},{10,6},{6,2},{2,0},{1,5},{5,9},... | collective-permute-start | bytes 743432 | tf_op jit(solution)/shard_map/ppermute | solution.py:515
  86.0 1.2 left_gradient.13.refs_4_.refs_3_
  87.2 1.7 %scatter_hop.14 = (f32[11,88,128]{2,1,0:T(8,128)S(1)}, f32[11,88,128]{2,1,0:T(8,128)S(1)}) custom-call(s32[8]{0:T(128)S(1)} %copy-done.5, bf16[22,88,128]{2,1,0:T(8,128)(2,1)S(1)} %get-tuple-element.72.refs_1_.refs_4_, bf16[2,22,16,128]{3,2,1,0:T(8,128)(2,1)S(1)} %get-tuple-element.78.refs_4_.refs_0_.refs_2_.refs_3_, ...), custom_call_target="tpu_custom_call" | custom-call | flops 1024 | bytes 1024 | tf_op jit(solution)/shard_map/scatter_hop/pallas_call | solution.py:93
  88.9 1.2 left_gradient.14.refs_3_.refs_4_
  90.1 1.2 left_gradient.15.refs_4_.refs_3_
  91.2 1.7 %scatter_hop.15 = (f32[11,88,128]{2,1,0:T(8,128)S(1)}, f32[11,88,128]{2,1,0:T(8,128)S(1)}) custom-call(s32[8]{0:T(128)S(1)} %copy-done.5, bf16[22,88,128]{2,1,0:T(8,128)(2,1)S(1)} %get-tuple-element.72.refs_1_.refs_4_, bf16[2,22,16,128]{3,2,1,0:T(8,128)(2,1)S(1)} %get-tuple-element.79.refs_4_.refs_0_.refs_2_.refs_3_, ...), custom_call_target="tpu_custom_call" | custom-call | flops 1024 | bytes 1024 | tf_op jit(solution)/shard_map/scatter_hop/pallas_call | solution.py:93
  93.1 2.1 %collective-permute-start.36 = (bf16[11,88,128]{2,1,0:T(8,128)(2,1)S(1)}, bf16[11,88,128]{2,1,0:T(8,128)(2,1)S(1)}, u32[]{:S(2)}, u32[]{:S(2)}) collective-permute-start(bf16[11,88,128]{2,1,0:T(8,128)(2,1)S(1)} %get-tuple-element.129), channel_id=1, source_target_pairs={{0,4},{4,8},{8,12},{12,14},{14,10},{10,6},{6,2},{2,0},{1,5},{5,9},... | collective-permute-start | bytes 743432 | tf_op jit(solution)/shard_map/ppermute | solution.py:515
  95.2 6.6 %output_side.1 = (bf16[22,88,128]{2,1,0:T(8,128)(2,1)}, f32[22,88,128]{2,1,0:T(8,128)S(1)}, f32[128,512]{1,0:T(8,128)S(1)}) custom-call(s32[8]{0:T(128)S(1)} %copy-done.5, bf16[22,88,128]{2,1,0:T(8,128)(2,1)S(1)} %get-tuple-element.71.refs_1_, bf16[22,88,128]{2,1,0:T(8,128)(2,1)S(1)} %copy-done.10, f32[22,88,128]{2,1,0:T(8,128)S(1)} %left_gradient.15.refs_4_.refs_3_, ...), custom_call_target="tpu_custom_call" | custom-call | flops 6600001024 | bytes 1024 | tf_op jit(solution)/shard_map/output_side/pallas_call | solution.py:93
  101.8 2.0 %right_gradient.1 = (bf16[22,88,256]{2,1,0:T(8,128)(2,1)S(1)}, bf16[64,768]{1,0:T(8,128)(2,1)S(1)}, bf16[64,768]{1,0:T(8,128)(2,1)S(1)}) custom-call(s32[8]{0:T(128)S(1)} %copy-done.5, bf16[22,88,128]{2,1,0:T(8,128)(2,1)S(1)} %get-tuple-element.71.refs_1_, bf16[128,640]{1,0:T(8,128)(2,1)S(1)} %copy-done.2, f32[128,512]{1,0:T(8,128)S(1)} %get-tuple-element.127.refs_3_, ...), custom_call_target="tpu_custom_call" | custom-call | flops 1024 | bytes 1024 | tf_op jit(solution)/shard_map/right_gradient/pallas_call | solution.py:93
  104.0 1.3 %collective-permute-done.37 = bf16[64,768]{1,0:T(8,128)(2,1)S(1)} collective-permute-done((bf16[64,768]{1,0:T(8,128)(2,1)S(1)}, bf16[64,768]{1,0:T(8,128)(2,1)S(1)}, u32[]{:S(2)}, u32[]{:S(2)}) %collective-permute-start.37) | collective-permute-done | bytes 98336 | tf_op jit(solution)/shard_map/ppermute | solution.py:77
  105.3 2.7 %collective-permute-start.40 = (bf16[64,768]{1,0:T(8,128)(2,1)S(1)}, bf16[64,768]{1,0:T(8,128)(2,1)S(1)}, u32[]{:S(2)}, u32[]{:S(2)}) collective-permute-start(bf16[64,768]{1,0:T(8,128)(2,1)S(1)} %add_convert_fusion.2), channel_id=1, source_target_pairs={{0,6},{2,4},{4,2},{6,0},{8,14},{10,12},{12,10},{14,8},{1,7},{3,5},... | collective-permute-start | bytes 294920 | tf_op jit(solution)/shard_map/ppermute | solution.py:684
  108.8 2.7 %collective-permute-done.40 = bf16[64,768]{1,0:T(8,128)(2,1)S(1)} collective-permute-done((bf16[64,768]{1,0:T(8,128)(2,1)S(1)}, bf16[64,768]{1,0:T(8,128)(2,1)S(1)}, u32[]{:S(2)}, u32[]{:S(2)}) %collective-permute-start.40) | collective-permute-done | bytes 98336 | tf_op jit(solution)/shard_map/ppermute | solution.py:684
  111.5 1.9 %collective-permute-done.39 = bf16[64,768]{1,0:T(8,128)(2,1)S(1)} collective-permute-done((bf16[64,768]{1,0:T(8,128)(2,1)S(1)}, bf16[64,768]{1,0:T(8,128)(2,1)S(1)}, u32[]{:S(2)}, u32[]{:S(2)}) %collective-permute-start.39) | collective-permute-done | bytes 98336 | tf_op jit(solution)/shard_map/ppermute | solution.py:684
  113.5 3.2 %collective-permute-start.41 = (bf16[64,768]{1,0:T(8,128)(2,1)S(1)}, bf16[64,768]{1,0:T(8,128)(2,1)S(1)}, u32[]{:S(2)}, u32[]{:S(2)}) collective-permute-start(bf16[64,768]{1,0:T(8,128)(2,1)S(1)} %add_convert_fusion.1), channel_id=1, source_target_pairs={{0,8},{2,10},{4,12},{6,14},{8,0},{10,2},{12,4},{14,6},{1,9},{3,11}... | collective-permute-start | bytes 294920 | tf_op jit(solution)/shard_map/ppermute | solution.py:684
  116.7 4.1 %pair_gradient.1 = bf16[22,88,128]{2,1,0:T(8,128)(2,1)} custom-call(bf16[22,88,128]{2,1,0:T(8,128)(2,1)S(1)} %copy-done.4, bf16[22,88,256]{2,1,0:T(8,128)(2,1)S(1)} %get-tuple-element.132.refs_1_, f32[1,128]{1,0:T(1,128)S(1)} %bitcast.22, bf16[128,640]{1,0:T(8,128)(2,1)S(1)} %copy-done.2, f32[22,88,128]{2,1,0:T(8,128)S(1)} %get-tuple-element.133.refs_4_), custom_call_target="tpu_custom_call" | custom-call | flops 3300001024 | bytes 1024 | tf_op jit(solution)/shard_map/pair_gradient/pallas_call | solution.py:93
  120.8 1.0 collective-permute-done.41
  121.9 1.3 %collective-permute-done.42.refs_1_ = bf16[64,768]{1,0:T(8,128)(2,1)S(1)} collective-permute-done((bf16[64,768]{1,0:T(8,128)(2,1)S(1)}, bf16[64,768]{1,0:T(8,128)(2,1)S(1)}, u32[]{:S(2)}, u32[]{:S(2)}) %collective-permute-start.42) | collective-permute-done | bytes 98336 | tf_op jit(solution)/shard_map/ppermute | solution.py:77
  123.2 0.8 weight_gradients.1
  (90 shorter events, 11.8 us)
Async XLA Ops:
  0.6 0.7 copy-start.5
  0.6 0.7 copy-start.8
  0.7 0.7 copy-start.9
  1.3 0.9 copy-start.1
  2.2 1.0 copy-start.3
  3.3 1.5 %copy-start.2 = (bf16[128,640]{1,0:T(8,128)(2,1)S(1)}, bf16[128,640]{1,0:T(8,128)(2,1)}, u32[]{:S(2)}) copy-start(bf16[128,640]{1,0:T(8,128)(2,1)} %refs_3_.3) | copy-start | bytes 491524
  3.3 1.5 %copy-start.10 = (bf16[22,88,128]{2,1,0:T(8,128)(2,1)S(1)}, bf16[22,88,128]{2,1,0:T(8,128)(2,1)}, u32[]{:S(2)}) copy-start(bf16[22,88,128]{2,1,0:T(8,128)(2,1)} %refs_2_.4) | copy-start | bytes 1486852
  6.2 16.4 %collective-permute-start.5 = (bf16[8,22,16,128]{3,2,1,0:T(8,128)(2,1)S(1)}, bf16[8,22,16,128]{3,2,1,0:T(8,128)(2,1)S(1)}, u32[]{:S(2)}, u32[]{:S(2)}) collective-permute-start(bf16[8,22,16,128]{3,2,1,0:T(8,128)(2,1)S(1)} %get-tuple-element.77.refs_2_.refs_6_), channel_id=1, source_target_pairs={{0,1},{1,0},{2,3},{3,2},{4,5},{5,4},{6,7},{7,6},{8,9},{9,8},{10,11... | collective-permute-start | bytes 2162696 | tf_op jit(solution)/shard_map/ppermute | solution.py:77
  6.7 9.2 %collective-permute-start = (bf16[11,88,128]{2,1,0:T(8,128)(2,1)S(1)}, bf16[11,88,128]{2,1,0:T(8,128)(2,1)S(1)}, u32[]{:S(2)}, u32[]{:S(2)}) collective-permute-start(bf16[11,88,128]{2,1,0:T(8,128)(2,1)S(1)} %get-tuple-element.73.refs_2_.refs_1_), channel_id=1, source_target_pairs={{0,4},{4,8},{8,12},{12,14},{14,10},{10,6},{6,2},{2,0},{1,5},{5,9},... | collective-permute-start | bytes 743432 | tf_op jit(solution)/shard_map/ppermute | solution.py:515
  9.3 8.8 %collective-permute-start.1 = (bf16[11,88,128]{2,1,0:T(8,128)(2,1)S(1)}, bf16[11,88,128]{2,1,0:T(8,128)(2,1)S(1)}, u32[]{:S(2)}, u32[]{:S(2)}) collective-permute-start(bf16[11,88,128]{2,1,0:T(8,128)(2,1)S(1)} %get-tuple-element.74.refs_3_.refs_2_), channel_id=1, source_target_pairs={{0,2},{4,0},{8,4},{12,8},{14,12},{10,14},{6,10},{2,6},{1,3},{5,1},... | collective-permute-start | bytes 743432 | tf_op jit(solution)/shard_map/ppermute | solution.py:518
  12.1 10.6 %copy-start = (bf16[128,128]{1,0:T(8,128)(2,1)S(1)}, bf16[128,128]{1,0:T(8,128)(2,1)}, u32[]{:S(2)}) copy-start(bf16[128,128]{1,0:T(8,128)(2,1)} %refs_5_.1) | copy-start | bytes 98308
  12.1 8.2 %collective-permute-start.8 = (bf16[2,22,16,128]{3,2,1,0:T(8,128)(2,1)S(1)}, bf16[2,22,16,128]{3,2,1,0:T(8,128)(2,1)S(1)}, u32[]{:S(2)}, u32[]{:S(2)}) collective-permute-start(bf16[2,22,16,128]{3,2,1,0:T(8,128)(2,1)S(1)} %triangle.8.refs_4_.refs_0_), channel_id=1, source_target_pairs={{0,1},{1,0},{2,3},{3,2},{4,5},{5,4},{6,7},{7,6},{8,9},{9,8},{10,11... | collective-permute-start | bytes 540680 | tf_op jit(solution)/shard_map/ppermute | solution.py:77
  12.3 11.6 %collective-permute-start.7 = (bf16[11,88,128]{2,1,0:T(8,128)(2,1)S(1)}, bf16[11,88,128]{2,1,0:T(8,128)(2,1)S(1)}, u32[]{:S(2)}, u32[]{:S(2)}) collective-permute-start(bf16[11,88,128]{2,1,0:T(8,128)(2,1)S(1)} %get-tuple-element.73.refs_2_.refs_1_), channel_id=1, source_target_pairs={{0,2},{4,0},{8,4},{12,8},{14,12},{10,14},{6,10},{2,6},{1,3},{5,1},... | collective-permute-start | bytes 743432 | tf_op jit(solution)/shard_map/ppermute | solution.py:518
  15.9 8.0 %collective-permute-start.6 = (bf16[11,88,128]{2,1,0:T(8,128)(2,1)S(1)}, bf16[11,88,128]{2,1,0:T(8,128)(2,1)S(1)}, u32[]{:S(2)}, u32[]{:S(2)}) collective-permute-start(bf16[11,88,128]{2,1,0:T(8,128)(2,1)S(1)} %get-tuple-element.74.refs_3_.refs_2_), channel_id=1, source_target_pairs={{0,4},{4,8},{8,12},{12,14},{14,10},{10,6},{6,2},{2,0},{1,5},{5,9},... | collective-permute-start | bytes 743432 | tf_op jit(solution)/shard_map/ppermute | solution.py:515
  20.2 8.1 %collective-permute-start.4 = (bf16[2,22,16,128]{3,2,1,0:T(8,128)(2,1)S(1)}, bf16[2,22,16,128]{3,2,1,0:T(8,128)(2,1)S(1)}, u32[]{:S(2)}, u32[]{:S(2)}) collective-permute-start(bf16[2,22,16,128]{3,2,1,0:T(8,128)(2,1)S(1)} %triangle.9.refs_7_.refs_0_), channel_id=1, source_target_pairs={{0,1},{1,0},{2,3},{3,2},{4,5},{5,4},{6,7},{7,6},{8,9},{9,8},{10,11... | collective-permute-start | bytes 540680 | tf_op jit(solution)/shard_map/ppermute | solution.py:77
  20.3 8.9 %collective-permute-start.2 = (bf16[11,88,128]{2,1,0:T(8,128)(2,1)S(1)}, bf16[11,88,128]{2,1,0:T(8,128)(2,1)S(1)}, u32[]{:S(2)}, u32[]{:S(2)}) collective-permute-start(bf16[11,88,128]{2,1,0:T(8,128)(2,1)S(1)} %collective-permute-done.refs_2_.refs_1_), channel_id=1, source_target_pairs={{0,4},{4,8},{8,12},{12,14},{14,10},{10,6},{6,2},{2,0},{1,5},{5,9},... | collective-permute-start | bytes 743432 | tf_op jit(solution)/shard_map/ppermute | solution.py:515
  22.6 8.8 %collective-permute-start.3 = (bf16[11,88,128]{2,1,0:T(8,128)(2,1)S(1)}, bf16[11,88,128]{2,1,0:T(8,128)(2,1)S(1)}, u32[]{:S(2)}, u32[]{:S(2)}) collective-permute-start(bf16[11,88,128]{2,1,0:T(8,128)(2,1)S(1)} %collective-permute-done.1.refs_3_.refs_2_), channel_id=1, source_target_pairs={{0,2},{4,0},{8,4},{12,8},{14,12},{10,14},{6,10},{2,6},{1,3},{5,1},... | collective-permute-start | bytes 743432 | tf_op jit(solution)/shard_map/ppermute | solution.py:518
  22.6 0.7 copy-start.6
  22.6 0.7 copy-start.7
  23.9 13.0 %collective-permute-start.12 = (bf16[11,88,128]{2,1,0:T(8,128)(2,1)S(1)}, bf16[11,88,128]{2,1,0:T(8,128)(2,1)S(1)}, u32[]{:S(2)}, u32[]{:S(2)}) collective-permute-start(bf16[11,88,128]{2,1,0:T(8,128)(2,1)S(1)} %collective-permute-done.6.refs_2_.refs_1_), channel_id=1, source_target_pairs={{0,4},{4,8},{8,12},{12,14},{14,10},{10,6},{6,2},{2,0},{1,5},{5,9},... | collective-permute-start | bytes 743432 | tf_op jit(solution)/shard_map/ppermute | solution.py:515
  25.9 11.0 %collective-permute-start.13 = (bf16[11,88,128]{2,1,0:T(8,128)(2,1)S(1)}, bf16[11,88,128]{2,1,0:T(8,128)(2,1)S(1)}, u32[]{:S(2)}, u32[]{:S(2)}) collective-permute-start(bf16[11,88,128]{2,1,0:T(8,128)(2,1)S(1)} %collective-permute-done.7.refs_3_.refs_2_), channel_id=1, source_target_pairs={{0,2},{4,0},{8,4},{12,8},{14,12},{10,14},{6,10},{2,6},{1,3},{5,1},... | collective-permute-start | bytes 743432 | tf_op jit(solution)/shard_map/ppermute | solution.py:518
  28.3 7.2 %collective-permute-start.14 = (bf16[2,22,16,128]{3,2,1,0:T(8,128)(2,1)S(1)}, bf16[2,22,16,128]{3,2,1,0:T(8,128)(2,1)S(1)}, u32[]{:S(2)}, u32[]{:S(2)}) collective-permute-start(bf16[2,22,16,128]{3,2,1,0:T(8,128)(2,1)S(1)} %triangle.10.refs_7_.refs_0_), channel_id=1, source_target_pairs={{0,1},{1,0},{2,3},{3,2},{4,5},{5,4},{6,7},{7,6},{8,9},{9,8},{10,11... | collective-permute-start | bytes 540680 | tf_op jit(solution)/shard_map/ppermute | solution.py:77
  34.2 6.7 %collective-permute-start.11 = (bf16[2,22,16,128]{3,2,1,0:T(8,128)(2,1)S(1)}, bf16[2,22,16,128]{3,2,1,0:T(8,128)(2,1)S(1)}, u32[]{:S(2)}, u32[]{:S(2)}) collective-permute-start(bf16[2,22,16,128]{3,2,1,0:T(8,128)(2,1)S(1)} %triangle.11.refs_7_.refs_0_), channel_id=1, source_target_pairs={{0,1},{1,0},{2,3},{3,2},{4,5},{5,4},{6,7},{7,6},{8,9},{9,8},{10,11... | collective-permute-start | bytes 540680 | tf_op jit(solution)/shard_map/ppermute | solution.py:77
  34.2 8.9 %collective-permute-start.9 = (bf16[11,88,128]{2,1,0:T(8,128)(2,1)S(1)}, bf16[11,88,128]{2,1,0:T(8,128)(2,1)S(1)}, u32[]{:S(2)}, u32[]{:S(2)}) collective-permute-start(bf16[11,88,128]{2,1,0:T(8,128)(2,1)S(1)} %collective-permute-done.2.refs_2_.refs_1_), channel_id=1, source_target_pairs={{0,4},{4,8},{8,12},{12,14},{14,10},{10,6},{6,2},{2,0},{1,5},{5,9},... | collective-permute-start | bytes 743432 | tf_op jit(solution)/shard_map/ppermute | solution.py:515
  35.5 8.8 %collective-permute-start.10 = (bf16[11,88,128]{2,1,0:T(8,128)(2,1)S(1)}, bf16[11,88,128]{2,1,0:T(8,128)(2,1)S(1)}, u32[]{:S(2)}, u32[]{:S(2)}) collective-permute-start(bf16[11,88,128]{2,1,0:T(8,128)(2,1)S(1)} %collective-permute-done.3.refs_3_.refs_2_), channel_id=1, source_target_pairs={{0,2},{4,0},{8,4},{12,8},{14,12},{10,14},{6,10},{2,6},{1,3},{5,1},... | collective-permute-start | bytes 743432 | tf_op jit(solution)/shard_map/ppermute | solution.py:518
  36.9 12.5 %collective-permute-start.17 = (bf16[11,88,128]{2,1,0:T(8,128)(2,1)S(1)}, bf16[11,88,128]{2,1,0:T(8,128)(2,1)S(1)}, u32[]{:S(2)}, u32[]{:S(2)}) collective-permute-start(bf16[11,88,128]{2,1,0:T(8,128)(2,1)S(1)} %collective-permute-done.12.refs_2_.refs_1_), channel_id=1, source_target_pairs={{0,4},{4,8},{8,12},{12,14},{14,10},{10,6},{6,2},{2,0},{1,5},{5,9},... | collective-permute-start | bytes 743432 | tf_op jit(solution)/shard_map/ppermute | solution.py:515
  38.2 11.5 %collective-permute-start.18 = (bf16[11,88,128]{2,1,0:T(8,128)(2,1)S(1)}, bf16[11,88,128]{2,1,0:T(8,128)(2,1)S(1)}, u32[]{:S(2)}, u32[]{:S(2)}) collective-permute-start(bf16[11,88,128]{2,1,0:T(8,128)(2,1)S(1)} %collective-permute-done.13.refs_3_.refs_2_), channel_id=1, source_target_pairs={{0,2},{4,0},{8,4},{12,8},{14,12},{10,14},{6,10},{2,6},{1,3},{5,1},... | collective-permute-start | bytes 743432 | tf_op jit(solution)/shard_map/ppermute | solution.py:518
  40.8 7.9 %collective-permute-start.19 = (bf16[2,22,16,128]{3,2,1,0:T(8,128)(2,1)S(1)}, bf16[2,22,16,128]{3,2,1,0:T(8,128)(2,1)S(1)}, u32[]{:S(2)}, u32[]{:S(2)}) collective-permute-start(bf16[2,22,16,128]{3,2,1,0:T(8,128)(2,1)S(1)} %triangle.12.refs_7_.refs_0_), channel_id=1, source_target_pairs={{0,1},{1,0},{2,3},{3,2},{4,5},{5,4},{6,7},{7,6},{8,9},{9,8},{10,11... | collective-permute-start | bytes 540680 | tf_op jit(solution)/shard_map/ppermute | solution.py:77
  44.4 10.2 %collective-permute-start.15 = (bf16[11,88,128]{2,1,0:T(8,128)(2,1)S(1)}, bf16[11,88,128]{2,1,0:T(8,128)(2,1)S(1)}, u32[]{:S(2)}, u32[]{:S(2)}) collective-permute-start(bf16[11,88,128]{2,1,0:T(8,128)(2,1)S(1)} %collective-permute-done.9.refs_2_.refs_1_), channel_id=1, source_target_pairs={{0,4},{4,8},{8,12},{12,14},{14,10},{10,6},{6,2},{2,0},{1,5},{5,9},... | collective-permute-start | bytes 743432 | tf_op jit(solution)/shard_map/ppermute | solution.py:515
  45.2 9.4 %collective-permute-start.16 = (bf16[11,88,128]{2,1,0:T(8,128)(2,1)S(1)}, bf16[11,88,128]{2,1,0:T(8,128)(2,1)S(1)}, u32[]{:S(2)}, u32[]{:S(2)}) collective-permute-start(bf16[11,88,128]{2,1,0:T(8,128)(2,1)S(1)} %collective-permute-done.10.refs_3_.refs_2_), channel_id=1, source_target_pairs={{0,2},{4,0},{8,4},{12,8},{14,12},{10,14},{6,10},{2,6},{1,3},{5,1},... | collective-permute-start | bytes 743432 | tf_op jit(solution)/shard_map/ppermute | solution.py:518
  48.8 2.9 %collective-permute-start.21 = (bf16[2,22,16,128]{3,2,1,0:T(8,128)(2,1)S(1)}, bf16[2,22,16,128]{3,2,1,0:T(8,128)(2,1)S(1)}, u32[]{:S(2)}, u32[]{:S(2)}) collective-permute-start(bf16[2,22,16,128]{3,2,1,0:T(8,128)(2,1)S(1)} %triangle.13.refs_7_.refs_0_), channel_id=1, source_target_pairs={{0,1},{1,0},{2,3},{3,2},{4,5},{5,4},{6,7},{7,6},{8,9},{9,8},{10,11... | collective-permute-start | bytes 540680 | tf_op jit(solution)/shard_map/ppermute | solution.py:77
  51.4 1.5 %collective-permute-start.20 = (bf16[2,22,16,128]{3,2,1,0:T(8,128)(2,1)S(1)}, bf16[2,22,16,128]{3,2,1,0:T(8,128)(2,1)S(1)}, u32[]{:S(2)}, u32[]{:S(2)}) collective-permute-start(bf16[2,22,16,128]{3,2,1,0:T(8,128)(2,1)S(1)} %triangle.14.refs_7_.refs_0_), channel_id=1, source_target_pairs={{0,1},{1,0},{2,3},{3,2},{4,5},{5,4},{6,7},{7,6},{8,9},{9,8},{10,11... | collective-permute-start | bytes 540680 | tf_op jit(solution)/shard_map/ppermute | solution.py:77
  57.0 3.7 %collective-permute-start.22 = (bf16[2,22,16,128]{3,2,1,0:T(8,128)(2,1)S(1)}, bf16[2,22,16,128]{3,2,1,0:T(8,128)(2,1)S(1)}, u32[]{:S(2)}, u32[]{:S(2)}) collective-permute-start(bf16[2,22,16,128]{3,2,1,0:T(8,128)(2,1)S(1)} %triangle.15.refs_3_.refs_0_), channel_id=1, source_target_pairs={{0,1},{1,0},{2,3},{3,2},{4,5},{5,4},{6,7},{7,6},{8,9},{9,8},{10,11... | collective-permute-start | bytes 540680 | tf_op jit(solution)/shard_map/ppermute | solution.py:77
  57.3 10.5 %collective-permute-start.24 = (bf16[11,88,128]{2,1,0:T(8,128)(2,1)S(1)}, bf16[11,88,128]{2,1,0:T(8,128)(2,1)S(1)}, u32[]{:S(2)}, u32[]{:S(2)}) collective-permute-start(bf16[11,88,128]{2,1,0:T(8,128)(2,1)S(1)} %get-tuple-element.98), channel_id=1, source_target_pairs={{0,4},{4,8},{8,12},{12,14},{14,10},{10,6},{6,2},{2,0},{1,5},{5,9},... | collective-permute-start | bytes 743432 | tf_op jit(solution)/shard_map/ppermute | solution.py:515
  57.8 10.0 %collective-permute-start.23 = (bf16[11,88,128]{2,1,0:T(8,128)(2,1)S(1)}, bf16[11,88,128]{2,1,0:T(8,128)(2,1)S(1)}, u32[]{:S(2)}, u32[]{:S(2)}) collective-permute-start(bf16[11,88,128]{2,1,0:T(8,128)(2,1)S(1)} %get-tuple-element.93.refs_4_), channel_id=1, source_target_pairs={{0,2},{4,0},{8,4},{12,8},{14,12},{10,14},{6,10},{2,6},{1,3},{5,1},... | collective-permute-start | bytes 743432 | tf_op jit(solution)/shard_map/ppermute | solution.py:518
  62.8 10.2 %collective-permute-start.26 = (bf16[11,88,128]{2,1,0:T(8,128)(2,1)S(1)}, bf16[11,88,128]{2,1,0:T(8,128)(2,1)S(1)}, u32[]{:S(2)}, u32[]{:S(2)}) collective-permute-start(bf16[11,88,128]{2,1,0:T(8,128)(2,1)S(1)} %get-tuple-element.102), channel_id=1, source_target_pairs={{0,4},{4,8},{8,12},{12,14},{14,10},{10,6},{6,2},{2,0},{1,5},{5,9},... | collective-permute-start | bytes 743432 | tf_op jit(solution)/shard_map/ppermute | solution.py:515
  62.8 10.2 %collective-permute-start.25 = (bf16[11,88,128]{2,1,0:T(8,128)(2,1)S(1)}, bf16[11,88,128]{2,1,0:T(8,128)(2,1)S(1)}, u32[]{:S(2)}, u32[]{:S(2)}) collective-permute-start(bf16[11,88,128]{2,1,0:T(8,128)(2,1)S(1)} %get-tuple-element.95.refs_4_), channel_id=1, source_target_pairs={{0,2},{4,0},{8,4},{12,8},{14,12},{10,14},{6,10},{2,6},{1,3},{5,1},... | collective-permute-start | bytes 743432 | tf_op jit(solution)/shard_map/ppermute | solution.py:518
  68.0 9.9 %collective-permute-start.28 = (bf16[11,88,128]{2,1,0:T(8,128)(2,1)S(1)}, bf16[11,88,128]{2,1,0:T(8,128)(2,1)S(1)}, u32[]{:S(2)}, u32[]{:S(2)}) collective-permute-start(bf16[11,88,128]{2,1,0:T(8,128)(2,1)S(1)} %get-tuple-element.106), channel_id=1, source_target_pairs={{0,4},{4,8},{8,12},{12,14},{14,10},{10,6},{6,2},{2,0},{1,5},{5,9},... | collective-permute-start | bytes 743432 | tf_op jit(solution)/shard_map/ppermute | solution.py:515
  70.0 8.3 %collective-permute-start.27 = (bf16[11,88,128]{2,1,0:T(8,128)(2,1)S(1)}, bf16[11,88,128]{2,1,0:T(8,128)(2,1)S(1)}, u32[]{:S(2)}, u32[]{:S(2)}) collective-permute-start(bf16[11,88,128]{2,1,0:T(8,128)(2,1)S(1)} %get-tuple-element.99.refs_4_), channel_id=1, source_target_pairs={{0,2},{4,0},{8,4},{12,8},{14,12},{10,14},{6,10},{2,6},{1,3},{5,1},... | collective-permute-start | bytes 743432 | tf_op jit(solution)/shard_map/ppermute | solution.py:518
  73.1 10.5 %collective-permute-start.30 = (bf16[11,88,128]{2,1,0:T(8,128)(2,1)S(1)}, bf16[11,88,128]{2,1,0:T(8,128)(2,1)S(1)}, u32[]{:S(2)}, u32[]{:S(2)}) collective-permute-start(bf16[11,88,128]{2,1,0:T(8,128)(2,1)S(1)} %get-tuple-element.110), channel_id=1, source_target_pairs={{0,4},{4,8},{8,12},{12,14},{14,10},{10,6},{6,2},{2,0},{1,5},{5,9},... | collective-permute-start | bytes 743432 | tf_op jit(solution)/shard_map/ppermute | solution.py:515
  73.7 9.9 %collective-permute-start.29 = (bf16[11,88,128]{2,1,0:T(8,128)(2,1)S(1)}, bf16[11,88,128]{2,1,0:T(8,128)(2,1)S(1)}, u32[]{:S(2)}, u32[]{:S(2)}) collective-permute-start(bf16[11,88,128]{2,1,0:T(8,128)(2,1)S(1)} %get-tuple-element.103.refs_4_), channel_id=1, source_target_pairs={{0,2},{4,0},{8,4},{12,8},{14,12},{10,14},{6,10},{2,6},{1,3},{5,1},... | collective-permute-start | bytes 743432 | tf_op jit(solution)/shard_map/ppermute | solution.py:518
  78.4 14.6 %collective-permute-start.33 = (bf16[11,88,128]{2,1,0:T(8,128)(2,1)S(1)}, bf16[11,88,128]{2,1,0:T(8,128)(2,1)S(1)}, u32[]{:S(2)}, u32[]{:S(2)}) collective-permute-start(bf16[11,88,128]{2,1,0:T(8,128)(2,1)S(1)} %get-tuple-element.107.refs_4_), channel_id=1, source_target_pairs={{0,2},{4,0},{8,4},{12,8},{14,12},{10,14},{6,10},{2,6},{1,3},{5,1},... | collective-permute-start | bytes 743432 | tf_op jit(solution)/shard_map/ppermute | solution.py:518
  81.5 11.5 %collective-permute-start.34 = (bf16[11,88,128]{2,1,0:T(8,128)(2,1)S(1)}, bf16[11,88,128]{2,1,0:T(8,128)(2,1)S(1)}, u32[]{:S(2)}, u32[]{:S(2)}) collective-permute-start(bf16[11,88,128]{2,1,0:T(8,128)(2,1)S(1)} %get-tuple-element.124), channel_id=1, source_target_pairs={{0,4},{4,8},{8,12},{12,14},{14,10},{10,6},{6,2},{2,0},{1,5},{5,9},... | collective-permute-start | bytes 743432 | tf_op jit(solution)/shard_map/ppermute | solution.py:515
  83.7 9.2 %collective-permute-start.32 = (bf16[11,88,128]{2,1,0:T(8,128)(2,1)S(1)}, bf16[11,88,128]{2,1,0:T(8,128)(2,1)S(1)}, u32[]{:S(2)}, u32[]{:S(2)}) collective-permute-start(bf16[11,88,128]{2,1,0:T(8,128)(2,1)S(1)} %get-tuple-element.123), channel_id=1, source_target_pairs={{0,4},{4,8},{8,12},{12,14},{14,10},{10,6},{6,2},{2,0},{1,5},{5,9},... | collective-permute-start | bytes 743432 | tf_op jit(solution)/shard_map/ppermute | solution.py:515
  86.0 7.0 %collective-permute-start.31 = (bf16[11,88,128]{2,1,0:T(8,128)(2,1)S(1)}, bf16[11,88,128]{2,1,0:T(8,128)(2,1)S(1)}, u32[]{:S(2)}, u32[]{:S(2)}) collective-permute-start(bf16[11,88,128]{2,1,0:T(8,128)(2,1)S(1)} %get-tuple-element.111.refs_4_), channel_id=1, source_target_pairs={{0,2},{4,0},{8,4},{12,8},{14,12},{10,14},{6,10},{2,6},{1,3},{5,1},... | collective-permute-start | bytes 743432 | tf_op jit(solution)/shard_map/ppermute | solution.py:518
  93.1 8.7 %collective-permute-start.36 = (bf16[11,88,128]{2,1,0:T(8,128)(2,1)S(1)}, bf16[11,88,128]{2,1,0:T(8,128)(2,1)S(1)}, u32[]{:S(2)}, u32[]{:S(2)}) collective-permute-start(bf16[11,88,128]{2,1,0:T(8,128)(2,1)S(1)} %get-tuple-element.129), channel_id=1, source_target_pairs={{0,4},{4,8},{8,12},{12,14},{14,10},{10,6},{6,2},{2,0},{1,5},{5,9},... | collective-permute-start | bytes 743432 | tf_op jit(solution)/shard_map/ppermute | solution.py:515
  95.2 6.6 %collective-permute-start.35 = (bf16[11,88,128]{2,1,0:T(8,128)(2,1)S(1)}, bf16[11,88,128]{2,1,0:T(8,128)(2,1)S(1)}, u32[]{:S(2)}, u32[]{:S(2)}) collective-permute-start(bf16[11,88,128]{2,1,0:T(8,128)(2,1)S(1)} %get-tuple-element.125.refs_15_), channel_id=1, source_target_pairs={{0,2},{4,0},{8,4},{12,8},{14,12},{10,14},{6,10},{2,6},{1,3},{5,1},... | collective-permute-start | bytes 743432 | tf_op jit(solution)/shard_map/ppermute | solution.py:518
  103.9 12.8 %copy-start.4 = (bf16[22,88,128]{2,1,0:T(8,128)(2,1)S(1)}, bf16[22,88,128]{2,1,0:T(8,128)(2,1)}, u32[]{:S(2)}) copy-start(bf16[22,88,128]{2,1,0:T(8,128)(2,1)} %refs_0_.41) | copy-start | bytes 1486852
  103.9 1.4 %collective-permute-start.37 = (bf16[64,768]{1,0:T(8,128)(2,1)S(1)}, bf16[64,768]{1,0:T(8,128)(2,1)S(1)}, u32[]{:S(2)}, u32[]{:S(2)}) collective-permute-start(bf16[64,768]{1,0:T(8,128)(2,1)S(1)} %get-tuple-element.131), channel_id=1, source_target_pairs={{0,1},{1,0},{2,3},{3,2},{4,5},{5,4},{6,7},{7,6},{8,9},{9,8},{10,11... | collective-permute-start | bytes 294920 | tf_op jit(solution)/shard_map/ppermute | solution.py:77
  105.3 6.2 %collective-permute-start.40 = (bf16[64,768]{1,0:T(8,128)(2,1)S(1)}, bf16[64,768]{1,0:T(8,128)(2,1)S(1)}, u32[]{:S(2)}, u32[]{:S(2)}) collective-permute-start(bf16[64,768]{1,0:T(8,128)(2,1)S(1)} %add_convert_fusion.2), channel_id=1, source_target_pairs={{0,6},{2,4},{4,2},{6,0},{8,14},{10,12},{12,10},{14,8},{1,7},{3,5},... | collective-permute-start | bytes 294920 | tf_op jit(solution)/shard_map/ppermute | solution.py:684
  108.0 5.4 %collective-permute-start.39 = (bf16[64,768]{1,0:T(8,128)(2,1)S(1)}, bf16[64,768]{1,0:T(8,128)(2,1)S(1)}, u32[]{:S(2)}, u32[]{:S(2)}) collective-permute-start(bf16[64,768]{1,0:T(8,128)(2,1)S(1)} %add_convert_fusion.2), channel_id=1, source_target_pairs={{0,4},{2,6},{4,0},{6,2},{8,12},{10,14},{12,8},{14,10},{1,5},{3,7},... | collective-permute-start | bytes 294920 | tf_op jit(solution)/shard_map/ppermute | solution.py:684
  108.5 4.9 %collective-permute-start.38 = (bf16[64,768]{1,0:T(8,128)(2,1)S(1)}, bf16[64,768]{1,0:T(8,128)(2,1)S(1)}, u32[]{:S(2)}, u32[]{:S(2)}) collective-permute-start(bf16[64,768]{1,0:T(8,128)(2,1)S(1)} %add_convert_fusion.2), channel_id=1, source_target_pairs={{0,2},{2,0},{4,6},{6,4},{8,10},{10,8},{12,14},{14,12},{1,3},{3,1},... | collective-permute-start | bytes 294920 | tf_op jit(solution)/shard_map/ppermute | solution.py:684
  113.5 8.3 %collective-permute-start.41 = (bf16[64,768]{1,0:T(8,128)(2,1)S(1)}, bf16[64,768]{1,0:T(8,128)(2,1)S(1)}, u32[]{:S(2)}, u32[]{:S(2)}) collective-permute-start(bf16[64,768]{1,0:T(8,128)(2,1)S(1)} %add_convert_fusion.1), channel_id=1, source_target_pairs={{0,8},{2,10},{4,12},{6,14},{8,0},{10,2},{12,4},{14,6},{1,9},{3,11}... | collective-permute-start | bytes 294920 | tf_op jit(solution)/shard_map/ppermute | solution.py:684
  121.8 1.4 %collective-permute-start.42 = (bf16[64,768]{1,0:T(8,128)(2,1)S(1)}, bf16[64,768]{1,0:T(8,128)(2,1)S(1)}, u32[]{:S(2)}, u32[]{:S(2)}) collective-permute-start(bf16[64,768]{1,0:T(8,128)(2,1)S(1)} %add_convert_fusion.refs_0_), channel_id=1, source_target_pairs={{0,1},{1,0},{2,3},{3,2},{4,5},{5,4},{6,7},{7,6},{8,9},{9,8},{10,11... | collective-permute-start | bytes 294920 | tf_op jit(solution)/shard_map/ppermute | solution.py:77

commit v3 on v2

--- a/solution.py
+++ b/solution.py
@@ -597,14 +597,17 @@
 
     arrived = {0: [], 1: []}
 
+    prepared = {}
+
+    def prepare(s, chain):
+        prepared[s, chain] = scatter(2 * s - 1 + chain, [0, 1], [], f32)
+
     def send(s, chain, after=()):
-        group, picks = 2 * s - 1 + chain, [0, 1]
         if arrived[chain]:
-            terms = scatter(group, picks, [], f32)
             x, y = call(
                 add_kernel,
                 "scatter_add",
-                [*terms, *arrived[chain]],
+                [*prepared[s, chain], *arrived[chain]],
                 [VMEM] * 4,
                 [shape_of((short, half, hidden), bf16)] * 2,
                 (),
@@ -612,7 +615,7 @@
             )
             last[:] = [x]
         else:
-            x, y = scatter(group, picks, [])
+            x, y = scatter(2 * s - 1 + chain, [0, 1], [])
         arrived[chain] = [behind(x), ahead(y)]
 
     def output_side():
@@ -654,16 +657,20 @@
     normal(steps - 1)
     send(hops, 0)
     add_lefts(1)
-    send(hops - 2, 1)
+    prepare(hops - 2, 1)
+    prepare(hops - 1, 0)
     for s in range(hops - 1, 0, -1):
-        add_lefts(1)
-        if s == 1:
+        if s > 1:
+            send(s - 1, 1)
+        send(s, 0, arrived[1] if s == 1 else ())
+        if s == 2:
             own_a, own_b = scatter(0, [0, 1], [], f32)
-            add_lefts(2)
-        send(s, 0, arrived[1] if s == 1 else ())
-        if s > 2:
+        if s > 1:
             add_lefts(1)
-            send(s - 2, 1)
+            if s > 2:
+                prepare(s - 2, 1)
+            prepare(s - 1, 0)
+            add_lefts(1 if s > 2 else 2)
     add_lefts(steps)
     update, gradient, early = output_side()
     arrived1, arrived2 = arrived[0], [arrived[1][1], arrived[1][0]]

time: 124 us -> 126 us (1.016)
  waiting for transfers between devices: 17.9 us -> 20.7 us
  starting transfers between devices: 40.6 us -> 39.1 us
    ppermute x14, starting transfers between devices: 18.8 us -> 25 us  [ahead(): return lax.ppermute(x, 'row', forward)]
    ppermute x14, starting transfers between devices: 13.2 us -> 7.62 us  [behind(): return lax.ppermute(x, 'row', backward)]
    ppermute x14, waiting for transfers between devices: 4.68 us -> 7.22 us  [behind(): return lax.ppermute(x, 'row', backward)]
    ppermute x4, starting transfers between devices: 6.74 us -> 4.92 us  [from_row(): return lax.ppermute(mine, 'row', [(r, r ^ apart) for r in range(row_count)])]
  transfers between devices with their start and end apart: 43 -> 43, of which waited for: 14 -> 16; matrix products, arithmetic and copies ran while one was open for 0% -> 0% of each run, Pallas kernels for 42% -> 42%
where the time goes in v3:
time: 126 us; the launch traced here: 125 us
  Pallas kernels  61.1 us (48%)
  starting transfers between devices  39.1 us (31%)
  waiting for transfers between devices  20.7 us (16%)
  local copies, waits for them, and re-layouts  3.3 us (3%)
    pallas_call x43, Pallas kernels, call(): pl.pallas_call(body, out_shape=list(outs), in_specs=list(specs) + [ANY] *...  61.1 us
    ppermute x14, starting transfers between devices, ahead(): return lax.ppermute(x, 'row', forward)  25 us
    ppermute x14, starting transfers between devices, behind(): return lax.ppermute(x, 'row', backward)  7.62 us
    ppermute x14, waiting for transfers between devices, behind(): return lax.ppermute(x, 'row', backward)  7.22 us
    ppermute x4, waiting for transfers between devices, from_row(): return lax.ppermute(mine, 'row', [(r, r ^ apart) for r in range(row_count)])  6.65 us
    ppermute x4, starting transfers between devices, from_row(): return lax.ppermute(mine, 'row', [(r, r ^ apart) for r in range(row_count)])  4.92 us
    ppermute x11, waiting for transfers between devices, swap_col(): return lax.ppermute(x, 'col', [(0, 1), (1, 0)])  3.44 us
    ppermute x14, waiting for transfers between devices, ahead(): return lax.ppermute(x, 'row', forward)  3.4 us
  transfers between devices with their start and end apart: 43, of which 16 were waited for; matrix products, arithmetic and copies ran while one was open for 0% of the time, Pallas kernels for 42%

profile of v3, /device:TPU:0, one launch (start us, length us, event | category | flops | bytes accessed | tf_op | source)
XLA Modules:
  0.0 125.5 jit_solution(13777604127522175388)
XLA Ops:
  1.3 0.9 copy-done.1
  2.2 1.0 copy-done.3
  3.3 1.5 %input_side.1 = (bf16[11,88,128]{2,1,0:T(8,128)(2,1)S(1)}, bf16[11,88,128]{2,1,0:T(8,128)(2,1)S(1)}, bf16[22,88,128]{2,1,0:T(8,128)(2,1)S(1)}) custom-call(s32[8]{0:T(128)S(1)} %copy-done.5, bf16[22,88,128]{2,1,0:T(8,128)(2,1)S(1)} %copy-done.3, f32[1,128]{1,0:T(1,128)S(1)} %bitcast.21, f32[1,128]{1,0:T(1,128)S(1)} %bitcast.20, bf16[128,640]{1,0:T(8,128)(2,1)S(1)} %copy-done.1), custom_call_target="tpu_custom_call" | custom-call | flops 1024 | bytes 1024 | tf_op jit(solution)/shard_map/input_side/pallas_call | solution.py:93
  4.8 1.4 %left_side.1 = (bf16[22,88,128]{2,1,0:T(8,128)(2,1)S(1)}, bf16[8,22,16,128]{3,2,1,0:T(8,128)(2,1)S(1)}) custom-call(s32[8]{0:T(128)S(1)} %copy-done.5, bf16[22,88,128]{2,1,0:T(8,128)(2,1)S(1)} %get-tuple-element.71.refs_1_, bf16[22,88,128]{2,1,0:T(8,128)(2,1)S(1)} %copy-done.10, bf16[128,640]{1,0:T(8,128)(2,1)S(1)} %copy-done.2), custom_call_target="tpu_custom_call" | custom-call | flops 4400001024 | bytes 1024 | tf_op jit(solution)/shard_map/left_side/pallas_call | solution.py:93
  6.7 2.6 %collective-permute-start = (bf16[11,88,128]{2,1,0:T(8,128)(2,1)S(1)}, bf16[11,88,128]{2,1,0:T(8,128)(2,1)S(1)}, u32[]{:S(2)}, u32[]{:S(2)}) collective-permute-start(bf16[11,88,128]{2,1,0:T(8,128)(2,1)S(1)} %get-tuple-element.73.refs_2_.refs_1_), channel_id=1, source_target_pairs={{0,4},{4,8},{8,12},{12,14},{14,10},{10,6},{6,2},{2,0},{1,5},{5,9},... | collective-permute-start | bytes 743432 | tf_op jit(solution)/shard_map/ppermute | solution.py:515
  9.4 1.8 %triangle.8.refs_4_.refs_0_ = bf16[2,22,16,128]{3,2,1,0:T(8,128)(2,1)S(1)} custom-call(s32[8]{0:T(128)S(1)} %copy-done.5, bf16[22,88,128]{2,1,0:T(8,128)(2,1)S(1)} %get-tuple-element.72.refs_1_.refs_4_, bf16[11,88,128]{2,1,0:T(8,128)(2,1)S(1)} %get-tuple-element.73.refs_2_.refs_1_, bf16[11,88,128]{2,1,0:T(8,128)(2,1)S(1)} %get-tuple-element.74.refs_3_.refs_2_, ...), custom_call_target="tpu_custom_call" | custom-call | flops 1024 | bytes 1024 | tf_op jit(solution)/shard_map/triangle/pallas_call | solution.py:93
  11.4 2.6 %collective-permute-start.7 = (bf16[11,88,128]{2,1,0:T(8,128)(2,1)S(1)}, bf16[11,88,128]{2,1,0:T(8,128)(2,1)S(1)}, u32[]{:S(2)}, u32[]{:S(2)}) collective-permute-start(bf16[11,88,128]{2,1,0:T(8,128)(2,1)S(1)} %get-tuple-element.73.refs_2_.refs_1_), channel_id=1, source_target_pairs={{0,2},{4,0},{8,4},{12,8},{14,12},{10,14},{6,10},{2,6},{1,3},{5,1},... | collective-permute-start | bytes 743432 | tf_op jit(solution)/shard_map/ppermute | solution.py:518
  14.0 1.9 %collective-permute-done.refs_2_.refs_1_ = bf16[11,88,128]{2,1,0:T(8,128)(2,1)S(1)} collective-permute-done((bf16[11,88,128]{2,1,0:T(8,128)(2,1)S(1)}, bf16[11,88,128]{2,1,0:T(8,128)(2,1)S(1)}, u32[]{:S(2)}, u32[]{:S(2)}) %collective-permute-start) | collective-permute-done | bytes 247840 | tf_op jit(solution)/shard_map/ppermute | solution.py:515
  15.9 1.8 %collective-permute-start.6 = (bf16[11,88,128]{2,1,0:T(8,128)(2,1)S(1)}, bf16[11,88,128]{2,1,0:T(8,128)(2,1)S(1)}, u32[]{:S(2)}, u32[]{:S(2)}) collective-permute-start(bf16[11,88,128]{2,1,0:T(8,128)(2,1)S(1)} %get-tuple-element.74.refs_3_.refs_2_), channel_id=1, source_target_pairs={{0,4},{4,8},{8,12},{12,14},{14,10},{10,6},{6,2},{2,0},{1,5},{5,9},... | collective-permute-start | bytes 743432 | tf_op jit(solution)/shard_map/ppermute | solution.py:515
  18.2 2.2 %triangle.9.refs_7_.refs_0_ = bf16[2,22,16,128]{3,2,1,0:T(8,128)(2,1)S(1)} custom-call(s32[8]{0:T(128)S(1)} %copy-done.5, bf16[22,88,128]{2,1,0:T(8,128)(2,1)S(1)} %get-tuple-element.72.refs_1_.refs_4_, bf16[11,88,128]{2,1,0:T(8,128)(2,1)S(1)} %collective-permute-done.refs_2_.refs_1_, bf16[11,88,128]{2,1,0:T(8,128)(2,1)S(1)} %collective-permute-done.1.refs_3_.refs_2_, ...), custom_call_target="tpu_custom_call" | custom-call | flops 1024 | bytes 1024 | tf_op jit(solution)/shard_map/triangle/pallas_call | solution.py:93
  20.5 1.6 %collective-permute-start.2 = (bf16[11,88,128]{2,1,0:T(8,128)(2,1)S(1)}, bf16[11,88,128]{2,1,0:T(8,128)(2,1)S(1)}, u32[]{:S(2)}, u32[]{:S(2)}) collective-permute-start(bf16[11,88,128]{2,1,0:T(8,128)(2,1)S(1)} %collective-permute-done.refs_2_.refs_1_), channel_id=1, source_target_pairs={{0,4},{4,8},{8,12},{12,14},{14,10},{10,6},{6,2},{2,0},{1,5},{5,9},... | collective-permute-start | bytes 743432 | tf_op jit(solution)/shard_map/ppermute | solution.py:515
  23.8 1.6 %collective-permute-start.12 = (bf16[11,88,128]{2,1,0:T(8,128)(2,1)S(1)}, bf16[11,88,128]{2,1,0:T(8,128)(2,1)S(1)}, u32[]{:S(2)}, u32[]{:S(2)}) collective-permute-start(bf16[11,88,128]{2,1,0:T(8,128)(2,1)S(1)} %collective-permute-done.6.refs_2_.refs_1_), channel_id=1, source_target_pairs={{0,4},{4,8},{8,12},{12,14},{14,10},{10,6},{6,2},{2,0},{1,5},{5,9},... | collective-permute-start | bytes 743432 | tf_op jit(solution)/shard_map/ppermute | solution.py:515
  25.4 0.8 collective-permute-start.13
  26.2 2.5 %triangle.10.refs_7_.refs_0_ = bf16[2,22,16,128]{3,2,1,0:T(8,128)(2,1)S(1)} custom-call(s32[8]{0:T(128)S(1)} %copy-done.5, bf16[22,88,128]{2,1,0:T(8,128)(2,1)S(1)} %get-tuple-element.72.refs_1_.refs_4_, bf16[11,88,128]{2,1,0:T(8,128)(2,1)S(1)} %collective-permute-done.6.refs_2_.refs_1_, bf16[11,88,128]{2,1,0:T(8,128)(2,1)S(1)} %collective-permute-done.7.refs_3_.refs_2_, ...), custom_call_target="tpu_custom_call" | custom-call | flops 1024 | bytes 1024 | tf_op jit(solution)/shard_map/triangle/pallas_call | solution.py:93
  29.4 1.5 %collective-permute-done.3.refs_3_.refs_2_ = bf16[11,88,128]{2,1,0:T(8,128)(2,1)S(1)} collective-permute-done((bf16[11,88,128]{2,1,0:T(8,128)(2,1)S(1)}, bf16[11,88,128]{2,1,0:T(8,128)(2,1)S(1)}, u32[]{:S(2)}, u32[]{:S(2)}) %collective-permute-start.3) | collective-permute-done | bytes 247840 | tf_op jit(solution)/shard_map/ppermute | solution.py:518
  30.9 2.2 %triangle.11.refs_7_.refs_0_ = bf16[2,22,16,128]{3,2,1,0:T(8,128)(2,1)S(1)} custom-call(s32[8]{0:T(128)S(1)} %copy-done.5, bf16[22,88,128]{2,1,0:T(8,128)(2,1)S(1)} %get-tuple-element.72.refs_1_.refs_4_, bf16[11,88,128]{2,1,0:T(8,128)(2,1)S(1)} %collective-permute-done.2.refs_2_.refs_1_, bf16[11,88,128]{2,1,0:T(8,128)(2,1)S(1)} %collective-permute-done.3.refs_3_.refs_2_, ...), custom_call_target="tpu_custom_call" | custom-call | flops 1024 | bytes 1024 | tf_op jit(solution)/shard_map/triangle/pallas_call | solution.py:93
  33.2 1.3 %collective-permute-start.9 = (bf16[11,88,128]{2,1,0:T(8,128)(2,1)S(1)}, bf16[11,88,128]{2,1,0:T(8,128)(2,1)S(1)}, u32[]{:S(2)}, u32[]{:S(2)}) collective-permute-start(bf16[11,88,128]{2,1,0:T(8,128)(2,1)S(1)} %collective-permute-done.2.refs_2_.refs_1_), channel_id=1, source_target_pairs={{0,4},{4,8},{8,12},{12,14},{14,10},{10,6},{6,2},{2,0},{1,5},{5,9},... | collective-permute-start | bytes 743432 | tf_op jit(solution)/shard_map/ppermute | solution.py:515
  34.5 0.8 collective-permute-start.10
  35.9 1.3 %collective-permute-start.17 = (bf16[11,88,128]{2,1,0:T(8,128)(2,1)S(1)}, bf16[11,88,128]{2,1,0:T(8,128)(2,1)S(1)}, u32[]{:S(2)}, u32[]{:S(2)}) collective-permute-start(bf16[11,88,128]{2,1,0:T(8,128)(2,1)S(1)} %collective-permute-done.12.refs_2_.refs_1_), channel_id=1, source_target_pairs={{0,4},{4,8},{8,12},{12,14},{14,10},{10,6},{6,2},{2,0},{1,5},{5,9},... | collective-permute-start | bytes 743432 | tf_op jit(solution)/shard_map/ppermute | solution.py:515
  37.1 0.8 collective-permute-start.18
  37.9 2.0 %triangle.12.refs_7_.refs_0_ = bf16[2,22,16,128]{3,2,1,0:T(8,128)(2,1)S(1)} custom-call(s32[8]{0:T(128)S(1)} %copy-done.5, bf16[22,88,128]{2,1,0:T(8,128)(2,1)S(1)} %get-tuple-element.72.refs_1_.refs_4_, bf16[11,88,128]{2,1,0:T(8,128)(2,1)S(1)} %collective-permute-done.12.refs_2_.refs_1_, bf16[11,88,128]{2,1,0:T(8,128)(2,1)S(1)} %collective-permute-done.13.refs_3_.refs_2_, ...), custom_call_target="tpu_custom_call" | custom-call | flops 1024 | bytes 1024 | tf_op jit(solution)/shard_map/triangle/pallas_call | solution.py:93
  40.6 1.5 %collective-permute-done.9.refs_2_.refs_1_ = bf16[11,88,128]{2,1,0:T(8,128)(2,1)S(1)} collective-permute-done((bf16[11,88,128]{2,1,0:T(8,128)(2,1)S(1)}, bf16[11,88,128]{2,1,0:T(8,128)(2,1)S(1)}, u32[]{:S(2)}, u32[]{:S(2)}) %collective-permute-start.9) | collective-permute-done | bytes 247840 | tf_op jit(solution)/shard_map/ppermute | solution.py:515
  42.1 1.3 %collective-permute-done.10.refs_3_.refs_2_ = bf16[11,88,128]{2,1,0:T(8,128)(2,1)S(1)} collective-permute-done((bf16[11,88,128]{2,1,0:T(8,128)(2,1)S(1)}, bf16[11,88,128]{2,1,0:T(8,128)(2,1)S(1)}, u32[]{:S(2)}, u32[]{:S(2)}) %collective-permute-start.10) | collective-permute-done | bytes 247840 | tf_op jit(solution)/shard_map/ppermute | solution.py:518
  43.3 1.9 %collective-permute-start.15 = (bf16[11,88,128]{2,1,0:T(8,128)(2,1)S(1)}, bf16[11,88,128]{2,1,0:T(8,128)(2,1)S(1)}, u32[]{:S(2)}, u32[]{:S(2)}) collective-permute-start(bf16[11,88,128]{2,1,0:T(8,128)(2,1)S(1)} %collective-permute-done.9.refs_2_.refs_1_), channel_id=1, source_target_pairs={{0,4},{4,8},{8,12},{12,14},{14,10},{10,6},{6,2},{2,0},{1,5},{5,9},... | collective-permute-start | bytes 743432 | tf_op jit(solution)/shard_map/ppermute | solution.py:515
  45.3 2.0 %triangle.13.refs_7_.refs_0_ = bf16[2,22,16,128]{3,2,1,0:T(8,128)(2,1)S(1)} custom-call(s32[8]{0:T(128)S(1)} %copy-done.5, bf16[22,88,128]{2,1,0:T(8,128)(2,1)S(1)} %get-tuple-element.72.refs_1_.refs_4_, bf16[11,88,128]{2,1,0:T(8,128)(2,1)S(1)} %collective-permute-done.9.refs_2_.refs_1_, bf16[11,88,128]{2,1,0:T(8,128)(2,1)S(1)} %collective-permute-done.10.refs_3_.refs_2_, ...), custom_call_target="tpu_custom_call" | custom-call | flops 1024 | bytes 1024 | tf_op jit(solution)/shard_map/triangle/pallas_call | solution.py:93
  48.6 2.7 %triangle.14.refs_7_.refs_0_ = bf16[2,22,16,128]{3,2,1,0:T(8,128)(2,1)S(1)} custom-call(s32[8]{0:T(128)S(1)} %copy-done.5, bf16[22,88,128]{2,1,0:T(8,128)(2,1)S(1)} %get-tuple-element.72.refs_1_.refs_4_, bf16[11,88,128]{2,1,0:T(8,128)(2,1)S(1)} %collective-permute-done.17.refs_2_.refs_1_, bf16[11,88,128]{2,1,0:T(8,128)(2,1)S(1)} %collective-permute-done.18.refs_3_.refs_2_, ...), custom_call_target="tpu_custom_call" | custom-call | flops 1024 | bytes 1024 | tf_op jit(solution)/shard_map/triangle/pallas_call | solution.py:93
  52.0 0.8 collective-permute-done.20.refs_1_
  53.4 1.7 %scatter_hop.8 = (bf16[11,88,128]{2,1,0:T(8,128)(2,1)S(1)}, bf16[11,88,128]{2,1,0:T(8,128)(2,1)S(1)}) custom-call(s32[8]{0:T(128)S(1)} %copy-done.5, bf16[22,88,128]{2,1,0:T(8,128)(2,1)S(1)} %get-tuple-element.72.refs_1_.refs_4_, bf16[2,22,16,128]{3,2,1,0:T(8,128)(2,1)S(1)} %get-tuple-element.92.refs_2_.refs_3_.refs_4_.refs_0_, ...), custom_call_target="tpu_custom_call" | custom-call | flops 1024 | bytes 1024 | tf_op jit(solution)/shard_map/scatter_hop/pallas_call | solution.py:93
  55.1 2.4 %triangle.15.refs_3_.refs_0_ = bf16[2,22,16,128]{3,2,1,0:T(8,128)(2,1)S(1)} custom-call(s32[8]{0:T(128)S(1)} %copy-done.5, bf16[22,88,128]{2,1,0:T(8,128)(2,1)S(1)} %get-tuple-element.72.refs_1_.refs_4_, bf16[11,88,128]{2,1,0:T(8,128)(2,1)S(1)} %collective-permute-done.15.refs_2_.refs_1_, bf16[11,88,128]{2,1,0:T(8,128)(2,1)S(1)} %collective-permute-done.16.refs_3_.refs_2_, ...), custom_call_target="tpu_custom_call" | custom-call | flops 1024 | bytes 1024 | tf_op jit(solution)/shard_map/triangle/pallas_call | solution.py:93
  57.7 1.5 %collective-permute-start.26 = (bf16[11,88,128]{2,1,0:T(8,128)(2,1)S(1)}, bf16[11,88,128]{2,1,0:T(8,128)(2,1)S(1)}, u32[]{:S(2)}, u32[]{:S(2)}) collective-permute-start(bf16[11,88,128]{2,1,0:T(8,128)(2,1)S(1)} %get-tuple-element.101), channel_id=1, source_target_pairs={{0,4},{4,8},{8,12},{12,14},{14,10},{10,6},{6,2},{2,0},{1,5},{5,9},... | collective-permute-start | bytes 743432 | tf_op jit(solution)/shard_map/ppermute | solution.py:515
  59.7 1.1 left_gradient.8.refs_7_.refs_3_
  61.4 1.5 %scatter_hop.9 = (bf16[11,88,128]{2,1,0:T(8,128)(2,1)S(1)}, bf16[11,88,128]{2,1,0:T(8,128)(2,1)S(1)}) custom-call(s32[8]{0:T(128)S(1)} %copy-done.5, bf16[22,88,128]{2,1,0:T(8,128)(2,1)S(1)} %get-tuple-element.72.refs_1_.refs_4_, bf16[2,22,16,128]{3,2,1,0:T(8,128)(2,1)S(1)} %get-tuple-element.94.refs_2_.refs_3_.refs_4_.refs_0_, ...), custom_call_target="tpu_custom_call" | custom-call | flops 1024 | bytes 1024 | tf_op jit(solution)/shard_map/scatter_hop/pallas_call | solution.py:93
  62.9 1.8 %collective-permute-start.24 = (bf16[11,88,128]{2,1,0:T(8,128)(2,1)S(1)}, bf16[11,88,128]{2,1,0:T(8,128)(2,1)S(1)}, u32[]{:S(2)}, u32[]{:S(2)}) collective-permute-start(bf16[11,88,128]{2,1,0:T(8,128)(2,1)S(1)} %get-tuple-element.99), channel_id=1, source_target_pairs={{0,4},{4,8},{8,12},{12,14},{14,10},{10,6},{6,2},{2,0},{1,5},{5,9},... | collective-permute-start | bytes 743432 | tf_op jit(solution)/shard_map/ppermute | solution.py:515
  65.0 1.2 left_gradient.9.refs_4_.refs_3_
  66.2 1.5 %scatter_hop.10 = (f32[11,88,128]{2,1,0:T(8,128)S(1)}, f32[11,88,128]{2,1,0:T(8,128)S(1)}) custom-call(s32[8]{0:T(128)S(1)} %copy-done.5, bf16[22,88,128]{2,1,0:T(8,128)(2,1)S(1)} %get-tuple-element.72.refs_1_.refs_4_, bf16[2,22,16,128]{3,2,1,0:T(8,128)(2,1)S(1)} %get-tuple-element.90.refs_4_.refs_2_.refs_3_.refs_0_, ...), custom_call_target="tpu_custom_call" | custom-call | flops 1024 | bytes 1024 | tf_op jit(solution)/shard_map/scatter_hop/pallas_call | solution.py:93
  67.7 1.5 %scatter_hop.11 = (f32[11,88,128]{2,1,0:T(8,128)S(1)}, f32[11,88,128]{2,1,0:T(8,128)S(1)}) custom-call(s32[8]{0:T(128)S(1)} %copy-done.5, bf16[22,88,128]{2,1,0:T(8,128)(2,1)S(1)} %get-tuple-element.72.refs_1_.refs_4_, bf16[2,22,16,128]{3,2,1,0:T(8,128)(2,1)S(1)} %get-tuple-element.91.refs_7_.refs_2_.refs_3_.refs_0_, ...), custom_call_target="tpu_custom_call" | custom-call | flops 1024 | bytes 1024 | tf_op jit(solution)/shard_map/scatter_hop/pallas_call | solution.py:93
  69.3 2.0 %collective-permute-start.30 = (bf16[11,88,128]{2,1,0:T(8,128)(2,1)S(1)}, bf16[11,88,128]{2,1,0:T(8,128)(2,1)S(1)}, u32[]{:S(2)}, u32[]{:S(2)}) collective-permute-start(bf16[11,88,128]{2,1,0:T(8,128)(2,1)S(1)} %get-tuple-element.109), channel_id=1, source_target_pairs={{0,4},{4,8},{8,12},{12,14},{14,10},{10,6},{6,2},{2,0},{1,5},{5,9},... | collective-permute-start | bytes 743432 | tf_op jit(solution)/shard_map/ppermute | solution.py:515
  71.4 1.1 collective-permute-done.23.refs_2_
  72.6 1.8 %collective-permute-start.28 = (bf16[11,88,128]{2,1,0:T(8,128)(2,1)S(1)}, bf16[11,88,128]{2,1,0:T(8,128)(2,1)S(1)}, u32[]{:S(2)}, u32[]{:S(2)}) collective-permute-start(bf16[11,88,128]{2,1,0:T(8,128)(2,1)S(1)} %get-tuple-element.107), channel_id=1, source_target_pairs={{0,4},{4,8},{8,12},{12,14},{14,10},{10,6},{6,2},{2,0},{1,5},{5,9},... | collective-permute-start | bytes 743432 | tf_op jit(solution)/shard_map/ppermute | solution.py:515
  74.7 1.2 left_gradient.10.refs_4_.refs_3_
  75.9 1.7 %scatter_hop.12 = (f32[11,88,128]{2,1,0:T(8,128)S(1)}, f32[11,88,128]{2,1,0:T(8,128)S(1)}) custom-call(s32[8]{0:T(128)S(1)} %copy-done.5, bf16[22,88,128]{2,1,0:T(8,128)(2,1)S(1)} %get-tuple-element.72.refs_1_.refs_4_, bf16[2,22,16,128]{3,2,1,0:T(8,128)(2,1)S(1)} %get-tuple-element.84.refs_4_.refs_0_.refs_2_.refs_3_, ...), custom_call_target="tpu_custom_call" | custom-call | flops 1024 | bytes 1024 | tf_op jit(solution)/shard_map/scatter_hop/pallas_call | solution.py:93
  77.6 1.5 %scatter_hop.13 = (f32[11,88,128]{2,1,0:T(8,128)S(1)}, f32[11,88,128]{2,1,0:T(8,128)S(1)}) custom-call(s32[8]{0:T(128)S(1)} %copy-done.5, bf16[22,88,128]{2,1,0:T(8,128)(2,1)S(1)} %get-tuple-element.72.refs_1_.refs_4_, bf16[2,22,16,128]{3,2,1,0:T(8,128)(2,1)S(1)} %get-tuple-element.85.refs_4_.refs_2_.refs_3_.refs_0_, ...), custom_call_target="tpu_custom_call" | custom-call | flops 1024 | bytes 1024 | tf_op jit(solution)/shard_map/scatter_hop/pallas_call | solution.py:93
  79.1 1.2 left_gradient.11.refs_4_.refs_3_
  80.4 1.7 %collective-permute-start.34 = (bf16[11,88,128]{2,1,0:T(8,128)(2,1)S(1)}, bf16[11,88,128]{2,1,0:T(8,128)(2,1)S(1)}, u32[]{:S(2)}, u32[]{:S(2)}) collective-permute-start(bf16[11,88,128]{2,1,0:T(8,128)(2,1)S(1)} %get-tuple-element.116), channel_id=1, source_target_pairs={{0,4},{4,8},{8,12},{12,14},{14,10},{10,6},{6,2},{2,0},{1,5},{5,9},... | collective-permute-start | bytes 743432 | tf_op jit(solution)/shard_map/ppermute | solution.py:515
  82.5 1.7 %collective-permute-done.27.refs_2_ = bf16[11,88,128]{2,1,0:T(8,128)(2,1)S(1)} collective-permute-done((bf16[11,88,128]{2,1,0:T(8,128)(2,1)S(1)}, bf16[11,88,128]{2,1,0:T(8,128)(2,1)S(1)}, u32[]{:S(2)}, u32[]{:S(2)}) %collective-permute-start.27) | collective-permute-done | bytes 247840 | tf_op jit(solution)/shard_map/ppermute | solution.py:518
  84.3 2.5 %collective-permute-start.32 = (bf16[11,88,128]{2,1,0:T(8,128)(2,1)S(1)}, bf16[11,88,128]{2,1,0:T(8,128)(2,1)S(1)}, u32[]{:S(2)}, u32[]{:S(2)}) collective-permute-start(bf16[11,88,128]{2,1,0:T(8,128)(2,1)S(1)} %get-tuple-element.115), channel_id=1, source_target_pairs={{0,4},{4,8},{8,12},{12,14},{14,10},{10,6},{6,2},{2,0},{1,5},{5,9},... | collective-permute-start | bytes 743432 | tf_op jit(solution)/shard_map/ppermute | solution.py:515
  86.8 1.5 %scatter_hop.14 = (f32[11,88,128]{2,1,0:T(8,128)S(1)}, f32[11,88,128]{2,1,0:T(8,128)S(1)}) custom-call(s32[8]{0:T(128)S(1)} %copy-done.5, bf16[22,88,128]{2,1,0:T(8,128)(2,1)S(1)} %get-tuple-element.72.refs_1_.refs_4_, bf16[2,22,16,128]{3,2,1,0:T(8,128)(2,1)S(1)} %get-tuple-element.78.refs_4_.refs_0_.refs_2_.refs_3_, ...), custom_call_target="tpu_custom_call" | custom-call | flops 1024 | bytes 1024 | tf_op jit(solution)/shard_map/scatter_hop/pallas_call | solution.py:93
  88.3 1.2 left_gradient.12.refs_4_.refs_3_
  89.5 1.7 %scatter_hop.15 = (f32[11,88,128]{2,1,0:T(8,128)S(1)}, f32[11,88,128]{2,1,0:T(8,128)S(1)}) custom-call(s32[8]{0:T(128)S(1)} %copy-done.5, bf16[22,88,128]{2,1,0:T(8,128)(2,1)S(1)} %get-tuple-element.72.refs_1_.refs_4_, bf16[2,22,16,128]{3,2,1,0:T(8,128)(2,1)S(1)} %get-tuple-element.79.refs_4_.refs_0_.refs_2_.refs_3_, ...), custom_call_target="tpu_custom_call" | custom-call | flops 1024 | bytes 1024 | tf_op jit(solution)/shard_map/scatter_hop/pallas_call | solution.py:93
  91.2 1.2 left_gradient.13.refs_3_.refs_4_
  92.4 1.2 left_gradient.14.refs_4_.refs_3_
  94.2 1.6 %collective-permute-start.36 = (bf16[11,88,128]{2,1,0:T(8,128)(2,1)S(1)}, bf16[11,88,128]{2,1,0:T(8,128)(2,1)S(1)}, u32[]{:S(2)}, u32[]{:S(2)}) collective-permute-start(bf16[11,88,128]{2,1,0:T(8,128)(2,1)S(1)} %get-tuple-element.129), channel_id=1, source_target_pairs={{0,4},{4,8},{8,12},{12,14},{14,10},{10,6},{6,2},{2,0},{1,5},{5,9},... | collective-permute-start | bytes 743432 | tf_op jit(solution)/shard_map/ppermute | solution.py:515
  96.3 1.2 left_gradient.15.refs_3_.refs_15_
  97.5 6.7 %output_side.1 = (bf16[22,88,128]{2,1,0:T(8,128)(2,1)}, f32[22,88,128]{2,1,0:T(8,128)S(1)}, f32[128,512]{1,0:T(8,128)S(1)}) custom-call(s32[8]{0:T(128)S(1)} %copy-done.5, bf16[22,88,128]{2,1,0:T(8,128)(2,1)S(1)} %get-tuple-element.71.refs_1_, bf16[22,88,128]{2,1,0:T(8,128)(2,1)S(1)} %copy-done.10, f32[22,88,128]{2,1,0:T(8,128)S(1)} %left_gradient.15.refs_3_.refs_15_, ...), custom_call_target="tpu_custom_call" | custom-call | flops 6600001024 | bytes 1024 | tf_op jit(solution)/shard_map/output_side/pallas_call | solution.py:93
  104.1 2.0 %right_gradient.1 = (bf16[22,88,256]{2,1,0:T(8,128)(2,1)S(1)}, bf16[64,768]{1,0:T(8,128)(2,1)S(1)}, bf16[64,768]{1,0:T(8,128)(2,1)S(1)}) custom-call(s32[8]{0:T(128)S(1)} %copy-done.5, bf16[22,88,128]{2,1,0:T(8,128)(2,1)S(1)} %get-tuple-element.71.refs_1_, bf16[128,640]{1,0:T(8,128)(2,1)S(1)} %copy-done.2, f32[128,512]{1,0:T(8,128)S(1)} %get-tuple-element.127.refs_3_, ...), custom_call_target="tpu_custom_call" | custom-call | flops 1024 | bytes 1024 | tf_op jit(solution)/shard_map/right_gradient/pallas_call | solution.py:93
  106.3 1.3 %collective-permute-done.37 = bf16[64,768]{1,0:T(8,128)(2,1)S(1)} collective-permute-done((bf16[64,768]{1,0:T(8,128)(2,1)S(1)}, bf16[64,768]{1,0:T(8,128)(2,1)S(1)}, u32[]{:S(2)}, u32[]{:S(2)}) %collective-permute-start.37) | collective-permute-done | bytes 98336 | tf_op jit(solution)/shard_map/ppermute | solution.py:77
  107.7 1.7 %collective-permute-start.39 = (bf16[64,768]{1,0:T(8,128)(2,1)S(1)}, bf16[64,768]{1,0:T(8,128)(2,1)S(1)}, u32[]{:S(2)}, u32[]{:S(2)}) collective-permute-start(bf16[64,768]{1,0:T(8,128)(2,1)S(1)} %add_convert_fusion.2), channel_id=1, source_target_pairs={{0,4},{2,6},{4,0},{6,2},{8,12},{10,14},{12,8},{14,10},{1,5},{3,7},... | collective-permute-start | bytes 294920 | tf_op jit(solution)/shard_map/ppermute | solution.py:691
  109.4 1.7 %collective-permute-start.38 = (bf16[64,768]{1,0:T(8,128)(2,1)S(1)}, bf16[64,768]{1,0:T(8,128)(2,1)S(1)}, u32[]{:S(2)}, u32[]{:S(2)}) collective-permute-start(bf16[64,768]{1,0:T(8,128)(2,1)S(1)} %add_convert_fusion.2), channel_id=1, source_target_pairs={{0,2},{2,0},{4,6},{6,4},{8,10},{10,8},{12,14},{14,12},{1,3},{3,1},... | collective-permute-start | bytes 294920 | tf_op jit(solution)/shard_map/ppermute | solution.py:691
  111.2 3.0 %collective-permute-done.40 = bf16[64,768]{1,0:T(8,128)(2,1)S(1)} collective-permute-done((bf16[64,768]{1,0:T(8,128)(2,1)S(1)}, bf16[64,768]{1,0:T(8,128)(2,1)S(1)}, u32[]{:S(2)}, u32[]{:S(2)}) %collective-permute-start.40) | collective-permute-done | bytes 98336 | tf_op jit(solution)/shard_map/ppermute | solution.py:691
  114.4 1.1 collective-permute-done.38
  115.6 1.4 %collective-permute-start.41 = (bf16[64,768]{1,0:T(8,128)(2,1)S(1)}, bf16[64,768]{1,0:T(8,128)(2,1)S(1)}, u32[]{:S(2)}, u32[]{:S(2)}) collective-permute-start(bf16[64,768]{1,0:T(8,128)(2,1)S(1)} %add_convert_fusion.1), channel_id=1, source_target_pairs={{0,8},{2,10},{4,12},{6,14},{8,0},{10,2},{12,4},{14,6},{1,9},{3,11}... | collective-permute-start | bytes 294920 | tf_op jit(solution)/shard_map/ppermute | solution.py:691
  117.0 4.1 %pair_gradient.1 = bf16[22,88,128]{2,1,0:T(8,128)(2,1)} custom-call(bf16[22,88,128]{2,1,0:T(8,128)(2,1)S(1)} %copy-done.4, bf16[22,88,256]{2,1,0:T(8,128)(2,1)S(1)} %get-tuple-element.132.refs_1_, f32[1,128]{1,0:T(1,128)S(1)} %bitcast.22, bf16[128,640]{1,0:T(8,128)(2,1)S(1)} %copy-done.2, f32[22,88,128]{2,1,0:T(8,128)S(1)} %get-tuple-element.133.refs_4_), custom_call_target="tpu_custom_call" | custom-call | flops 3300001024 | bytes 1024 | tf_op jit(solution)/shard_map/pair_gradient/pallas_call | solution.py:93
  121.0 2.3 %collective-permute-done.41 = bf16[64,768]{1,0:T(8,128)(2,1)S(1)} collective-permute-done((bf16[64,768]{1,0:T(8,128)(2,1)S(1)}, bf16[64,768]{1,0:T(8,128)(2,1)S(1)}, u32[]{:S(2)}, u32[]{:S(2)}) %collective-permute-start.41) | collective-permute-done | bytes 98336 | tf_op jit(solution)/shard_map/ppermute | solution.py:691
  123.4 1.3 %collective-permute-done.42.refs_1_ = bf16[64,768]{1,0:T(8,128)(2,1)S(1)} collective-permute-done((bf16[64,768]{1,0:T(8,128)(2,1)S(1)}, bf16[64,768]{1,0:T(8,128)(2,1)S(1)}, u32[]{:S(2)}, u32[]{:S(2)}) %collective-permute-start.42) | collective-permute-done | bytes 98336 | tf_op jit(solution)/shard_map/ppermute | solution.py:77
  (90 shorter events, 13.3 us)
Async XLA Ops:
  0.6 0.7 copy-start.5
  0.6 0.7 copy-start.8
  0.7 0.7 copy-start.9
  1.3 0.9 copy-start.1
  2.2 1.0 copy-start.3
  3.3 1.5 %copy-start.2 = (bf16[128,640]{1,0:T(8,128)(2,1)S(1)}, bf16[128,640]{1,0:T(8,128)(2,1)}, u32[]{:S(2)}) copy-start(bf16[128,640]{1,0:T(8,128)(2,1)} %refs_3_.3) | copy-start | bytes 491524
  3.3 1.5 %copy-start.10 = (bf16[22,88,128]{2,1,0:T(8,128)(2,1)S(1)}, bf16[22,88,128]{2,1,0:T(8,128)(2,1)}, u32[]{:S(2)}) copy-start(bf16[22,88,128]{2,1,0:T(8,128)(2,1)} %refs_2_.4) | copy-start | bytes 1486852
  6.2 15.9 %collective-permute-start.5 = (bf16[8,22,16,128]{3,2,1,0:T(8,128)(2,1)S(1)}, bf16[8,22,16,128]{3,2,1,0:T(8,128)(2,1)S(1)}, u32[]{:S(2)}, u32[]{:S(2)}) collective-permute-start(bf16[8,22,16,128]{3,2,1,0:T(8,128)(2,1)S(1)} %get-tuple-element.77.refs_2_.refs_6_), channel_id=1, source_target_pairs={{0,1},{1,0},{2,3},{3,2},{4,5},{5,4},{6,7},{7,6},{8,9},{9,8},{10,11... | collective-permute-start | bytes 2162696 | tf_op jit(solution)/shard_map/ppermute | solution.py:77
  6.7 9.2 %collective-permute-start = (bf16[11,88,128]{2,1,0:T(8,128)(2,1)S(1)}, bf16[11,88,128]{2,1,0:T(8,128)(2,1)S(1)}, u32[]{:S(2)}, u32[]{:S(2)}) collective-permute-start(bf16[11,88,128]{2,1,0:T(8,128)(2,1)S(1)} %get-tuple-element.73.refs_2_.refs_1_), channel_id=1, source_target_pairs={{0,4},{4,8},{8,12},{12,14},{14,10},{10,6},{6,2},{2,0},{1,5},{5,9},... | collective-permute-start | bytes 743432 | tf_op jit(solution)/shard_map/ppermute | solution.py:515
  9.3 8.8 %collective-permute-start.1 = (bf16[11,88,128]{2,1,0:T(8,128)(2,1)S(1)}, bf16[11,88,128]{2,1,0:T(8,128)(2,1)S(1)}, u32[]{:S(2)}, u32[]{:S(2)}) collective-permute-start(bf16[11,88,128]{2,1,0:T(8,128)(2,1)S(1)} %get-tuple-element.74.refs_3_.refs_2_), channel_id=1, source_target_pairs={{0,2},{4,0},{8,4},{12,8},{14,12},{10,14},{6,10},{2,6},{1,3},{5,1},... | collective-permute-start | bytes 743432 | tf_op jit(solution)/shard_map/ppermute | solution.py:518
  11.2 11.3 %copy-start = (bf16[128,128]{1,0:T(8,128)(2,1)S(1)}, bf16[128,128]{1,0:T(8,128)(2,1)}, u32[]{:S(2)}) copy-start(bf16[128,128]{1,0:T(8,128)(2,1)} %refs_5_.1) | copy-start | bytes 98308
  11.2 9.2 %collective-permute-start.8 = (bf16[2,22,16,128]{3,2,1,0:T(8,128)(2,1)S(1)}, bf16[2,22,16,128]{3,2,1,0:T(8,128)(2,1)S(1)}, u32[]{:S(2)}, u32[]{:S(2)}) collective-permute-start(bf16[2,22,16,128]{3,2,1,0:T(8,128)(2,1)S(1)} %triangle.8.refs_4_.refs_0_), channel_id=1, source_target_pairs={{0,1},{1,0},{2,3},{3,2},{4,5},{5,4},{6,7},{7,6},{8,9},{9,8},{10,11... | collective-permute-start | bytes 540680 | tf_op jit(solution)/shard_map/ppermute | solution.py:77
  11.4 12.3 %collective-permute-start.7 = (bf16[11,88,128]{2,1,0:T(8,128)(2,1)S(1)}, bf16[11,88,128]{2,1,0:T(8,128)(2,1)S(1)}, u32[]{:S(2)}, u32[]{:S(2)}) collective-permute-start(bf16[11,88,128]{2,1,0:T(8,128)(2,1)S(1)} %get-tuple-element.73.refs_2_.refs_1_), channel_id=1, source_target_pairs={{0,2},{4,0},{8,4},{12,8},{14,12},{10,14},{6,10},{2,6},{1,3},{5,1},... | collective-permute-start | bytes 743432 | tf_op jit(solution)/shard_map/ppermute | solution.py:518
  15.9 7.9 %collective-permute-start.6 = (bf16[11,88,128]{2,1,0:T(8,128)(2,1)S(1)}, bf16[11,88,128]{2,1,0:T(8,128)(2,1)S(1)}, u32[]{:S(2)}, u32[]{:S(2)}) collective-permute-start(bf16[11,88,128]{2,1,0:T(8,128)(2,1)S(1)} %get-tuple-element.74.refs_3_.refs_2_), channel_id=1, source_target_pairs={{0,4},{4,8},{8,12},{12,14},{14,10},{10,6},{6,2},{2,0},{1,5},{5,9},... | collective-permute-start | bytes 743432 | tf_op jit(solution)/shard_map/ppermute | solution.py:515
  20.4 8.4 %collective-permute-start.4 = (bf16[2,22,16,128]{3,2,1,0:T(8,128)(2,1)S(1)}, bf16[2,22,16,128]{3,2,1,0:T(8,128)(2,1)S(1)}, u32[]{:S(2)}, u32[]{:S(2)}) collective-permute-start(bf16[2,22,16,128]{3,2,1,0:T(8,128)(2,1)S(1)} %triangle.9.refs_7_.refs_0_), channel_id=1, source_target_pairs={{0,1},{1,0},{2,3},{3,2},{4,5},{5,4},{6,7},{7,6},{8,9},{9,8},{10,11... | collective-permute-start | bytes 540680 | tf_op jit(solution)/shard_map/ppermute | solution.py:77
  20.5 8.9 %collective-permute-start.2 = (bf16[11,88,128]{2,1,0:T(8,128)(2,1)S(1)}, bf16[11,88,128]{2,1,0:T(8,128)(2,1)S(1)}, u32[]{:S(2)}, u32[]{:S(2)}) collective-permute-start(bf16[11,88,128]{2,1,0:T(8,128)(2,1)S(1)} %collective-permute-done.refs_2_.refs_1_), channel_id=1, source_target_pairs={{0,4},{4,8},{8,12},{12,14},{14,10},{10,6},{6,2},{2,0},{1,5},{5,9},... | collective-permute-start | bytes 743432 | tf_op jit(solution)/shard_map/ppermute | solution.py:515
  22.1 8.8 %collective-permute-start.3 = (bf16[11,88,128]{2,1,0:T(8,128)(2,1)S(1)}, bf16[11,88,128]{2,1,0:T(8,128)(2,1)S(1)}, u32[]{:S(2)}, u32[]{:S(2)}) collective-permute-start(bf16[11,88,128]{2,1,0:T(8,128)(2,1)S(1)} %collective-permute-done.1.refs_3_.refs_2_), channel_id=1, source_target_pairs={{0,2},{4,0},{8,4},{12,8},{14,12},{10,14},{6,10},{2,6},{1,3},{5,1},... | collective-permute-start | bytes 743432 | tf_op jit(solution)/shard_map/ppermute | solution.py:518
  22.5 0.7 copy-start.6
  22.5 0.7 copy-start.7
  23.8 12.1 %collective-permute-start.12 = (bf16[11,88,128]{2,1,0:T(8,128)(2,1)S(1)}, bf16[11,88,128]{2,1,0:T(8,128)(2,1)S(1)}, u32[]{:S(2)}, u32[]{:S(2)}) collective-permute-start(bf16[11,88,128]{2,1,0:T(8,128)(2,1)S(1)} %collective-permute-done.6.refs_2_.refs_1_), channel_id=1, source_target_pairs={{0,4},{4,8},{8,12},{12,14},{14,10},{10,6},{6,2},{2,0},{1,5},{5,9},... | collective-permute-start | bytes 743432 | tf_op jit(solution)/shard_map/ppermute | solution.py:515
  25.4 10.4 %collective-permute-start.13 = (bf16[11,88,128]{2,1,0:T(8,128)(2,1)S(1)}, bf16[11,88,128]{2,1,0:T(8,128)(2,1)S(1)}, u32[]{:S(2)}, u32[]{:S(2)}) collective-permute-start(bf16[11,88,128]{2,1,0:T(8,128)(2,1)S(1)} %collective-permute-done.7.refs_3_.refs_2_), channel_id=1, source_target_pairs={{0,2},{4,0},{8,4},{12,8},{14,12},{10,14},{6,10},{2,6},{1,3},{5,1},... | collective-permute-start | bytes 743432 | tf_op jit(solution)/shard_map/ppermute | solution.py:518
  28.7 5.7 %collective-permute-start.14 = (bf16[2,22,16,128]{3,2,1,0:T(8,128)(2,1)S(1)}, bf16[2,22,16,128]{3,2,1,0:T(8,128)(2,1)S(1)}, u32[]{:S(2)}, u32[]{:S(2)}) collective-permute-start(bf16[2,22,16,128]{3,2,1,0:T(8,128)(2,1)S(1)} %triangle.10.refs_7_.refs_0_), channel_id=1, source_target_pairs={{0,1},{1,0},{2,3},{3,2},{4,5},{5,4},{6,7},{7,6},{8,9},{9,8},{10,11... | collective-permute-start | bytes 540680 | tf_op jit(solution)/shard_map/ppermute | solution.py:77
  33.1 6.8 %collective-permute-start.11 = (bf16[2,22,16,128]{3,2,1,0:T(8,128)(2,1)S(1)}, bf16[2,22,16,128]{3,2,1,0:T(8,128)(2,1)S(1)}, u32[]{:S(2)}, u32[]{:S(2)}) collective-permute-start(bf16[2,22,16,128]{3,2,1,0:T(8,128)(2,1)S(1)} %triangle.11.refs_7_.refs_0_), channel_id=1, source_target_pairs={{0,1},{1,0},{2,3},{3,2},{4,5},{5,4},{6,7},{7,6},{8,9},{9,8},{10,11... | collective-permute-start | bytes 540680 | tf_op jit(solution)/shard_map/ppermute | solution.py:77
  33.2 8.9 %collective-permute-start.9 = (bf16[11,88,128]{2,1,0:T(8,128)(2,1)S(1)}, bf16[11,88,128]{2,1,0:T(8,128)(2,1)S(1)}, u32[]{:S(2)}, u32[]{:S(2)}) collective-permute-start(bf16[11,88,128]{2,1,0:T(8,128)(2,1)S(1)} %collective-permute-done.2.refs_2_.refs_1_), channel_id=1, source_target_pairs={{0,4},{4,8},{8,12},{12,14},{14,10},{10,6},{6,2},{2,0},{1,5},{5,9},... | collective-permute-start | bytes 743432 | tf_op jit(solution)/shard_map/ppermute | solution.py:515
  34.5 8.8 %collective-permute-start.10 = (bf16[11,88,128]{2,1,0:T(8,128)(2,1)S(1)}, bf16[11,88,128]{2,1,0:T(8,128)(2,1)S(1)}, u32[]{:S(2)}, u32[]{:S(2)}) collective-permute-start(bf16[11,88,128]{2,1,0:T(8,128)(2,1)S(1)} %collective-permute-done.3.refs_3_.refs_2_), channel_id=1, source_target_pairs={{0,2},{4,0},{8,4},{12,8},{14,12},{10,14},{6,10},{2,6},{1,3},{5,1},... | collective-permute-start | bytes 743432 | tf_op jit(solution)/shard_map/ppermute | solution.py:518
  35.9 12.2 %collective-permute-start.17 = (bf16[11,88,128]{2,1,0:T(8,128)(2,1)S(1)}, bf16[11,88,128]{2,1,0:T(8,128)(2,1)S(1)}, u32[]{:S(2)}, u32[]{:S(2)}) collective-permute-start(bf16[11,88,128]{2,1,0:T(8,128)(2,1)S(1)} %collective-permute-done.12.refs_2_.refs_1_), channel_id=1, source_target_pairs={{0,4},{4,8},{8,12},{12,14},{14,10},{10,6},{6,2},{2,0},{1,5},{5,9},... | collective-permute-start | bytes 743432 | tf_op jit(solution)/shard_map/ppermute | solution.py:515
  37.1 11.5 %collective-permute-start.18 = (bf16[11,88,128]{2,1,0:T(8,128)(2,1)S(1)}, bf16[11,88,128]{2,1,0:T(8,128)(2,1)S(1)}, u32[]{:S(2)}, u32[]{:S(2)}) collective-permute-start(bf16[11,88,128]{2,1,0:T(8,128)(2,1)S(1)} %collective-permute-done.13.refs_3_.refs_2_), channel_id=1, source_target_pairs={{0,2},{4,0},{8,4},{12,8},{14,12},{10,14},{6,10},{2,6},{1,3},{5,1},... | collective-permute-start | bytes 743432 | tf_op jit(solution)/shard_map/ppermute | solution.py:518
  40.0 7.4 %collective-permute-start.19 = (bf16[2,22,16,128]{3,2,1,0:T(8,128)(2,1)S(1)}, bf16[2,22,16,128]{3,2,1,0:T(8,128)(2,1)S(1)}, u32[]{:S(2)}, u32[]{:S(2)}) collective-permute-start(bf16[2,22,16,128]{3,2,1,0:T(8,128)(2,1)S(1)} %triangle.12.refs_7_.refs_0_), channel_id=1, source_target_pairs={{0,1},{1,0},{2,3},{3,2},{4,5},{5,4},{6,7},{7,6},{8,9},{9,8},{10,11... | collective-permute-start | bytes 540680 | tf_op jit(solution)/shard_map/ppermute | solution.py:77
  43.3 11.8 %collective-permute-start.15 = (bf16[11,88,128]{2,1,0:T(8,128)(2,1)S(1)}, bf16[11,88,128]{2,1,0:T(8,128)(2,1)S(1)}, u32[]{:S(2)}, u32[]{:S(2)}) collective-permute-start(bf16[11,88,128]{2,1,0:T(8,128)(2,1)S(1)} %collective-permute-done.9.refs_2_.refs_1_), channel_id=1, source_target_pairs={{0,4},{4,8},{8,12},{12,14},{14,10},{10,6},{6,2},{2,0},{1,5},{5,9},... | collective-permute-start | bytes 743432 | tf_op jit(solution)/shard_map/ppermute | solution.py:515
  45.2 9.9 %collective-permute-start.16 = (bf16[11,88,128]{2,1,0:T(8,128)(2,1)S(1)}, bf16[11,88,128]{2,1,0:T(8,128)(2,1)S(1)}, u32[]{:S(2)}, u32[]{:S(2)}) collective-permute-start(bf16[11,88,128]{2,1,0:T(8,128)(2,1)S(1)} %collective-permute-done.10.refs_3_.refs_2_), channel_id=1, source_target_pairs={{0,2},{4,0},{8,4},{12,8},{14,12},{10,14},{6,10},{2,6},{1,3},{5,1},... | collective-permute-start | bytes 743432 | tf_op jit(solution)/shard_map/ppermute | solution.py:518
  47.4 4.0 %collective-permute-start.21 = (bf16[2,22,16,128]{3,2,1,0:T(8,128)(2,1)S(1)}, bf16[2,22,16,128]{3,2,1,0:T(8,128)(2,1)S(1)}, u32[]{:S(2)}, u32[]{:S(2)}) collective-permute-start(bf16[2,22,16,128]{3,2,1,0:T(8,128)(2,1)S(1)} %triangle.13.refs_7_.refs_0_), channel_id=1, source_target_pairs={{0,1},{1,0},{2,3},{3,2},{4,5},{5,4},{6,7},{7,6},{8,9},{9,8},{10,11... | collective-permute-start | bytes 540680 | tf_op jit(solution)/shard_map/ppermute | solution.py:77
  51.3 1.5 %collective-permute-start.20 = (bf16[2,22,16,128]{3,2,1,0:T(8,128)(2,1)S(1)}, bf16[2,22,16,128]{3,2,1,0:T(8,128)(2,1)S(1)}, u32[]{:S(2)}, u32[]{:S(2)}) collective-permute-start(bf16[2,22,16,128]{3,2,1,0:T(8,128)(2,1)S(1)} %triangle.14.refs_7_.refs_0_), channel_id=1, source_target_pairs={{0,1},{1,0},{2,3},{3,2},{4,5},{5,4},{6,7},{7,6},{8,9},{9,8},{10,11... | collective-permute-start | bytes 540680 | tf_op jit(solution)/shard_map/ppermute | solution.py:77
  57.5 3.4 %collective-permute-start.22 = (bf16[2,22,16,128]{3,2,1,0:T(8,128)(2,1)S(1)}, bf16[2,22,16,128]{3,2,1,0:T(8,128)(2,1)S(1)}, u32[]{:S(2)}, u32[]{:S(2)}) collective-permute-start(bf16[2,22,16,128]{3,2,1,0:T(8,128)(2,1)S(1)} %triangle.15.refs_3_.refs_0_), channel_id=1, source_target_pairs={{0,1},{1,0},{2,3},{3,2},{4,5},{5,4},{6,7},{7,6},{8,9},{9,8},{10,11... | collective-permute-start | bytes 540680 | tf_op jit(solution)/shard_map/ppermute | solution.py:77
  57.7 11.5 %collective-permute-start.26 = (bf16[11,88,128]{2,1,0:T(8,128)(2,1)S(1)}, bf16[11,88,128]{2,1,0:T(8,128)(2,1)S(1)}, u32[]{:S(2)}, u32[]{:S(2)}) collective-permute-start(bf16[11,88,128]{2,1,0:T(8,128)(2,1)S(1)} %get-tuple-element.101), channel_id=1, source_target_pairs={{0,4},{4,8},{8,12},{12,14},{14,10},{10,6},{6,2},{2,0},{1,5},{5,9},... | collective-permute-start | bytes 743432 | tf_op jit(solution)/shard_map/ppermute | solution.py:515
  59.2 10.0 %collective-permute-start.25 = (bf16[11,88,128]{2,1,0:T(8,128)(2,1)S(1)}, bf16[11,88,128]{2,1,0:T(8,128)(2,1)S(1)}, u32[]{:S(2)}, u32[]{:S(2)}) collective-permute-start(bf16[11,88,128]{2,1,0:T(8,128)(2,1)S(1)} %get-tuple-element.93.refs_4_), channel_id=1, source_target_pairs={{0,2},{4,0},{8,4},{12,8},{14,12},{10,14},{6,10},{2,6},{1,3},{5,1},... | collective-permute-start | bytes 743432 | tf_op jit(solution)/shard_map/ppermute | solution.py:518
  62.9 8.5 %collective-permute-start.24 = (bf16[11,88,128]{2,1,0:T(8,128)(2,1)S(1)}, bf16[11,88,128]{2,1,0:T(8,128)(2,1)S(1)}, u32[]{:S(2)}, u32[]{:S(2)}) collective-permute-start(bf16[11,88,128]{2,1,0:T(8,128)(2,1)S(1)} %get-tuple-element.99), channel_id=1, source_target_pairs={{0,4},{4,8},{8,12},{12,14},{14,10},{10,6},{6,2},{2,0},{1,5},{5,9},... | collective-permute-start | bytes 743432 | tf_op jit(solution)/shard_map/ppermute | solution.py:515
  64.7 7.8 %collective-permute-start.23 = (bf16[11,88,128]{2,1,0:T(8,128)(2,1)S(1)}, bf16[11,88,128]{2,1,0:T(8,128)(2,1)S(1)}, u32[]{:S(2)}, u32[]{:S(2)}) collective-permute-start(bf16[11,88,128]{2,1,0:T(8,128)(2,1)S(1)} %get-tuple-element.95.refs_4_), channel_id=1, source_target_pairs={{0,2},{4,0},{8,4},{12,8},{14,12},{10,14},{6,10},{2,6},{1,3},{5,1},... | collective-permute-start | bytes 743432 | tf_op jit(solution)/shard_map/ppermute | solution.py:518
  69.3 11.0 %collective-permute-start.30 = (bf16[11,88,128]{2,1,0:T(8,128)(2,1)S(1)}, bf16[11,88,128]{2,1,0:T(8,128)(2,1)S(1)}, u32[]{:S(2)}, u32[]{:S(2)}) collective-permute-start(bf16[11,88,128]{2,1,0:T(8,128)(2,1)S(1)} %get-tuple-element.109), channel_id=1, source_target_pairs={{0,4},{4,8},{8,12},{12,14},{14,10},{10,6},{6,2},{2,0},{1,5},{5,9},... | collective-permute-start | bytes 743432 | tf_op jit(solution)/shard_map/ppermute | solution.py:515
  71.3 9.0 %collective-permute-start.29 = (bf16[11,88,128]{2,1,0:T(8,128)(2,1)S(1)}, bf16[11,88,128]{2,1,0:T(8,128)(2,1)S(1)}, u32[]{:S(2)}, u32[]{:S(2)}) collective-permute-start(bf16[11,88,128]{2,1,0:T(8,128)(2,1)S(1)} %get-tuple-element.102.refs_4_), channel_id=1, source_target_pairs={{0,2},{4,0},{8,4},{12,8},{14,12},{10,14},{6,10},{2,6},{1,3},{5,1},... | collective-permute-start | bytes 743432 | tf_op jit(solution)/shard_map/ppermute | solution.py:518
  72.6 9.9 %collective-permute-start.28 = (bf16[11,88,128]{2,1,0:T(8,128)(2,1)S(1)}, bf16[11,88,128]{2,1,0:T(8,128)(2,1)S(1)}, u32[]{:S(2)}, u32[]{:S(2)}) collective-permute-start(bf16[11,88,128]{2,1,0:T(8,128)(2,1)S(1)} %get-tuple-element.107), channel_id=1, source_target_pairs={{0,4},{4,8},{8,12},{12,14},{14,10},{10,6},{6,2},{2,0},{1,5},{5,9},... | collective-permute-start | bytes 743432 | tf_op jit(solution)/shard_map/ppermute | solution.py:515
  74.4 9.8 %collective-permute-start.27 = (bf16[11,88,128]{2,1,0:T(8,128)(2,1)S(1)}, bf16[11,88,128]{2,1,0:T(8,128)(2,1)S(1)}, u32[]{:S(2)}, u32[]{:S(2)}) collective-permute-start(bf16[11,88,128]{2,1,0:T(8,128)(2,1)S(1)} %get-tuple-element.103.refs_4_), channel_id=1, source_target_pairs={{0,2},{4,0},{8,4},{12,8},{14,12},{10,14},{6,10},{2,6},{1,3},{5,1},... | collective-permute-start | bytes 743432 | tf_op jit(solution)/shard_map/ppermute | solution.py:518
  80.4 13.2 %collective-permute-start.34 = (bf16[11,88,128]{2,1,0:T(8,128)(2,1)S(1)}, bf16[11,88,128]{2,1,0:T(8,128)(2,1)S(1)}, u32[]{:S(2)}, u32[]{:S(2)}) collective-permute-start(bf16[11,88,128]{2,1,0:T(8,128)(2,1)S(1)} %get-tuple-element.116), channel_id=1, source_target_pairs={{0,4},{4,8},{8,12},{12,14},{14,10},{10,6},{6,2},{2,0},{1,5},{5,9},... | collective-permute-start | bytes 743432 | tf_op jit(solution)/shard_map/ppermute | solution.py:515
  82.1 11.5 %collective-permute-start.33 = (bf16[11,88,128]{2,1,0:T(8,128)(2,1)S(1)}, bf16[11,88,128]{2,1,0:T(8,128)(2,1)S(1)}, u32[]{:S(2)}, u32[]{:S(2)}) collective-permute-start(bf16[11,88,128]{2,1,0:T(8,128)(2,1)S(1)} %get-tuple-element.110.refs_4_), channel_id=1, source_target_pairs={{0,2},{4,0},{8,4},{12,8},{14,12},{10,14},{6,10},{2,6},{1,3},{5,1},... | collective-permute-start | bytes 743432 | tf_op jit(solution)/shard_map/ppermute | solution.py:518
  84.3 9.3 %collective-permute-start.32 = (bf16[11,88,128]{2,1,0:T(8,128)(2,1)S(1)}, bf16[11,88,128]{2,1,0:T(8,128)(2,1)S(1)}, u32[]{:S(2)}, u32[]{:S(2)}) collective-permute-start(bf16[11,88,128]{2,1,0:T(8,128)(2,1)S(1)} %get-tuple-element.115), channel_id=1, source_target_pairs={{0,4},{4,8},{8,12},{12,14},{14,10},{10,6},{6,2},{2,0},{1,5},{5,9},... | collective-permute-start | bytes 743432 | tf_op jit(solution)/shard_map/ppermute | solution.py:515
  86.8 7.3 %collective-permute-start.31 = (bf16[11,88,128]{2,1,0:T(8,128)(2,1)S(1)}, bf16[11,88,128]{2,1,0:T(8,128)(2,1)S(1)}, u32[]{:S(2)}, u32[]{:S(2)}) collective-permute-start(bf16[11,88,128]{2,1,0:T(8,128)(2,1)S(1)} %get-tuple-element.111.refs_4_), channel_id=1, source_target_pairs={{0,2},{4,0},{8,4},{12,8},{14,12},{10,14},{6,10},{2,6},{1,3},{5,1},... | collective-permute-start | bytes 743432 | tf_op jit(solution)/shard_map/ppermute | solution.py:518
  94.2 9.9 %collective-permute-start.36 = (bf16[11,88,128]{2,1,0:T(8,128)(2,1)S(1)}, bf16[11,88,128]{2,1,0:T(8,128)(2,1)S(1)}, u32[]{:S(2)}, u32[]{:S(2)}) collective-permute-start(bf16[11,88,128]{2,1,0:T(8,128)(2,1)S(1)} %get-tuple-element.129), channel_id=1, source_target_pairs={{0,4},{4,8},{8,12},{12,14},{14,10},{10,6},{6,2},{2,0},{1,5},{5,9},... | collective-permute-start | bytes 743432 | tf_op jit(solution)/shard_map/ppermute | solution.py:515
  95.8 8.3 %collective-permute-start.35 = (bf16[11,88,128]{2,1,0:T(8,128)(2,1)S(1)}, bf16[11,88,128]{2,1,0:T(8,128)(2,1)S(1)}, u32[]{:S(2)}, u32[]{:S(2)}) collective-permute-start(bf16[11,88,128]{2,1,0:T(8,128)(2,1)S(1)} %get-tuple-element.117.refs_4_), channel_id=1, source_target_pairs={{0,2},{4,0},{8,4},{12,8},{14,12},{10,14},{6,10},{2,6},{1,3},{5,1},... | collective-permute-start | bytes 743432 | tf_op jit(solution)/shard_map/ppermute | solution.py:518
  106.2 10.8 %copy-start.4 = (bf16[22,88,128]{2,1,0:T(8,128)(2,1)S(1)}, bf16[22,88,128]{2,1,0:T(8,128)(2,1)}, u32[]{:S(2)}) copy-start(bf16[22,88,128]{2,1,0:T(8,128)(2,1)} %refs_0_.41) | copy-start | bytes 1486852
  106.2 1.4 %collective-permute-start.37 = (bf16[64,768]{1,0:T(8,128)(2,1)S(1)}, bf16[64,768]{1,0:T(8,128)(2,1)S(1)}, u32[]{:S(2)}, u32[]{:S(2)}) collective-permute-start(bf16[64,768]{1,0:T(8,128)(2,1)S(1)} %get-tuple-element.131), channel_id=1, source_target_pairs={{0,1},{1,0},{2,3},{3,2},{4,5},{5,4},{6,7},{7,6},{8,9},{9,8},{10,11... | collective-permute-start | bytes 294920 | tf_op jit(solution)/shard_map/ppermute | solution.py:77
  107.6 6.6 %collective-permute-start.40 = (bf16[64,768]{1,0:T(8,128)(2,1)S(1)}, bf16[64,768]{1,0:T(8,128)(2,1)S(1)}, u32[]{:S(2)}, u32[]{:S(2)}) collective-permute-start(bf16[64,768]{1,0:T(8,128)(2,1)S(1)} %add_convert_fusion.2), channel_id=1, source_target_pairs={{0,6},{2,4},{4,2},{6,0},{8,14},{10,12},{12,10},{14,8},{1,7},{3,5},... | collective-permute-start | bytes 294920 | tf_op jit(solution)/shard_map/ppermute | solution.py:691
  107.7 6.7 %collective-permute-start.39 = (bf16[64,768]{1,0:T(8,128)(2,1)S(1)}, bf16[64,768]{1,0:T(8,128)(2,1)S(1)}, u32[]{:S(2)}, u32[]{:S(2)}) collective-permute-start(bf16[64,768]{1,0:T(8,128)(2,1)S(1)} %add_convert_fusion.2), channel_id=1, source_target_pairs={{0,4},{2,6},{4,0},{6,2},{8,12},{10,14},{12,8},{14,10},{1,5},{3,7},... | collective-permute-start | bytes 294920 | tf_op jit(solution)/shard_map/ppermute | solution.py:691
  109.4 6.1 %collective-permute-start.38 = (bf16[64,768]{1,0:T(8,128)(2,1)S(1)}, bf16[64,768]{1,0:T(8,128)(2,1)S(1)}, u32[]{:S(2)}, u32[]{:S(2)}) collective-permute-start(bf16[64,768]{1,0:T(8,128)(2,1)S(1)} %add_convert_fusion.2), channel_id=1, source_target_pairs={{0,2},{2,0},{4,6},{6,4},{8,10},{10,8},{12,14},{14,12},{1,3},{3,1},... | collective-permute-start | bytes 294920 | tf_op jit(solution)/shard_map/ppermute | solution.py:691
  115.6 7.7 %collective-permute-start.41 = (bf16[64,768]{1,0:T(8,128)(2,1)S(1)}, bf16[64,768]{1,0:T(8,128)(2,1)S(1)}, u32[]{:S(2)}, u32[]{:S(2)}) collective-permute-start(bf16[64,768]{1,0:T(8,128)(2,1)S(1)} %add_convert_fusion.1), channel_id=1, source_target_pairs={{0,8},{2,10},{4,12},{6,14},{8,0},{10,2},{12,4},{14,6},{1,9},{3,11}... | collective-permute-start | bytes 294920 | tf_op jit(solution)/shard_map/ppermute | solution.py:691
  123.3 1.4 %collective-permute-start.42 = (bf16[64,768]{1,0:T(8,128)(2,1)S(1)}, bf16[64,768]{1,0:T(8,128)(2,1)S(1)}, u32[]{:S(2)}, u32[]{:S(2)}) collective-permute-start(bf16[64,768]{1,0:T(8,128)(2,1)S(1)} %add_convert_fusion.refs_0_), channel_id=1, source_target_pairs={{0,1},{1,0},{2,3},{3,2},{4,5},{5,4},{6,7},{7,6},{8,9},{9,8},{10,11... | collective-permute-start | bytes 294920 | tf_op jit(solution)/shard_map/ppermute | solution.py:77

commit v4 on v3

--- a/solution.py
+++ b/solution.py
@@ -559,7 +559,6 @@
         partials.append(
             triangle(row_count, slot, halves[s], chain_lengths, left, groups[s], padded, last)
         )
-        others.append(swap_col(partials[s]))
         last[:] = [partials[s]]
 
     def normal(s):
@@ -645,8 +644,12 @@
             normal(s - 1)
             send(hops - 1, 1)
         triangles(s)
+        sent = partials[s]
         if 0 < s < steps - 1:
             normal(s - 1)
+        if 2 < s < steps - 2:
+            sent, _ = lax.optimization_barrier((sent, last[0]))
+        others.append(swap_col(sent))
     waiting = list(range(steps))
 
     def add_lefts(count):
@@ -656,7 +659,7 @@
     add_lefts(1)
     normal(steps - 1)
     send(hops, 0)
-    add_lefts(1)
+    add_lefts(2)
     prepare(hops - 2, 1)
     prepare(hops - 1, 0)
     for s in range(hops - 1, 0, -1):

time: 126 us -> 126 us (level)
  starting transfers between devices: 39.1 us -> 41 us
    ppermute x4, starting transfers between devices: 4.92 us -> 7.34 us  [from_row(): return lax.ppermute(mine, 'row', [(r, r ^ apart) for r in range(row_count)])]
    ppermute x14, starting transfers between devices: 25 us -> 23.2 us  [ahead(): return lax.ppermute(x, 'row', forward)]
    ppermute x4, waiting for transfers between devices: 6.65 us -> 5.27 us  [from_row(): return lax.ppermute(mine, 'row', [(r, r ^ apart) for r in range(row_count)])]
    ppermute x14, waiting for transfers between devices: 7.22 us -> 8.49 us  [behind(): return lax.ppermute(x, 'row', backward)]
  transfers between devices with their start and end apart: 43 -> 43, of which waited for: 16 -> 17; matrix products, arithmetic and copies ran while one was open for 0% -> 0% of each run, Pallas kernels for 42% -> 42%
where the time goes in v4:
time: 126 us
  Pallas kernels  60.6 us (48%)
  starting transfers between devices  41 us (33%)
  waiting for transfers between devices  19.9 us (16%)
  local copies, waits for them, and re-layouts  3.3 us (3%)
    pallas_call x43, Pallas kernels, call(): pl.pallas_call(body, out_shape=list(outs), in_specs=list(specs) + [ANY] *...  60.6 us
    ppermute x14, starting transfers between devices, ahead(): return lax.ppermute(x, 'row', forward)  23.2 us
    ppermute x14, starting transfers between devices, behind(): return lax.ppermute(x, 'row', backward)  8.63 us
    ppermute x14, waiting for transfers between devices, behind(): return lax.ppermute(x, 'row', backward)  8.49 us
    ppermute x4, starting transfers between devices, from_row(): return lax.ppermute(mine, 'row', [(r, r ^ apart) for r in range(row_count)])  7.34 us
    ppermute x4, waiting for transfers between devices, from_row(): return lax.ppermute(mine, 'row', [(r, r ^ apart) for r in range(row_count)])  5.27 us
    unnamed x22, local copies, waits for them, and re-layouts  3.3 us
    ppermute x11, waiting for transfers between devices, swap_col(): return lax.ppermute(x, 'col', [(0, 1), (1, 0)])  3.23 us
  transfers between devices with their start and end apart: 43, of which 17 were waited for; matrix products, arithmetic and copies ran while one was open for 0% of the time, Pallas kernels for 42%

profile of v4, /device:TPU:0, one launch (start us, length us, event | category | flops | bytes accessed | tf_op | source)
XLA Modules:
  0.0 126.1 jit_solution(11255821959501521732)
XLA Ops:
  1.3 0.9 copy-done.1
  2.2 1.0 copy-done.3
  3.3 1.5 %input_side.1 = (bf16[11,88,128]{2,1,0:T(8,128)(2,1)S(1)}, bf16[11,88,128]{2,1,0:T(8,128)(2,1)S(1)}, bf16[22,88,128]{2,1,0:T(8,128)(2,1)S(1)}) custom-call(s32[8]{0:T(128)S(1)} %copy-done.5, bf16[22,88,128]{2,1,0:T(8,128)(2,1)S(1)} %copy-done.3, f32[1,128]{1,0:T(1,128)S(1)} %bitcast.21, f32[1,128]{1,0:T(1,128)S(1)} %bitcast.20, bf16[128,640]{1,0:T(8,128)(2,1)S(1)} %copy-done.1), custom_call_target="tpu_custom_call" | custom-call | flops 1024 | bytes 1024 | tf_op jit(solution)/shard_map/input_side/pallas_call | solution.py:93
  4.8 1.4 %left_side.1 = (bf16[22,88,128]{2,1,0:T(8,128)(2,1)S(1)}, bf16[8,22,16,128]{3,2,1,0:T(8,128)(2,1)S(1)}) custom-call(s32[8]{0:T(128)S(1)} %copy-done.5, bf16[22,88,128]{2,1,0:T(8,128)(2,1)S(1)} %get-tuple-element.74.refs_1_, bf16[22,88,128]{2,1,0:T(8,128)(2,1)S(1)} %copy-done.10, bf16[128,640]{1,0:T(8,128)(2,1)S(1)} %copy-done.2), custom_call_target="tpu_custom_call" | custom-call | flops 4400001024 | bytes 1024 | tf_op jit(solution)/shard_map/left_side/pallas_call | solution.py:93
  6.7 2.6 %collective-permute-start = (bf16[11,88,128]{2,1,0:T(8,128)(2,1)S(1)}, bf16[11,88,128]{2,1,0:T(8,128)(2,1)S(1)}, u32[]{:S(2)}, u32[]{:S(2)}) collective-permute-start(bf16[11,88,128]{2,1,0:T(8,128)(2,1)S(1)} %get-tuple-element.76.refs_2_.refs_1_), channel_id=1, source_target_pairs={{0,4},{4,8},{8,12},{12,14},{14,10},{10,6},{6,2},{2,0},{1,5},{5,9},... | collective-permute-start | bytes 743432 | tf_op jit(solution)/shard_map/ppermute | solution.py:515
  9.4 2.7 %triangle.8.refs_4_.refs_0_ = bf16[2,22,16,128]{3,2,1,0:T(8,128)(2,1)S(1)} custom-call(s32[8]{0:T(128)S(1)} %copy-done.5, bf16[22,88,128]{2,1,0:T(8,128)(2,1)S(1)} %get-tuple-element.75.refs_1_.refs_4_, bf16[11,88,128]{2,1,0:T(8,128)(2,1)S(1)} %get-tuple-element.76.refs_2_.refs_1_, bf16[11,88,128]{2,1,0:T(8,128)(2,1)S(1)} %get-tuple-element.77.refs_3_.refs_2_, ...), custom_call_target="tpu_custom_call" | custom-call | flops 1024 | bytes 1024 | tf_op jit(solution)/shard_map/triangle/pallas_call | solution.py:93
  12.3 1.5 %collective-permute-start.7 = (bf16[11,88,128]{2,1,0:T(8,128)(2,1)S(1)}, bf16[11,88,128]{2,1,0:T(8,128)(2,1)S(1)}, u32[]{:S(2)}, u32[]{:S(2)}) collective-permute-start(bf16[11,88,128]{2,1,0:T(8,128)(2,1)S(1)} %get-tuple-element.76.refs_2_.refs_1_), channel_id=1, source_target_pairs={{0,2},{4,0},{8,4},{12,8},{14,12},{10,14},{6,10},{2,6},{1,3},{5,1},... | collective-permute-start | bytes 743432 | tf_op jit(solution)/shard_map/ppermute | solution.py:518
  13.8 2.1 %collective-permute-done.refs_2_.refs_1_ = bf16[11,88,128]{2,1,0:T(8,128)(2,1)S(1)} collective-permute-done((bf16[11,88,128]{2,1,0:T(8,128)(2,1)S(1)}, bf16[11,88,128]{2,1,0:T(8,128)(2,1)S(1)}, u32[]{:S(2)}, u32[]{:S(2)}) %collective-permute-start) | collective-permute-done | bytes 247840 | tf_op jit(solution)/shard_map/ppermute | solution.py:515
  15.9 1.8 %collective-permute-start.6 = (bf16[11,88,128]{2,1,0:T(8,128)(2,1)S(1)}, bf16[11,88,128]{2,1,0:T(8,128)(2,1)S(1)}, u32[]{:S(2)}, u32[]{:S(2)}) collective-permute-start(bf16[11,88,128]{2,1,0:T(8,128)(2,1)S(1)} %get-tuple-element.77.refs_3_.refs_2_), channel_id=1, source_target_pairs={{0,4},{4,8},{8,12},{12,14},{14,10},{10,6},{6,2},{2,0},{1,5},{5,9},... | collective-permute-start | bytes 743432 | tf_op jit(solution)/shard_map/ppermute | solution.py:515
  18.2 2.2 %triangle.9.refs_7_.refs_0_ = bf16[2,22,16,128]{3,2,1,0:T(8,128)(2,1)S(1)} custom-call(s32[8]{0:T(128)S(1)} %copy-done.5, bf16[22,88,128]{2,1,0:T(8,128)(2,1)S(1)} %get-tuple-element.75.refs_1_.refs_4_, bf16[11,88,128]{2,1,0:T(8,128)(2,1)S(1)} %collective-permute-done.refs_2_.refs_1_, bf16[11,88,128]{2,1,0:T(8,128)(2,1)S(1)} %collective-permute-done.1.refs_3_.refs_2_, ...), custom_call_target="tpu_custom_call" | custom-call | flops 1024 | bytes 1024 | tf_op jit(solution)/shard_map/triangle/pallas_call | solution.py:93
  20.4 1.3 %collective-permute-start.2 = (bf16[11,88,128]{2,1,0:T(8,128)(2,1)S(1)}, bf16[11,88,128]{2,1,0:T(8,128)(2,1)S(1)}, u32[]{:S(2)}, u32[]{:S(2)}) collective-permute-start(bf16[11,88,128]{2,1,0:T(8,128)(2,1)S(1)} %collective-permute-done.refs_2_.refs_1_), channel_id=1, source_target_pairs={{0,4},{4,8},{8,12},{12,14},{14,10},{10,6},{6,2},{2,0},{1,5},{5,9},... | collective-permute-start | bytes 743432 | tf_op jit(solution)/shard_map/ppermute | solution.py:515
  21.7 0.8 collective-permute-start.3
  22.5 0.6 copy-done.6
  23.8 2.4 %triangle.10.refs_7_.refs_0_ = bf16[2,22,16,128]{3,2,1,0:T(8,128)(2,1)S(1)} custom-call(s32[8]{0:T(128)S(1)} %copy-done.5, bf16[22,88,128]{2,1,0:T(8,128)(2,1)S(1)} %get-tuple-element.75.refs_1_.refs_4_, bf16[11,88,128]{2,1,0:T(8,128)(2,1)S(1)} %collective-permute-done.6.refs_2_.refs_1_, bf16[11,88,128]{2,1,0:T(8,128)(2,1)S(1)} %collective-permute-done.7.refs_3_.refs_2_, ...), custom_call_target="tpu_custom_call" | custom-call | flops 1024 | bytes 1024 | tf_op jit(solution)/shard_map/triangle/pallas_call | solution.py:93
  26.2 2.3 %collective-permute-start.13 = (bf16[11,88,128]{2,1,0:T(8,128)(2,1)S(1)}, bf16[11,88,128]{2,1,0:T(8,128)(2,1)S(1)}, u32[]{:S(2)}, u32[]{:S(2)}) collective-permute-start(bf16[11,88,128]{2,1,0:T(8,128)(2,1)S(1)} %collective-permute-done.6.refs_2_.refs_1_), channel_id=1, source_target_pairs={{0,4},{4,8},{8,12},{12,14},{14,10},{10,6},{6,2},{2,0},{1,5},{5,9},... | collective-permute-start | bytes 743432 | tf_op jit(solution)/shard_map/ppermute | solution.py:515
  29.1 1.3 %collective-permute-done.3.refs_3_.refs_2_ = bf16[11,88,128]{2,1,0:T(8,128)(2,1)S(1)} collective-permute-done((bf16[11,88,128]{2,1,0:T(8,128)(2,1)S(1)}, bf16[11,88,128]{2,1,0:T(8,128)(2,1)S(1)}, u32[]{:S(2)}, u32[]{:S(2)}) %collective-permute-start.3) | collective-permute-done | bytes 247840 | tf_op jit(solution)/shard_map/ppermute | solution.py:518
  30.3 1.8 %triangle.11.refs_7_.refs_0_ = bf16[2,22,16,128]{3,2,1,0:T(8,128)(2,1)S(1)} custom-call(s32[8]{0:T(128)S(1)} %copy-done.5, bf16[22,88,128]{2,1,0:T(8,128)(2,1)S(1)} %get-tuple-element.75.refs_1_.refs_4_, bf16[11,88,128]{2,1,0:T(8,128)(2,1)S(1)} %collective-permute-done.2.refs_2_.refs_1_, bf16[11,88,128]{2,1,0:T(8,128)(2,1)S(1)} %collective-permute-done.3.refs_3_.refs_2_, ...), custom_call_target="tpu_custom_call" | custom-call | flops 1024 | bytes 1024 | tf_op jit(solution)/shard_map/triangle/pallas_call | solution.py:93
  32.8 2.5 %collective-permute-start.9 = (bf16[11,88,128]{2,1,0:T(8,128)(2,1)S(1)}, bf16[11,88,128]{2,1,0:T(8,128)(2,1)S(1)}, u32[]{:S(2)}, u32[]{:S(2)}) collective-permute-start(bf16[11,88,128]{2,1,0:T(8,128)(2,1)S(1)} %collective-permute-done.2.refs_2_.refs_1_), channel_id=1, source_target_pairs={{0,4},{4,8},{8,12},{12,14},{14,10},{10,6},{6,2},{2,0},{1,5},{5,9},... | collective-permute-start | bytes 743432 | tf_op jit(solution)/shard_map/ppermute | solution.py:515
  35.3 1.3 %collective-permute-done.14.refs_3_.refs_2_ = bf16[11,88,128]{2,1,0:T(8,128)(2,1)S(1)} collective-permute-done((bf16[11,88,128]{2,1,0:T(8,128)(2,1)S(1)}, bf16[11,88,128]{2,1,0:T(8,128)(2,1)S(1)}, u32[]{:S(2)}, u32[]{:S(2)}) %collective-permute-start.14) | collective-permute-done | bytes 247840 | tf_op jit(solution)/shard_map/ppermute | solution.py:518
  36.6 1.1 collective-permute-start.17
  37.7 0.9 collective-permute-start.18
  38.6 2.0 %triangle.12.refs_7_.refs_0_ = bf16[2,22,16,128]{3,2,1,0:T(8,128)(2,1)S(1)} custom-call(s32[8]{0:T(128)S(1)} %copy-done.5, bf16[22,88,128]{2,1,0:T(8,128)(2,1)S(1)} %get-tuple-element.75.refs_1_.refs_4_, bf16[11,88,128]{2,1,0:T(8,128)(2,1)S(1)} %collective-permute-done.13.refs_2_.refs_1_, bf16[11,88,128]{2,1,0:T(8,128)(2,1)S(1)} %collective-permute-done.14.refs_3_.refs_2_, ...), custom_call_target="tpu_custom_call" | custom-call | flops 1024 | bytes 1024 | tf_op jit(solution)/shard_map/triangle/pallas_call | solution.py:93
  41.7 2.5 %collective-permute-done.10.refs_3_.refs_2_ = bf16[11,88,128]{2,1,0:T(8,128)(2,1)S(1)} collective-permute-done((bf16[11,88,128]{2,1,0:T(8,128)(2,1)S(1)}, bf16[11,88,128]{2,1,0:T(8,128)(2,1)S(1)}, u32[]{:S(2)}, u32[]{:S(2)}) %collective-permute-start.10) | collective-permute-done | bytes 247840 | tf_op jit(solution)/shard_map/ppermute | solution.py:518
  44.6 1.5 %collective-permute-start.16 = (bf16[11,88,128]{2,1,0:T(8,128)(2,1)S(1)}, bf16[11,88,128]{2,1,0:T(8,128)(2,1)S(1)}, u32[]{:S(2)}, u32[]{:S(2)}) collective-permute-start(bf16[11,88,128]{2,1,0:T(8,128)(2,1)S(1)} %collective-permute-done.10.refs_3_.refs_2_), channel_id=1, source_target_pairs={{0,2},{4,0},{8,4},{12,8},{14,12},{10,14},{6,10},{2,6},{1,3},{5,1},... | collective-permute-start | bytes 743432 | tf_op jit(solution)/shard_map/ppermute | solution.py:518
  46.2 2.4 %triangle.13.refs_7_.refs_0_ = bf16[2,22,16,128]{3,2,1,0:T(8,128)(2,1)S(1)} custom-call(s32[8]{0:T(128)S(1)} %copy-done.5, bf16[22,88,128]{2,1,0:T(8,128)(2,1)S(1)} %get-tuple-element.75.refs_1_.refs_4_, bf16[11,88,128]{2,1,0:T(8,128)(2,1)S(1)} %collective-permute-done.9.refs_2_.refs_1_, bf16[11,88,128]{2,1,0:T(8,128)(2,1)S(1)} %collective-permute-done.10.refs_3_.refs_2_, ...), custom_call_target="tpu_custom_call" | custom-call | flops 1024 | bytes 1024 | tf_op jit(solution)/shard_map/triangle/pallas_call | solution.py:93
  49.4 1.7 %triangle.14.refs_7_.refs_0_ = bf16[2,22,16,128]{3,2,1,0:T(8,128)(2,1)S(1)} custom-call(s32[8]{0:T(128)S(1)} %copy-done.5, bf16[22,88,128]{2,1,0:T(8,128)(2,1)S(1)} %get-tuple-element.75.refs_1_.refs_4_, bf16[11,88,128]{2,1,0:T(8,128)(2,1)S(1)} %collective-permute-done.17.refs_2_.refs_1_, bf16[11,88,128]{2,1,0:T(8,128)(2,1)S(1)} %collective-permute-done.18.refs_3_.refs_2_, ...), custom_call_target="tpu_custom_call" | custom-call | flops 1024 | bytes 1024 | tf_op jit(solution)/shard_map/triangle/pallas_call | solution.py:93
  52.0 0.6 collective-permute-done.20.refs_1_
  53.2 1.2 scatter_hop.8
  54.4 2.2 %triangle.15.refs_3_.refs_0_ = bf16[2,22,16,128]{3,2,1,0:T(8,128)(2,1)S(1)} custom-call(s32[8]{0:T(128)S(1)} %copy-done.5, bf16[22,88,128]{2,1,0:T(8,128)(2,1)S(1)} %get-tuple-element.75.refs_1_.refs_4_, bf16[11,88,128]{2,1,0:T(8,128)(2,1)S(1)} %collective-permute-done.15.refs_2_.refs_1_, bf16[11,88,128]{2,1,0:T(8,128)(2,1)S(1)} %collective-permute-done.16.refs_3_.refs_2_, ...), custom_call_target="tpu_custom_call" | custom-call | flops 1024 | bytes 1024 | tf_op jit(solution)/shard_map/triangle/pallas_call | solution.py:93
  57.4 1.5 %collective-permute-start.25 = (bf16[11,88,128]{2,1,0:T(8,128)(2,1)S(1)}, bf16[11,88,128]{2,1,0:T(8,128)(2,1)S(1)}, u32[]{:S(2)}, u32[]{:S(2)}) collective-permute-start(bf16[11,88,128]{2,1,0:T(8,128)(2,1)S(1)} %get-tuple-element.99.refs_4_), channel_id=1, source_target_pairs={{0,2},{4,0},{8,4},{12,8},{14,12},{10,14},{6,10},{2,6},{1,3},{5,1},... | collective-permute-start | bytes 743432 | tf_op jit(solution)/shard_map/ppermute | solution.py:518
  58.9 1.1 left_gradient.8.refs_7_.refs_3_
  60.6 1.5 %scatter_hop.9 = (bf16[11,88,128]{2,1,0:T(8,128)(2,1)S(1)}, bf16[11,88,128]{2,1,0:T(8,128)(2,1)S(1)}) custom-call(s32[8]{0:T(128)S(1)} %copy-done.5, bf16[22,88,128]{2,1,0:T(8,128)(2,1)S(1)} %get-tuple-element.75.refs_1_.refs_4_, bf16[2,22,16,128]{3,2,1,0:T(8,128)(2,1)S(1)} %get-tuple-element.100.refs_2_.refs_3_.refs_4_.refs_0_, ...), custom_call_target="tpu_custom_call" | custom-call | flops 1024 | bytes 1024 | tf_op jit(solution)/shard_map/scatter_hop/pallas_call | solution.py:93
  62.5 1.7 %collective-permute-start.23 = (bf16[11,88,128]{2,1,0:T(8,128)(2,1)S(1)}, bf16[11,88,128]{2,1,0:T(8,128)(2,1)S(1)}, u32[]{:S(2)}, u32[]{:S(2)}) collective-permute-start(bf16[11,88,128]{2,1,0:T(8,128)(2,1)S(1)} %get-tuple-element.101.refs_4_), channel_id=1, source_target_pairs={{0,2},{4,0},{8,4},{12,8},{14,12},{10,14},{6,10},{2,6},{1,3},{5,1},... | collective-permute-start | bytes 743432 | tf_op jit(solution)/shard_map/ppermute | solution.py:518
  64.2 1.2 left_gradient.9.refs_3_.refs_4_
  65.4 1.2 left_gradient.10.refs_4_.refs_3_
  66.6 1.5 %scatter_hop.10 = (f32[11,88,128]{2,1,0:T(8,128)S(1)}, f32[11,88,128]{2,1,0:T(8,128)S(1)}) custom-call(s32[8]{0:T(128)S(1)} %copy-done.5, bf16[22,88,128]{2,1,0:T(8,128)(2,1)S(1)} %get-tuple-element.75.refs_1_.refs_4_, bf16[2,22,16,128]{3,2,1,0:T(8,128)(2,1)S(1)} %get-tuple-element.95.refs_4_.refs_2_.refs_3_.refs_0_, ...), custom_call_target="tpu_custom_call" | custom-call | flops 1024 | bytes 1024 | tf_op jit(solution)/shard_map/scatter_hop/pallas_call | solution.py:93
  68.1 1.7 %scatter_hop.11 = (f32[11,88,128]{2,1,0:T(8,128)S(1)}, f32[11,88,128]{2,1,0:T(8,128)S(1)}) custom-call(s32[8]{0:T(128)S(1)} %copy-done.5, bf16[22,88,128]{2,1,0:T(8,128)(2,1)S(1)} %get-tuple-element.75.refs_1_.refs_4_, bf16[2,22,16,128]{3,2,1,0:T(8,128)(2,1)S(1)} %get-tuple-element.97.refs_7_.refs_2_.refs_3_.refs_0_, ...), custom_call_target="tpu_custom_call" | custom-call | flops 1024 | bytes 1024 | tf_op jit(solution)/shard_map/scatter_hop/pallas_call | solution.py:93
  69.9 1.6 %collective-permute-start.30 = (bf16[11,88,128]{2,1,0:T(8,128)(2,1)S(1)}, bf16[11,88,128]{2,1,0:T(8,128)(2,1)S(1)}, u32[]{:S(2)}, u32[]{:S(2)}) collective-permute-start(bf16[11,88,128]{2,1,0:T(8,128)(2,1)S(1)} %get-tuple-element.115), channel_id=1, source_target_pairs={{0,4},{4,8},{8,12},{12,14},{14,10},{10,6},{6,2},{2,0},{1,5},{5,9},... | collective-permute-start | bytes 743432 | tf_op jit(solution)/shard_map/ppermute | solution.py:515
  72.1 2.1 %collective-permute-start.28 = (bf16[11,88,128]{2,1,0:T(8,128)(2,1)S(1)}, bf16[11,88,128]{2,1,0:T(8,128)(2,1)S(1)}, u32[]{:S(2)}, u32[]{:S(2)}) collective-permute-start(bf16[11,88,128]{2,1,0:T(8,128)(2,1)S(1)} %get-tuple-element.113), channel_id=1, source_target_pairs={{0,4},{4,8},{8,12},{12,14},{14,10},{10,6},{6,2},{2,0},{1,5},{5,9},... | collective-permute-start | bytes 743432 | tf_op jit(solution)/shard_map/ppermute | solution.py:515
  74.2 1.2 left_gradient.11.refs_4_.refs_3_
  75.4 1.7 %scatter_hop.12 = (f32[11,88,128]{2,1,0:T(8,128)S(1)}, f32[11,88,128]{2,1,0:T(8,128)S(1)}) custom-call(s32[8]{0:T(128)S(1)} %copy-done.5, bf16[22,88,128]{2,1,0:T(8,128)(2,1)S(1)} %get-tuple-element.75.refs_1_.refs_4_, bf16[2,22,16,128]{3,2,1,0:T(8,128)(2,1)S(1)} %get-tuple-element.85.refs_4_.refs_0_.refs_2_.refs_3_, ...), custom_call_target="tpu_custom_call" | custom-call | flops 1024 | bytes 1024 | tf_op jit(solution)/shard_map/scatter_hop/pallas_call | solution.py:93
  77.1 1.5 %scatter_hop.13 = (f32[11,88,128]{2,1,0:T(8,128)S(1)}, f32[11,88,128]{2,1,0:T(8,128)S(1)}) custom-call(s32[8]{0:T(128)S(1)} %copy-done.5, bf16[22,88,128]{2,1,0:T(8,128)(2,1)S(1)} %get-tuple-element.75.refs_1_.refs_4_, bf16[2,22,16,128]{3,2,1,0:T(8,128)(2,1)S(1)} %get-tuple-element.89.refs_4_.refs_0_.refs_2_.refs_3_, ...), custom_call_target="tpu_custom_call" | custom-call | flops 1024 | bytes 1024 | tf_op jit(solution)/shard_map/scatter_hop/pallas_call | solution.py:93
  78.6 1.2 left_gradient.12.refs_4_.refs_3_
  80.5 2.1 %collective-permute-start.34 = (bf16[11,88,128]{2,1,0:T(8,128)(2,1)S(1)}, bf16[11,88,128]{2,1,0:T(8,128)(2,1)S(1)}, u32[]{:S(2)}, u32[]{:S(2)}) collective-permute-start(bf16[11,88,128]{2,1,0:T(8,128)(2,1)S(1)} %get-tuple-element.130), channel_id=1, source_target_pairs={{0,4},{4,8},{8,12},{12,14},{14,10},{10,6},{6,2},{2,0},{1,5},{5,9},... | collective-permute-start | bytes 743432 | tf_op jit(solution)/shard_map/ppermute | solution.py:515
  83.1 2.1 %collective-permute-done.27.refs_2_ = bf16[11,88,128]{2,1,0:T(8,128)(2,1)S(1)} collective-permute-done((bf16[11,88,128]{2,1,0:T(8,128)(2,1)S(1)}, bf16[11,88,128]{2,1,0:T(8,128)(2,1)S(1)}, u32[]{:S(2)}, u32[]{:S(2)}) %collective-permute-start.27) | collective-permute-done | bytes 247840 | tf_op jit(solution)/shard_map/ppermute | solution.py:518
  85.3 2.6 %collective-permute-start.32 = (bf16[11,88,128]{2,1,0:T(8,128)(2,1)S(1)}, bf16[11,88,128]{2,1,0:T(8,128)(2,1)S(1)}, u32[]{:S(2)}, u32[]{:S(2)}) collective-permute-start(bf16[11,88,128]{2,1,0:T(8,128)(2,1)S(1)} %get-tuple-element.129), channel_id=1, source_target_pairs={{0,4},{4,8},{8,12},{12,14},{14,10},{10,6},{6,2},{2,0},{1,5},{5,9},... | collective-permute-start | bytes 743432 | tf_op jit(solution)/shard_map/ppermute | solution.py:515
  87.8 1.7 %scatter_hop.14 = (f32[11,88,128]{2,1,0:T(8,128)S(1)}, f32[11,88,128]{2,1,0:T(8,128)S(1)}) custom-call(s32[8]{0:T(128)S(1)} %copy-done.5, bf16[22,88,128]{2,1,0:T(8,128)(2,1)S(1)} %get-tuple-element.75.refs_1_.refs_4_, bf16[2,22,16,128]{3,2,1,0:T(8,128)(2,1)S(1)} %get-tuple-element.81.refs_4_.refs_0_.refs_2_.refs_3_, ...), custom_call_target="tpu_custom_call" | custom-call | flops 1024 | bytes 1024 | tf_op jit(solution)/shard_map/scatter_hop/pallas_call | solution.py:93
  89.5 1.2 left_gradient.13.refs_4_.refs_3_
  90.7 1.7 %scatter_hop.15 = (f32[11,88,128]{2,1,0:T(8,128)S(1)}, f32[11,88,128]{2,1,0:T(8,128)S(1)}) custom-call(s32[8]{0:T(128)S(1)} %copy-done.5, bf16[22,88,128]{2,1,0:T(8,128)(2,1)S(1)} %get-tuple-element.75.refs_1_.refs_4_, bf16[2,22,16,128]{3,2,1,0:T(8,128)(2,1)S(1)} %get-tuple-element.82.refs_4_.refs_0_.refs_2_.refs_3_, ...), custom_call_target="tpu_custom_call" | custom-call | flops 1024 | bytes 1024 | tf_op jit(solution)/shard_map/scatter_hop/pallas_call | solution.py:93
  92.5 1.2 left_gradient.14.refs_3_.refs_4_
  93.6 1.2 left_gradient.15.refs_4_.refs_3_
  95.0 2.0 %collective-permute-start.36 = (bf16[11,88,128]{2,1,0:T(8,128)(2,1)S(1)}, bf16[11,88,128]{2,1,0:T(8,128)(2,1)S(1)}, u32[]{:S(2)}, u32[]{:S(2)}) collective-permute-start(bf16[11,88,128]{2,1,0:T(8,128)(2,1)S(1)} %get-tuple-element.135), channel_id=1, source_target_pairs={{0,4},{4,8},{8,12},{12,14},{14,10},{10,6},{6,2},{2,0},{1,5},{5,9},... | collective-permute-start | bytes 743432 | tf_op jit(solution)/shard_map/ppermute | solution.py:515
  97.1 6.6 %output_side.1 = (bf16[22,88,128]{2,1,0:T(8,128)(2,1)}, f32[22,88,128]{2,1,0:T(8,128)S(1)}, f32[128,512]{1,0:T(8,128)S(1)}) custom-call(s32[8]{0:T(128)S(1)} %copy-done.5, bf16[22,88,128]{2,1,0:T(8,128)(2,1)S(1)} %get-tuple-element.74.refs_1_, bf16[22,88,128]{2,1,0:T(8,128)(2,1)S(1)} %copy-done.10, f32[22,88,128]{2,1,0:T(8,128)S(1)} %left_gradient.15.refs_4_.refs_3_, ...), custom_call_target="tpu_custom_call" | custom-call | flops 6600001024 | bytes 1024 | tf_op jit(solution)/shard_map/output_side/pallas_call | solution.py:93
  103.7 2.0 %right_gradient.1 = (bf16[22,88,256]{2,1,0:T(8,128)(2,1)S(1)}, bf16[64,768]{1,0:T(8,128)(2,1)S(1)}, bf16[64,768]{1,0:T(8,128)(2,1)S(1)}) custom-call(s32[8]{0:T(128)S(1)} %copy-done.5, bf16[22,88,128]{2,1,0:T(8,128)(2,1)S(1)} %get-tuple-element.74.refs_1_, bf16[128,640]{1,0:T(8,128)(2,1)S(1)} %copy-done.2, f32[128,512]{1,0:T(8,128)S(1)} %get-tuple-element.133.refs_3_, ...), custom_call_target="tpu_custom_call" | custom-call | flops 1024 | bytes 1024 | tf_op jit(solution)/shard_map/right_gradient/pallas_call | solution.py:93
  105.8 1.3 %collective-permute-done.37 = bf16[64,768]{1,0:T(8,128)(2,1)S(1)} collective-permute-done((bf16[64,768]{1,0:T(8,128)(2,1)S(1)}, bf16[64,768]{1,0:T(8,128)(2,1)S(1)}, u32[]{:S(2)}, u32[]{:S(2)}) %collective-permute-start.37) | collective-permute-done | bytes 98336 | tf_op jit(solution)/shard_map/ppermute | solution.py:77
  107.7 1.7 %collective-permute-start.39 = (bf16[64,768]{1,0:T(8,128)(2,1)S(1)}, bf16[64,768]{1,0:T(8,128)(2,1)S(1)}, u32[]{:S(2)}, u32[]{:S(2)}) collective-permute-start(bf16[64,768]{1,0:T(8,128)(2,1)S(1)} %add_convert_fusion.2), channel_id=1, source_target_pairs={{0,4},{2,6},{4,0},{6,2},{8,12},{10,14},{12,8},{14,10},{1,5},{3,7},... | collective-permute-start | bytes 294920 | tf_op jit(solution)/shard_map/ppermute | solution.py:694
  109.5 1.4 %collective-permute-start.38 = (bf16[64,768]{1,0:T(8,128)(2,1)S(1)}, bf16[64,768]{1,0:T(8,128)(2,1)S(1)}, u32[]{:S(2)}, u32[]{:S(2)}) collective-permute-start(bf16[64,768]{1,0:T(8,128)(2,1)S(1)} %add_convert_fusion.2), channel_id=1, source_target_pairs={{0,2},{2,0},{4,6},{6,4},{8,10},{10,8},{12,14},{14,12},{1,3},{3,1},... | collective-permute-start | bytes 294920 | tf_op jit(solution)/shard_map/ppermute | solution.py:694
  110.8 2.4 %collective-permute-done.40 = bf16[64,768]{1,0:T(8,128)(2,1)S(1)} collective-permute-done((bf16[64,768]{1,0:T(8,128)(2,1)S(1)}, bf16[64,768]{1,0:T(8,128)(2,1)S(1)}, u32[]{:S(2)}, u32[]{:S(2)}) %collective-permute-start.40) | collective-permute-done | bytes 98336 | tf_op jit(solution)/shard_map/ppermute | solution.py:694
  113.2 1.4 %collective-permute-done.39 = bf16[64,768]{1,0:T(8,128)(2,1)S(1)} collective-permute-done((bf16[64,768]{1,0:T(8,128)(2,1)S(1)}, bf16[64,768]{1,0:T(8,128)(2,1)S(1)}, u32[]{:S(2)}, u32[]{:S(2)}) %collective-permute-start.39) | collective-permute-done | bytes 98336 | tf_op jit(solution)/shard_map/ppermute | solution.py:694
  115.1 3.7 %collective-permute-start.41 = (bf16[64,768]{1,0:T(8,128)(2,1)S(1)}, bf16[64,768]{1,0:T(8,128)(2,1)S(1)}, u32[]{:S(2)}, u32[]{:S(2)}) collective-permute-start(bf16[64,768]{1,0:T(8,128)(2,1)S(1)} %add_convert_fusion.1), channel_id=1, source_target_pairs={{0,8},{2,10},{4,12},{6,14},{8,0},{10,2},{12,4},{14,6},{1,9},{3,11}... | collective-permute-start | bytes 294920 | tf_op jit(solution)/shard_map/ppermute | solution.py:694
  118.8 4.1 %pair_gradient.1 = bf16[22,88,128]{2,1,0:T(8,128)(2,1)} custom-call(bf16[22,88,128]{2,1,0:T(8,128)(2,1)S(1)} %copy-done.4, bf16[22,88,256]{2,1,0:T(8,128)(2,1)S(1)} %get-tuple-element.138.refs_1_, f32[1,128]{1,0:T(1,128)S(1)} %bitcast.22, bf16[128,640]{1,0:T(8,128)(2,1)S(1)} %copy-done.2, f32[22,88,128]{2,1,0:T(8,128)S(1)} %get-tuple-element.139.refs_4_), custom_call_target="tpu_custom_call" | custom-call | flops 3300001024 | bytes 1024 | tf_op jit(solution)/shard_map/pair_gradient/pallas_call | solution.py:93
  122.9 1.0 collective-permute-done.41
  124.0 1.3 %collective-permute-done.42.refs_1_ = bf16[64,768]{1,0:T(8,128)(2,1)S(1)} collective-permute-done((bf16[64,768]{1,0:T(8,128)(2,1)S(1)}, bf16[64,768]{1,0:T(8,128)(2,1)S(1)}, u32[]{:S(2)}, u32[]{:S(2)}) %collective-permute-start.42) | collective-permute-done | bytes 98336 | tf_op jit(solution)/shard_map/ppermute | solution.py:77
  125.3 0.8 weight_gradients.1
  (90 shorter events, 12.9 us)
Async XLA Ops:
  0.6 0.7 copy-start.5
  0.6 0.7 copy-start.8
  0.7 0.7 copy-start.9
  1.3 0.9 copy-start.1
  2.2 1.0 copy-start.3
  3.3 1.5 %copy-start.2 = (bf16[128,640]{1,0:T(8,128)(2,1)S(1)}, bf16[128,640]{1,0:T(8,128)(2,1)}, u32[]{:S(2)}) copy-start(bf16[128,640]{1,0:T(8,128)(2,1)} %refs_3_.3) | copy-start | bytes 491524
  3.3 1.5 %copy-start.10 = (bf16[22,88,128]{2,1,0:T(8,128)(2,1)S(1)}, bf16[22,88,128]{2,1,0:T(8,128)(2,1)}, u32[]{:S(2)}) copy-start(bf16[22,88,128]{2,1,0:T(8,128)(2,1)} %refs_2_.4) | copy-start | bytes 1486852
  6.2 15.6 %collective-permute-start.5 = (bf16[8,22,16,128]{3,2,1,0:T(8,128)(2,1)S(1)}, bf16[8,22,16,128]{3,2,1,0:T(8,128)(2,1)S(1)}, u32[]{:S(2)}, u32[]{:S(2)}) collective-permute-start(bf16[8,22,16,128]{3,2,1,0:T(8,128)(2,1)S(1)} %get-tuple-element.80.refs_2_.refs_6_), channel_id=1, source_target_pairs={{0,1},{1,0},{2,3},{3,2},{4,5},{5,4},{6,7},{7,6},{8,9},{9,8},{10,11... | collective-permute-start | bytes 2162696 | tf_op jit(solution)/shard_map/ppermute | solution.py:77
  6.7 9.2 %collective-permute-start = (bf16[11,88,128]{2,1,0:T(8,128)(2,1)S(1)}, bf16[11,88,128]{2,1,0:T(8,128)(2,1)S(1)}, u32[]{:S(2)}, u32[]{:S(2)}) collective-permute-start(bf16[11,88,128]{2,1,0:T(8,128)(2,1)S(1)} %get-tuple-element.76.refs_2_.refs_1_), channel_id=1, source_target_pairs={{0,4},{4,8},{8,12},{12,14},{14,10},{10,6},{6,2},{2,0},{1,5},{5,9},... | collective-permute-start | bytes 743432 | tf_op jit(solution)/shard_map/ppermute | solution.py:515
  9.3 8.8 %collective-permute-start.1 = (bf16[11,88,128]{2,1,0:T(8,128)(2,1)S(1)}, bf16[11,88,128]{2,1,0:T(8,128)(2,1)S(1)}, u32[]{:S(2)}, u32[]{:S(2)}) collective-permute-start(bf16[11,88,128]{2,1,0:T(8,128)(2,1)S(1)} %get-tuple-element.77.refs_3_.refs_2_), channel_id=1, source_target_pairs={{0,2},{4,0},{8,4},{12,8},{14,12},{10,14},{6,10},{2,6},{1,3},{5,1},... | collective-permute-start | bytes 743432 | tf_op jit(solution)/shard_map/ppermute | solution.py:518
  12.1 10.5 %copy-start = (bf16[128,128]{1,0:T(8,128)(2,1)S(1)}, bf16[128,128]{1,0:T(8,128)(2,1)}, u32[]{:S(2)}) copy-start(bf16[128,128]{1,0:T(8,128)(2,1)} %refs_5_.1) | copy-start | bytes 98308
  12.1 8.4 %collective-permute-start.8 = (bf16[2,22,16,128]{3,2,1,0:T(8,128)(2,1)S(1)}, bf16[2,22,16,128]{3,2,1,0:T(8,128)(2,1)S(1)}, u32[]{:S(2)}, u32[]{:S(2)}) collective-permute-start(bf16[2,22,16,128]{3,2,1,0:T(8,128)(2,1)S(1)} %triangle.8.refs_4_.refs_0_), channel_id=1, source_target_pairs={{0,1},{1,0},{2,3},{3,2},{4,5},{5,4},{6,7},{7,6},{8,9},{9,8},{10,11... | collective-permute-start | bytes 540680 | tf_op jit(solution)/shard_map/ppermute | solution.py:77
  12.3 11.5 %collective-permute-start.7 = (bf16[11,88,128]{2,1,0:T(8,128)(2,1)S(1)}, bf16[11,88,128]{2,1,0:T(8,128)(2,1)S(1)}, u32[]{:S(2)}, u32[]{:S(2)}) collective-permute-start(bf16[11,88,128]{2,1,0:T(8,128)(2,1)S(1)} %get-tuple-element.76.refs_2_.refs_1_), channel_id=1, source_target_pairs={{0,2},{4,0},{8,4},{12,8},{14,12},{10,14},{6,10},{2,6},{1,3},{5,1},... | collective-permute-start | bytes 743432 | tf_op jit(solution)/shard_map/ppermute | solution.py:518
  15.9 7.9 %collective-permute-start.6 = (bf16[11,88,128]{2,1,0:T(8,128)(2,1)S(1)}, bf16[11,88,128]{2,1,0:T(8,128)(2,1)S(1)}, u32[]{:S(2)}, u32[]{:S(2)}) collective-permute-start(bf16[11,88,128]{2,1,0:T(8,128)(2,1)S(1)} %get-tuple-element.77.refs_3_.refs_2_), channel_id=1, source_target_pairs={{0,4},{4,8},{8,12},{12,14},{14,10},{10,6},{6,2},{2,0},{1,5},{5,9},... | collective-permute-start | bytes 743432 | tf_op jit(solution)/shard_map/ppermute | solution.py:515
  20.4 8.1 %collective-permute-start.4 = (bf16[2,22,16,128]{3,2,1,0:T(8,128)(2,1)S(1)}, bf16[2,22,16,128]{3,2,1,0:T(8,128)(2,1)S(1)}, u32[]{:S(2)}, u32[]{:S(2)}) collective-permute-start(bf16[2,22,16,128]{3,2,1,0:T(8,128)(2,1)S(1)} %triangle.9.refs_7_.refs_0_), channel_id=1, source_target_pairs={{0,1},{1,0},{2,3},{3,2},{4,5},{5,4},{6,7},{7,6},{8,9},{9,8},{10,11... | collective-permute-start | bytes 540680 | tf_op jit(solution)/shard_map/ppermute | solution.py:77
  20.4 8.6 %collective-permute-start.2 = (bf16[11,88,128]{2,1,0:T(8,128)(2,1)S(1)}, bf16[11,88,128]{2,1,0:T(8,128)(2,1)S(1)}, u32[]{:S(2)}, u32[]{:S(2)}) collective-permute-start(bf16[11,88,128]{2,1,0:T(8,128)(2,1)S(1)} %collective-permute-done.refs_2_.refs_1_), channel_id=1, source_target_pairs={{0,4},{4,8},{8,12},{12,14},{14,10},{10,6},{6,2},{2,0},{1,5},{5,9},... | collective-permute-start | bytes 743432 | tf_op jit(solution)/shard_map/ppermute | solution.py:515
  21.7 8.6 %collective-permute-start.3 = (bf16[11,88,128]{2,1,0:T(8,128)(2,1)S(1)}, bf16[11,88,128]{2,1,0:T(8,128)(2,1)S(1)}, u32[]{:S(2)}, u32[]{:S(2)}) collective-permute-start(bf16[11,88,128]{2,1,0:T(8,128)(2,1)S(1)} %collective-permute-done.1.refs_3_.refs_2_), channel_id=1, source_target_pairs={{0,2},{4,0},{8,4},{12,8},{14,12},{10,14},{6,10},{2,6},{1,3},{5,1},... | collective-permute-start | bytes 743432 | tf_op jit(solution)/shard_map/ppermute | solution.py:518
  22.5 0.7 copy-start.6
  22.5 0.7 copy-start.7
  26.1 6.0 %collective-permute-start.11 = (bf16[2,22,16,128]{3,2,1,0:T(8,128)(2,1)S(1)}, bf16[2,22,16,128]{3,2,1,0:T(8,128)(2,1)S(1)}, u32[]{:S(2)}, u32[]{:S(2)}) collective-permute-start(bf16[2,22,16,128]{3,2,1,0:T(8,128)(2,1)S(1)} %triangle.10.refs_7_.refs_0_), channel_id=1, source_target_pairs={{0,1},{1,0},{2,3},{3,2},{4,5},{5,4},{6,7},{7,6},{8,9},{9,8},{10,11... | collective-permute-start | bytes 540680 | tf_op jit(solution)/shard_map/ppermute | solution.py:77
  26.2 9.1 %collective-permute-start.13 = (bf16[11,88,128]{2,1,0:T(8,128)(2,1)S(1)}, bf16[11,88,128]{2,1,0:T(8,128)(2,1)S(1)}, u32[]{:S(2)}, u32[]{:S(2)}) collective-permute-start(bf16[11,88,128]{2,1,0:T(8,128)(2,1)S(1)} %collective-permute-done.6.refs_2_.refs_1_), channel_id=1, source_target_pairs={{0,4},{4,8},{8,12},{12,14},{14,10},{10,6},{6,2},{2,0},{1,5},{5,9},... | collective-permute-start | bytes 743432 | tf_op jit(solution)/shard_map/ppermute | solution.py:515
  28.5 8.1 %collective-permute-start.14 = (bf16[11,88,128]{2,1,0:T(8,128)(2,1)S(1)}, bf16[11,88,128]{2,1,0:T(8,128)(2,1)S(1)}, u32[]{:S(2)}, u32[]{:S(2)}) collective-permute-start(bf16[11,88,128]{2,1,0:T(8,128)(2,1)S(1)} %collective-permute-done.7.refs_3_.refs_2_), channel_id=1, source_target_pairs={{0,2},{4,0},{8,4},{12,8},{14,12},{10,14},{6,10},{2,6},{1,3},{5,1},... | collective-permute-start | bytes 743432 | tf_op jit(solution)/shard_map/ppermute | solution.py:518
  32.7 7.9 %collective-permute-start.12 = (bf16[2,22,16,128]{3,2,1,0:T(8,128)(2,1)S(1)}, bf16[2,22,16,128]{3,2,1,0:T(8,128)(2,1)S(1)}, u32[]{:S(2)}, u32[]{:S(2)}) collective-permute-start(bf16[2,22,16,128]{3,2,1,0:T(8,128)(2,1)S(1)} %triangle.11.refs_7_.refs_0_), channel_id=1, source_target_pairs={{0,1},{1,0},{2,3},{3,2},{4,5},{5,4},{6,7},{7,6},{8,9},{9,8},{10,11... | collective-permute-start | bytes 540680 | tf_op jit(solution)/shard_map/ppermute | solution.py:77
  32.8 8.9 %collective-permute-start.9 = (bf16[11,88,128]{2,1,0:T(8,128)(2,1)S(1)}, bf16[11,88,128]{2,1,0:T(8,128)(2,1)S(1)}, u32[]{:S(2)}, u32[]{:S(2)}) collective-permute-start(bf16[11,88,128]{2,1,0:T(8,128)(2,1)S(1)} %collective-permute-done.2.refs_2_.refs_1_), channel_id=1, source_target_pairs={{0,4},{4,8},{8,12},{12,14},{14,10},{10,6},{6,2},{2,0},{1,5},{5,9},... | collective-permute-start | bytes 743432 | tf_op jit(solution)/shard_map/ppermute | solution.py:515
  35.3 8.8 %collective-permute-start.10 = (bf16[11,88,128]{2,1,0:T(8,128)(2,1)S(1)}, bf16[11,88,128]{2,1,0:T(8,128)(2,1)S(1)}, u32[]{:S(2)}, u32[]{:S(2)}) collective-permute-start(bf16[11,88,128]{2,1,0:T(8,128)(2,1)S(1)} %collective-permute-done.3.refs_3_.refs_2_), channel_id=1, source_target_pairs={{0,2},{4,0},{8,4},{12,8},{14,12},{10,14},{6,10},{2,6},{1,3},{5,1},... | collective-permute-start | bytes 743432 | tf_op jit(solution)/shard_map/ppermute | solution.py:518
  36.6 12.6 %collective-permute-start.17 = (bf16[11,88,128]{2,1,0:T(8,128)(2,1)S(1)}, bf16[11,88,128]{2,1,0:T(8,128)(2,1)S(1)}, u32[]{:S(2)}, u32[]{:S(2)}) collective-permute-start(bf16[11,88,128]{2,1,0:T(8,128)(2,1)S(1)} %collective-permute-done.13.refs_2_.refs_1_), channel_id=1, source_target_pairs={{0,4},{4,8},{8,12},{12,14},{14,10},{10,6},{6,2},{2,0},{1,5},{5,9},... | collective-permute-start | bytes 743432 | tf_op jit(solution)/shard_map/ppermute | solution.py:515
  37.7 11.8 %collective-permute-start.18 = (bf16[11,88,128]{2,1,0:T(8,128)(2,1)S(1)}, bf16[11,88,128]{2,1,0:T(8,128)(2,1)S(1)}, u32[]{:S(2)}, u32[]{:S(2)}) collective-permute-start(bf16[11,88,128]{2,1,0:T(8,128)(2,1)S(1)} %collective-permute-done.14.refs_3_.refs_2_), channel_id=1, source_target_pairs={{0,2},{4,0},{8,4},{12,8},{14,12},{10,14},{6,10},{2,6},{1,3},{5,1},... | collective-permute-start | bytes 743432 | tf_op jit(solution)/shard_map/ppermute | solution.py:518
  41.2 7.4 %collective-permute-start.19 = (bf16[2,22,16,128]{3,2,1,0:T(8,128)(2,1)S(1)}, bf16[2,22,16,128]{3,2,1,0:T(8,128)(2,1)S(1)}, u32[]{:S(2)}, u32[]{:S(2)}) collective-permute-start(bf16[2,22,16,128]{3,2,1,0:T(8,128)(2,1)S(1)} %triangle.12.refs_7_.refs_0_), channel_id=1, source_target_pairs={{0,1},{1,0},{2,3},{3,2},{4,5},{5,4},{6,7},{7,6},{8,9},{9,8},{10,11... | collective-permute-start | bytes 540680 | tf_op jit(solution)/shard_map/ppermute | solution.py:77
  44.1 10.2 %collective-permute-start.15 = (bf16[11,88,128]{2,1,0:T(8,128)(2,1)S(1)}, bf16[11,88,128]{2,1,0:T(8,128)(2,1)S(1)}, u32[]{:S(2)}, u32[]{:S(2)}) collective-permute-start(bf16[11,88,128]{2,1,0:T(8,128)(2,1)S(1)} %collective-permute-done.9.refs_2_.refs_1_), channel_id=1, source_target_pairs={{0,4},{4,8},{8,12},{12,14},{14,10},{10,6},{6,2},{2,0},{1,5},{5,9},... | collective-permute-start | bytes 743432 | tf_op jit(solution)/shard_map/ppermute | solution.py:515
  44.6 9.8 %collective-permute-start.16 = (bf16[11,88,128]{2,1,0:T(8,128)(2,1)S(1)}, bf16[11,88,128]{2,1,0:T(8,128)(2,1)S(1)}, u32[]{:S(2)}, u32[]{:S(2)}) collective-permute-start(bf16[11,88,128]{2,1,0:T(8,128)(2,1)S(1)} %collective-permute-done.10.refs_3_.refs_2_), channel_id=1, source_target_pairs={{0,2},{4,0},{8,4},{12,8},{14,12},{10,14},{6,10},{2,6},{1,3},{5,1},... | collective-permute-start | bytes 743432 | tf_op jit(solution)/shard_map/ppermute | solution.py:518
  49.1 2.3 %collective-permute-start.21 = (bf16[2,22,16,128]{3,2,1,0:T(8,128)(2,1)S(1)}, bf16[2,22,16,128]{3,2,1,0:T(8,128)(2,1)S(1)}, u32[]{:S(2)}, u32[]{:S(2)}) collective-permute-start(bf16[2,22,16,128]{3,2,1,0:T(8,128)(2,1)S(1)} %triangle.13.refs_7_.refs_0_), channel_id=1, source_target_pairs={{0,1},{1,0},{2,3},{3,2},{4,5},{5,4},{6,7},{7,6},{8,9},{9,8},{10,11... | collective-permute-start | bytes 540680 | tf_op jit(solution)/shard_map/ppermute | solution.py:77
  51.1 1.5 %collective-permute-start.20 = (bf16[2,22,16,128]{3,2,1,0:T(8,128)(2,1)S(1)}, bf16[2,22,16,128]{3,2,1,0:T(8,128)(2,1)S(1)}, u32[]{:S(2)}, u32[]{:S(2)}) collective-permute-start(bf16[2,22,16,128]{3,2,1,0:T(8,128)(2,1)S(1)} %triangle.14.refs_7_.refs_0_), channel_id=1, source_target_pairs={{0,1},{1,0},{2,3},{3,2},{4,5},{5,4},{6,7},{7,6},{8,9},{9,8},{10,11... | collective-permute-start | bytes 540680 | tf_op jit(solution)/shard_map/ppermute | solution.py:77
  56.6 3.5 %collective-permute-start.22 = (bf16[2,22,16,128]{3,2,1,0:T(8,128)(2,1)S(1)}, bf16[2,22,16,128]{3,2,1,0:T(8,128)(2,1)S(1)}, u32[]{:S(2)}, u32[]{:S(2)}) collective-permute-start(bf16[2,22,16,128]{3,2,1,0:T(8,128)(2,1)S(1)} %triangle.15.refs_3_.refs_0_), channel_id=1, source_target_pairs={{0,1},{1,0},{2,3},{3,2},{4,5},{5,4},{6,7},{7,6},{8,9},{9,8},{10,11... | collective-permute-start | bytes 540680 | tf_op jit(solution)/shard_map/ppermute | solution.py:77
  56.9 12.9 %collective-permute-start.26 = (bf16[11,88,128]{2,1,0:T(8,128)(2,1)S(1)}, bf16[11,88,128]{2,1,0:T(8,128)(2,1)S(1)}, u32[]{:S(2)}, u32[]{:S(2)}) collective-permute-start(bf16[11,88,128]{2,1,0:T(8,128)(2,1)S(1)} %get-tuple-element.107), channel_id=1, source_target_pairs={{0,4},{4,8},{8,12},{12,14},{14,10},{10,6},{6,2},{2,0},{1,5},{5,9},... | collective-permute-start | bytes 743432 | tf_op jit(solution)/shard_map/ppermute | solution.py:515
  57.4 12.4 %collective-permute-start.25 = (bf16[11,88,128]{2,1,0:T(8,128)(2,1)S(1)}, bf16[11,88,128]{2,1,0:T(8,128)(2,1)S(1)}, u32[]{:S(2)}, u32[]{:S(2)}) collective-permute-start(bf16[11,88,128]{2,1,0:T(8,128)(2,1)S(1)} %get-tuple-element.99.refs_4_), channel_id=1, source_target_pairs={{0,2},{4,0},{8,4},{12,8},{14,12},{10,14},{6,10},{2,6},{1,3},{5,1},... | collective-permute-start | bytes 743432 | tf_op jit(solution)/shard_map/ppermute | solution.py:518
  62.1 9.9 %collective-permute-start.24 = (bf16[11,88,128]{2,1,0:T(8,128)(2,1)S(1)}, bf16[11,88,128]{2,1,0:T(8,128)(2,1)S(1)}, u32[]{:S(2)}, u32[]{:S(2)}) collective-permute-start(bf16[11,88,128]{2,1,0:T(8,128)(2,1)S(1)} %get-tuple-element.105), channel_id=1, source_target_pairs={{0,4},{4,8},{8,12},{12,14},{14,10},{10,6},{6,2},{2,0},{1,5},{5,9},... | collective-permute-start | bytes 743432 | tf_op jit(solution)/shard_map/ppermute | solution.py:515
  62.5 9.5 %collective-permute-start.23 = (bf16[11,88,128]{2,1,0:T(8,128)(2,1)S(1)}, bf16[11,88,128]{2,1,0:T(8,128)(2,1)S(1)}, u32[]{:S(2)}, u32[]{:S(2)}) collective-permute-start(bf16[11,88,128]{2,1,0:T(8,128)(2,1)S(1)} %get-tuple-element.101.refs_4_), channel_id=1, source_target_pairs={{0,2},{4,0},{8,4},{12,8},{14,12},{10,14},{6,10},{2,6},{1,3},{5,1},... | collective-permute-start | bytes 743432 | tf_op jit(solution)/shard_map/ppermute | solution.py:518
  69.9 9.9 %collective-permute-start.30 = (bf16[11,88,128]{2,1,0:T(8,128)(2,1)S(1)}, bf16[11,88,128]{2,1,0:T(8,128)(2,1)S(1)}, u32[]{:S(2)}, u32[]{:S(2)}) collective-permute-start(bf16[11,88,128]{2,1,0:T(8,128)(2,1)S(1)} %get-tuple-element.115), channel_id=1, source_target_pairs={{0,4},{4,8},{8,12},{12,14},{14,10},{10,6},{6,2},{2,0},{1,5},{5,9},... | collective-permute-start | bytes 743432 | tf_op jit(solution)/shard_map/ppermute | solution.py:515
  71.5 8.9 %collective-permute-start.29 = (bf16[11,88,128]{2,1,0:T(8,128)(2,1)S(1)}, bf16[11,88,128]{2,1,0:T(8,128)(2,1)S(1)}, u32[]{:S(2)}, u32[]{:S(2)}) collective-permute-start(bf16[11,88,128]{2,1,0:T(8,128)(2,1)S(1)} %get-tuple-element.108.refs_4_), channel_id=1, source_target_pairs={{0,2},{4,0},{8,4},{12,8},{14,12},{10,14},{6,10},{2,6},{1,3},{5,1},... | collective-permute-start | bytes 743432 | tf_op jit(solution)/shard_map/ppermute | solution.py:518
  72.1 10.9 %collective-permute-start.28 = (bf16[11,88,128]{2,1,0:T(8,128)(2,1)S(1)}, bf16[11,88,128]{2,1,0:T(8,128)(2,1)S(1)}, u32[]{:S(2)}, u32[]{:S(2)}) collective-permute-start(bf16[11,88,128]{2,1,0:T(8,128)(2,1)S(1)} %get-tuple-element.113), channel_id=1, source_target_pairs={{0,4},{4,8},{8,12},{12,14},{14,10},{10,6},{6,2},{2,0},{1,5},{5,9},... | collective-permute-start | bytes 743432 | tf_op jit(solution)/shard_map/ppermute | solution.py:515
  74.2 11.0 %collective-permute-start.27 = (bf16[11,88,128]{2,1,0:T(8,128)(2,1)S(1)}, bf16[11,88,128]{2,1,0:T(8,128)(2,1)S(1)}, u32[]{:S(2)}, u32[]{:S(2)}) collective-permute-start(bf16[11,88,128]{2,1,0:T(8,128)(2,1)S(1)} %get-tuple-element.109.refs_4_), channel_id=1, source_target_pairs={{0,2},{4,0},{8,4},{12,8},{14,12},{10,14},{6,10},{2,6},{1,3},{5,1},... | collective-permute-start | bytes 743432 | tf_op jit(solution)/shard_map/ppermute | solution.py:518
  80.5 14.3 %collective-permute-start.34 = (bf16[11,88,128]{2,1,0:T(8,128)(2,1)S(1)}, bf16[11,88,128]{2,1,0:T(8,128)(2,1)S(1)}, u32[]{:S(2)}, u32[]{:S(2)}) collective-permute-start(bf16[11,88,128]{2,1,0:T(8,128)(2,1)S(1)} %get-tuple-element.130), channel_id=1, source_target_pairs={{0,4},{4,8},{8,12},{12,14},{14,10},{10,6},{6,2},{2,0},{1,5},{5,9},... | collective-permute-start | bytes 743432 | tf_op jit(solution)/shard_map/ppermute | solution.py:515
  82.6 12.2 %collective-permute-start.33 = (bf16[11,88,128]{2,1,0:T(8,128)(2,1)S(1)}, bf16[11,88,128]{2,1,0:T(8,128)(2,1)S(1)}, u32[]{:S(2)}, u32[]{:S(2)}) collective-permute-start(bf16[11,88,128]{2,1,0:T(8,128)(2,1)S(1)} %get-tuple-element.116.refs_4_), channel_id=1, source_target_pairs={{0,2},{4,0},{8,4},{12,8},{14,12},{10,14},{6,10},{2,6},{1,3},{5,1},... | collective-permute-start | bytes 743432 | tf_op jit(solution)/shard_map/ppermute | solution.py:518
  85.3 9.6 %collective-permute-start.32 = (bf16[11,88,128]{2,1,0:T(8,128)(2,1)S(1)}, bf16[11,88,128]{2,1,0:T(8,128)(2,1)S(1)}, u32[]{:S(2)}, u32[]{:S(2)}) collective-permute-start(bf16[11,88,128]{2,1,0:T(8,128)(2,1)S(1)} %get-tuple-element.129), channel_id=1, source_target_pairs={{0,4},{4,8},{8,12},{12,14},{14,10},{10,6},{6,2},{2,0},{1,5},{5,9},... | collective-permute-start | bytes 743432 | tf_op jit(solution)/shard_map/ppermute | solution.py:515
  87.8 7.1 %collective-permute-start.31 = (bf16[11,88,128]{2,1,0:T(8,128)(2,1)S(1)}, bf16[11,88,128]{2,1,0:T(8,128)(2,1)S(1)}, u32[]{:S(2)}, u32[]{:S(2)}) collective-permute-start(bf16[11,88,128]{2,1,0:T(8,128)(2,1)S(1)} %get-tuple-element.117.refs_4_), channel_id=1, source_target_pairs={{0,2},{4,0},{8,4},{12,8},{14,12},{10,14},{6,10},{2,6},{1,3},{5,1},... | collective-permute-start | bytes 743432 | tf_op jit(solution)/shard_map/ppermute | solution.py:518
  95.0 8.7 %collective-permute-start.36 = (bf16[11,88,128]{2,1,0:T(8,128)(2,1)S(1)}, bf16[11,88,128]{2,1,0:T(8,128)(2,1)S(1)}, u32[]{:S(2)}, u32[]{:S(2)}) collective-permute-start(bf16[11,88,128]{2,1,0:T(8,128)(2,1)S(1)} %get-tuple-element.135), channel_id=1, source_target_pairs={{0,4},{4,8},{8,12},{12,14},{14,10},{10,6},{6,2},{2,0},{1,5},{5,9},... | collective-permute-start | bytes 743432 | tf_op jit(solution)/shard_map/ppermute | solution.py:515
  97.0 6.7 %collective-permute-start.35 = (bf16[11,88,128]{2,1,0:T(8,128)(2,1)S(1)}, bf16[11,88,128]{2,1,0:T(8,128)(2,1)S(1)}, u32[]{:S(2)}, u32[]{:S(2)}) collective-permute-start(bf16[11,88,128]{2,1,0:T(8,128)(2,1)S(1)} %get-tuple-element.131.refs_15_), channel_id=1, source_target_pairs={{0,2},{4,0},{8,4},{12,8},{14,12},{10,14},{6,10},{2,6},{1,3},{5,1},... | collective-permute-start | bytes 743432 | tf_op jit(solution)/shard_map/ppermute | solution.py:518
  105.8 13.1 %copy-start.4 = (bf16[22,88,128]{2,1,0:T(8,128)(2,1)S(1)}, bf16[22,88,128]{2,1,0:T(8,128)(2,1)}, u32[]{:S(2)}) copy-start(bf16[22,88,128]{2,1,0:T(8,128)(2,1)} %refs_0_.41) | copy-start | bytes 1486852
  105.8 1.4 %collective-permute-start.37 = (bf16[64,768]{1,0:T(8,128)(2,1)S(1)}, bf16[64,768]{1,0:T(8,128)(2,1)S(1)}, u32[]{:S(2)}, u32[]{:S(2)}) collective-permute-start(bf16[64,768]{1,0:T(8,128)(2,1)S(1)} %get-tuple-element.137), channel_id=1, source_target_pairs={{0,1},{1,0},{2,3},{3,2},{4,5},{5,4},{6,7},{7,6},{8,9},{9,8},{10,11... | collective-permute-start | bytes 294920 | tf_op jit(solution)/shard_map/ppermute | solution.py:77
  107.2 6.0 %collective-permute-start.40 = (bf16[64,768]{1,0:T(8,128)(2,1)S(1)}, bf16[64,768]{1,0:T(8,128)(2,1)S(1)}, u32[]{:S(2)}, u32[]{:S(2)}) collective-permute-start(bf16[64,768]{1,0:T(8,128)(2,1)S(1)} %add_convert_fusion.2), channel_id=1, source_target_pairs={{0,6},{2,4},{4,2},{6,0},{8,14},{10,12},{12,10},{14,8},{1,7},{3,5},... | collective-permute-start | bytes 294920 | tf_op jit(solution)/shard_map/ppermute | solution.py:694
  107.7 6.9 %collective-permute-start.39 = (bf16[64,768]{1,0:T(8,128)(2,1)S(1)}, bf16[64,768]{1,0:T(8,128)(2,1)S(1)}, u32[]{:S(2)}, u32[]{:S(2)}) collective-permute-start(bf16[64,768]{1,0:T(8,128)(2,1)S(1)} %add_convert_fusion.2), channel_id=1, source_target_pairs={{0,4},{2,6},{4,0},{6,2},{8,12},{10,14},{12,8},{14,10},{1,5},{3,7},... | collective-permute-start | bytes 294920 | tf_op jit(solution)/shard_map/ppermute | solution.py:694
  109.5 5.6 %collective-permute-start.38 = (bf16[64,768]{1,0:T(8,128)(2,1)S(1)}, bf16[64,768]{1,0:T(8,128)(2,1)S(1)}, u32[]{:S(2)}, u32[]{:S(2)}) collective-permute-start(bf16[64,768]{1,0:T(8,128)(2,1)S(1)} %add_convert_fusion.2), channel_id=1, source_target_pairs={{0,2},{2,0},{4,6},{6,4},{8,10},{10,8},{12,14},{14,12},{1,3},{3,1},... | collective-permute-start | bytes 294920 | tf_op jit(solution)/shard_map/ppermute | solution.py:694
  115.1 8.8 %collective-permute-start.41 = (bf16[64,768]{1,0:T(8,128)(2,1)S(1)}, bf16[64,768]{1,0:T(8,128)(2,1)S(1)}, u32[]{:S(2)}, u32[]{:S(2)}) collective-permute-start(bf16[64,768]{1,0:T(8,128)(2,1)S(1)} %add_convert_fusion.1), channel_id=1, source_target_pairs={{0,8},{2,10},{4,12},{6,14},{8,0},{10,2},{12,4},{14,6},{1,9},{3,11}... | collective-permute-start | bytes 294920 | tf_op jit(solution)/shard_map/ppermute | solution.py:694
  123.9 1.4 %collective-permute-start.42 = (bf16[64,768]{1,0:T(8,128)(2,1)S(1)}, bf16[64,768]{1,0:T(8,128)(2,1)S(1)}, u32[]{:S(2)}, u32[]{:S(2)}) collective-permute-start(bf16[64,768]{1,0:T(8,128)(2,1)S(1)} %add_convert_fusion.refs_0_), channel_id=1, source_target_pairs={{0,1},{1,0},{2,3},{3,2},{4,5},{5,4},{6,7},{7,6},{8,9},{9,8},{10,11... | collective-permute-start | bytes 294920 | tf_op jit(solution)/shard_map/ppermute | solution.py:77
